TPU v7x, 32 devices: a whole 2x2x4 slice. The times are simulated.
32 devices in a mesh: row: 16 (over z, x, core), col: 2 (over y).
Axes of the slice: x: 2, y: 2, z: 4, core: 2. Of those that a mesh axis runs over, the one named last changes fastest.
Arguments:
- right_sides: float32 [4, 64, 2048], P(None, 'col', 'row'), may hold values from -6 to 6
- factors: bfloat16 [6, 2048, 2048], P(None, 'row', 'col'), may hold values from -0.09375 to 0.09375
- pattern: int32 [6, 16, 16], P(None, 'row', 'col'), may hold values 0 or 1
- live_widths: int32 [4, 16], P(None, 'row'), may hold values from 64 to 128
- inverses: float32 [4, 16, 128, 128], P(None, 'row'), may hold values from -1 to 2, as said below
Outputs:
- solution: float32 [4, 64, 2048], P(None, 'col', 'row')
Inputs may be any that keep to these rules, and one draw needn't show every extreme that they name: Each 128 x 128 block of inverses is lower triangular with positive diagonal entries.
All inputs are finite; a program needn't handle non-finite values. No bound on the sum of `pattern` on one device may be relied on, other than what follows from the above.
Results may differ from a plain program's by a relative error of at most 0.0025.
Values may be sent and summed in bfloat16 or wider, within the bound.
No kernel may reach another device: no remote copies, remote signals or barrier semaphores. Data moves between devices by JAX's collectives and lax.ppermute only.
A program may use at most 64 MiB of HBM per device.

v0:
```python
import jax
import jax.numpy as jnp
from jax import lax
from jax.sharding import PartitionSpec as P


def pair_lookup(level_count):
    lookup = {}
    for lower_level in range(level_count):
        for above_level in range(lower_level + 1, level_count):
            lookup[above_level, lower_level] = len(lookup)
    return lookup


def live_mask(widths_row, block_width):
    column = lax.broadcasted_iota(jnp.int32, (widths_row.shape[0], block_width), 1)
    return (column < widths_row[:, None]).astype(jnp.float32).reshape(-1)


def apply_inverse(vector, inverse, live_part, transpose):
    row_count = vector.shape[0]
    block_count = inverse.shape[0]
    block_width = inverse.shape[1]
    shaped = (vector * live_part).reshape(row_count, block_count, block_width)
    einsum_form = "rkb,kba->rka" if transpose else "rkb,kab->rka"
    result = jnp.einsum(einsum_form, shaped, inverse, precision=lax.Precision.HIGHEST)
    return result.reshape(row_count, block_count * block_width) * live_part


def lower_update(solved_cols, factor, pattern_pair, block_width):
    rhs_total = solved_cols.shape[0]
    row_blocks = pattern_pair.shape[0]
    col_blocks = pattern_pair.shape[1]
    left_side = solved_cols.reshape(rhs_total, col_blocks, block_width)
    right_side = factor.reshape(row_blocks, block_width, col_blocks, block_width)
    partial_terms = jnp.einsum(
        "rjb,iajb->rija", left_side, right_side, preferred_element_type=jnp.float32
    )
    weights = pattern_pair.astype(jnp.float32)[None, :, :, None]
    summed = jnp.sum(partial_terms * weights, axis=2)
    return summed.reshape(rhs_total, row_blocks * block_width)


def upper_update(solved_rows, factor, pattern_pair, block_width):
    rhs_total = solved_rows.shape[0]
    row_blocks = pattern_pair.shape[0]
    col_blocks = pattern_pair.shape[1]
    left_side = solved_rows.reshape(rhs_total, row_blocks, block_width)
    right_side = factor.reshape(row_blocks, block_width, col_blocks, block_width)
    partial_terms = jnp.einsum(
        "ria,iajb->rijb", left_side, right_side, preferred_element_type=jnp.float32
    )
    weights = pattern_pair.astype(jnp.float32)[None, :, :, None]
    summed = jnp.sum(partial_terms * weights, axis=1)
    return summed.reshape(rhs_total, col_blocks * block_width)


def reduce_forward(stacked):
    return lax.psum_scatter(stacked, "col", scatter_dimension=1, tiled=True)


def reduce_backward(stacked):
    traded = lax.all_to_all(stacked, "col", split_axis=1, concat_axis=2, tiled=True)
    return lax.psum_scatter(traded, "row", scatter_dimension=2, tiled=True)


def local(right_sides, factors, pattern, live_widths, inverses):
    level_count = inverses.shape[0]
    block_width = inverses.shape[2]
    lookup = pair_lookup(level_count)
    masks = [live_mask(live_widths[height], block_width) for height in range(level_count)]
    local_rhs = right_sides.shape[1]
    local_rows = right_sides.shape[2]
    local_cols = factors.shape[2]
    pending = [jnp.zeros((local_rhs, local_rows), jnp.float32) for height in range(level_count)]
    solved = []
    for height in range(level_count):
        residual = right_sides[height] - pending[height]
        current = apply_inverse(residual, inverses[height], masks[height], False)
        solved.append(current)
        if height + 1 < level_count:
            rounded = current.astype(jnp.bfloat16)
            grouped = lax.all_gather(rounded, "col", axis=0, tiled=True)
            gathered = lax.all_gather(grouped, "row", axis=1, tiled=True)
            col_start = lax.axis_index("col") * local_cols
            spread_cols = lax.dynamic_slice_in_dim(gathered, col_start, local_cols, 1)
            contributions = [
                lower_update(
                    spread_cols,
                    factors[lookup[above_level, height]],
                    pattern[lookup[above_level, height]],
                    block_width,
                )
                for above_level in range(height + 1, level_count)
            ]
            reduced = reduce_forward(jnp.stack(contributions))
            for offset, above_level in enumerate(range(height + 1, level_count)):
                pending[above_level] = pending[above_level] + reduced[offset]
    pending_back = [
        jnp.zeros((local_rhs, local_rows), jnp.float32) for height in range(level_count)
    ]
    results = [None] * level_count
    for height in reversed(range(level_count)):
        corrected = solved[height] - pending_back[height]
        current = apply_inverse(corrected, inverses[height], masks[height], True)
        results[height] = current
        if height > 0:
            shared = lax.all_gather(current.astype(jnp.bfloat16), "col", axis=0, tiled=True)
            contributions = [
                upper_update(
                    shared,
                    factors[lookup[height, lower_level]],
                    pattern[lookup[height, lower_level]],
                    block_width,
                )
                for lower_level in range(height)
            ]
            reduced = reduce_backward(jnp.stack(contributions))
            for lower_level in range(height):
                pending_back[lower_level] = pending_back[lower_level] + reduced[lower_level]
    return jnp.stack(results)


def solution(mesh):
    return jax.shard_map(
        local,
        mesh=mesh,
        in_specs=(
            P(None, "col", "row"),
            P(None, "row", "col"),
            P(None, "row", "col"),
            P(None, "row"),
            P(None, "row", None, None),
        ),
        out_specs=P(None, "col", "row"),
        check_vma=False,
    )
```

profile of v0, /device:TPU:0, one launch (start us, length us, event | category | flops | bytes accessed | tf_op | source)
XLA Modules:
  0.0 345.7 jit_solution(15747841871180746042)
XLA Ops:
  6.5 1.5 fusion.125
  8.0 0.7 compare_convert_fusion.3
  8.7 0.7 convert_bitcast_fusion
  9.5 1.1 multiply_convert_fusion.5
  10.5 5.3 %all_gather.27 = bf16[64,128]{1,0:T(8,128)(2,1)S(1)} all-gather(bf16[32,128]{1,0:T(8,128)(2,1)S(1)} %get-tuple-element.21), channel_id=1, replica_groups=mesh['row'=16,'col'=2] {'col'}, dimensions={0}, use_global_device_ids=true | all-gather | bytes 24576 | tf_op jit(solution)/shard_map/all_gather | solution.py:83
  15.8 22.8 %all_gather.28 = bf16[64,2048]{1,0:T(8,128)(2,1)S(1)} all-gather(bf16[64,128]{1,0:T(8,128)(2,1)S(1)} %all_gather.27), channel_id=1, replica_groups=mesh['row'=16,'col'=2] {'row'}, dimensions={1}, use_global_device_ids=true | all-gather | bytes 278528 | tf_op jit(solution)/shard_map/all_gather | solution.py:84
  38.7 1.5 fusion.124
  40.7 0.2 fusion.20
  41.1 0.2 fusion.18
  41.3 0.6 pad_maximum_fusion.2
  42.4 0.7 compare_convert_fusion.2
  43.0 6.4 %reduce-scatter.7.cloned.1.call-done = f32[3,32,128]{2,1,0:T(8,128)} async-done(((f32[3,64,128]{2,1,0:T(8,128)}), f32[3,32,128]{2,1,0:T(8,128)}) %reduce-scatter.7.cloned.1.call-update) | async-done | bytes 49168 | tf_op jit(solution)/shard_map/reduce_scatter | solution.py:59
  49.4 1.0 multiply_convert_fusion.4
  50.5 4.4 %all_gather.29 = bf16[64,128]{1,0:T(8,128)(2,1)S(1)} all-gather(bf16[32,128]{1,0:T(8,128)(2,1)S(1)} %get-tuple-element.23), channel_id=1, replica_groups=mesh['row'=16,'col'=2] {'col'}, dimensions={0}, use_global_device_ids=true | all-gather | bytes 24576 | tf_op jit(solution)/shard_map/all_gather | solution.py:83
  54.8 22.0 %all_gather.30 = bf16[64,2048]{1,0:T(8,128)(2,1)S(1)} all-gather(bf16[64,128]{1,0:T(8,128)(2,1)S(1)} %all_gather.29), channel_id=1, replica_groups=mesh['row'=16,'col'=2] {'row'}, dimensions={1}, use_global_device_ids=true | all-gather | bytes 278528 | tf_op jit(solution)/shard_map/all_gather | solution.py:84
  77.1 0.2 fusion.21
  77.3 0.6 pad_maximum_fusion.3
  78.2 0.6 compare_convert_fusion.1
  78.8 5.5 %reduce-scatter.9.cloned.1.call-done = f32[2,32,128]{2,1,0:T(8,128)} async-done(((f32[2,64,128]{2,1,0:T(8,128)}), f32[2,32,128]{2,1,0:T(8,128)}) %reduce-scatter.9.cloned.1.call-update) | async-done | bytes 32784 | tf_op jit(solution)/shard_map/reduce_scatter | solution.py:59
  84.3 0.9 multiply_convert_fusion.3
  85.3 4.4 %all_gather.31 = bf16[64,128]{1,0:T(8,128)(2,1)S(1)} all-gather(bf16[32,128]{1,0:T(8,128)(2,1)S(1)} %get-tuple-element.25), channel_id=1, replica_groups=mesh['row'=16,'col'=2] {'col'}, dimensions={0}, use_global_device_ids=true | all-gather | bytes 24576 | tf_op jit(solution)/shard_map/all_gather | solution.py:83
  89.6 22.0 %all_gather.32 = bf16[64,2048]{1,0:T(8,128)(2,1)S(1)} all-gather(bf16[64,128]{1,0:T(8,128)(2,1)S(1)} %all_gather.31), channel_id=1, replica_groups=mesh['row'=16,'col'=2] {'row'}, dimensions={1}, use_global_device_ids=true | all-gather | bytes 278528 | tf_op jit(solution)/shard_map/all_gather | solution.py:84
  111.6 0.8 fusion.23
  112.5 0.7 compare_convert_fusion
  113.2 5.6 %reduce-scatter.11.cloned.1.call-done = f32[1,32,128]{2,1,0:T(8,128)} async-done(((f32[1,64,128]{2,1,0:T(8,128)}), f32[1,32,128]{2,1,0:T(8,128)}) %reduce-scatter.11.cloned.1.call-update) | async-done | bytes 16400 | tf_op jit(solution)/shard_map/reduce_scatter | solution.py:59
  118.8 1.0 fusion.27
  119.9 4.4 %all_gather.33 = bf16[64,128]{1,0:T(8,128)(2,1)S(1)} all-gather(bf16[32,128]{1,0:T(8,128)(2,1)S(1)} %multiply_convert_fusion.2), channel_id=1, replica_groups=mesh['row'=16,'col'=2] {'col'}, dimensions={0}, use_global_device_ids=true | all-gather | bytes 24576 | tf_op jit(solution)/shard_map/all_gather | solution.py:108
  124.5 0.2 fusion.13
  124.7 0.2 fusion.17
  125.4 0.7 pad_maximum_fusion
  126.1 14.7 %all_to_all.54 = f32[3,64,1024]{2,0,1:T(4,128)S(1)} all-to-all(f32[3,64,1024]{2,0,1:T(4,128)S(1)} %pad_maximum_fusion), channel_id=1, replica_groups=mesh['row'=16,'col'=2] {'col'}, dimensions={1} | all-to-all | bytes 1572864 | tf_op jit(solution)/shard_map/all_to_all | solution.py:63
  140.8 0.5 copy.30
  141.3 1.0 copy.63
  142.3 56.6 %reduce-scatter.13.cloned.1.call-done = f32[3,32,128]{2,1,0:T(8,128)} async-done(((f32[3,32,2048]{2,1,0:T(8,128)}), f32[3,32,128]{2,1,0:T(8,128)}) %reduce-scatter.13.cloned.1.call-update) | async-done | bytes 49168 | tf_op jit(solution)/shard_map/reduce_scatter | solution.py:64
  198.9 0.9 bitcast_multiply_fusion.1
  199.8 4.4 %all_gather.34 = bf16[64,128]{1,0:T(8,128)(2,1)S(1)} all-gather(bf16[32,128]{1,0:T(8,128)(2,1)S(1)} %multiply_convert_fusion.1), channel_id=1, replica_groups=mesh['row'=16,'col'=2] {'col'}, dimensions={0}, use_global_device_ids=true | all-gather | bytes 24576 | tf_op jit(solution)/shard_map/all_gather | solution.py:108
  204.4 0.2 fusion.11
  204.9 0.5 pad_maximum_fusion.1
  205.4 9.1 %all_to_all.55 = f32[2,64,1024]{2,0,1:T(2,128)S(1)} all-to-all(f32[2,64,1024]{2,0,1:T(2,128)S(1)} %pad_maximum_fusion.1), channel_id=1, replica_groups=mesh['row'=16,'col'=2] {'col'}, dimensions={1} | all-to-all | bytes 1048576 | tf_op jit(solution)/shard_map/all_to_all | solution.py:63
  214.7 0.8 copy.64
  215.6 53.9 %reduce-scatter.15.cloned.1.call-done = f32[2,32,128]{2,1,0:T(8,128)} async-done(((f32[2,32,2048]{2,1,0:T(8,128)}), f32[2,32,128]{2,1,0:T(8,128)}) %reduce-scatter.15.cloned.1.call-update) | async-done | bytes 32784 | tf_op jit(solution)/shard_map/reduce_scatter | solution.py:64
  269.6 0.9 bitcast_multiply_fusion.2
  270.5 4.4 %all_gather.35 = bf16[64,128]{1,0:T(8,128)(2,1)S(1)} all-gather(bf16[32,128]{1,0:T(8,128)(2,1)S(1)} %multiply_convert_fusion), channel_id=1, replica_groups=mesh['row'=16,'col'=2] {'col'}, dimensions={0}, use_global_device_ids=true | all-gather | bytes 24576 | tf_op jit(solution)/shard_map/all_gather | solution.py:108
  275.3 7.7 %all_to_all.56 = f32[1,64,1024]{2,0,1:T(1,128)S(1)} all-to-all(f32[1,64,1024]{2,0,1:T(1,128)S(1)} %bitcast.467), channel_id=1, replica_groups=mesh['row'=16,'col'=2] {'col'}, dimensions={1} | all-to-all | bytes 524288 | tf_op jit(solution)/shard_map/all_to_all | solution.py:63
  283.0 0.7 copy.65
  283.8 53.6 %reduce-scatter.17.cloned.1.call-done = f32[1,32,128]{2,1,0:T(8,128)} async-done(((f32[1,32,2048]{2,1,0:T(8,128)}), f32[1,32,128]{2,1,0:T(8,128)}) %reduce-scatter.17.cloned.1.call-update) | async-done | bytes 16400 | tf_op jit(solution)/shard_map/reduce_scatter | solution.py:64
  337.4 0.9 fusion.24
  338.2 0.6 pad_maximum_fusion.4
  (45 shorter events, 3.7 us)
Async XLA Ops:
  6.5 42.9 %reduce-scatter.7.cloned.1.call-start = ((), (), s32[]{:S(2)}) async-start(), calls=%async_computation.9 | async-start | bytes 147456 | tf_op jit(solution)/shard_map/reduce_scatter | solution.py:59
  40.5 9.0 %copy-start = (f32[4,1,128,128]{3,2,1,0:T(8,128)S(1)}, f32[4,1,128,128]{3,2,1,0:T(8,128)}, u32[]{:S(2)}) copy-start(f32[4,1,128,128]{3,2,1,0:T(8,128)} %param.9) | copy-start | bytes 786436
  40.5 9.0 %copy-start.1 = (f32[4,32,128]{2,1,0:T(8,128)S(1)}, f32[4,32,128]{2,1,0:T(8,128)}, u32[]{:S(2)}) copy-start(f32[4,32,128]{2,1,0:T(8,128)} %param.5) | copy-start | bytes 196612
  42.0 42.3 %reduce-scatter.9.cloned.1.call-start = ((), (), s32[]{:S(2)}) async-start(), calls=%async_computation.10 | async-start | bytes 98304 | tf_op jit(solution)/shard_map/reduce_scatter | solution.py:59
  49.4 34.9 %copy-start.2 = (f32[3,32,128]{2,1,0:T(8,128)S(1)}, f32[3,32,128]{2,1,0:T(8,128)}, u32[]{:S(2)}) copy-start(f32[3,32,128]{2,1,0:T(8,128)} %reduce-scatter.7.cloned.1.call-done) | copy-start | bytes 147460
  77.9 40.8 %reduce-scatter.11.cloned.1.call-start = ((), (), s32[]{:S(2)}) async-start(), calls=%async_computation.11 | async-start | bytes 49152 | tf_op jit(solution)/shard_map/reduce_scatter | solution.py:59
  112.5 86.4 %reduce-scatter.13.cloned.1.call-start = ((), (), s32[]{:S(2)}) async-start(), calls=%async_computation.12 | async-start | bytes 835584 | tf_op jit(solution)/shard_map/reduce_scatter | solution.py:64
  142.3 127.3 %reduce-scatter.15.cloned.1.call-start = ((), (), s32[]{:S(2)}) async-start(), calls=%async_computation.13 | async-start | bytes 557056 | tf_op jit(solution)/shard_map/reduce_scatter | solution.py:64
  214.5 55.0 %copy-start.3 = (f32[3,32,128]{2,1,0:T(8,128)S(1)}, f32[3,32,128]{2,1,0:T(8,128)}, u32[]{:S(2)}) copy-start(f32[3,32,128]{2,1,0:T(8,128)} %reduce-scatter.13.cloned.1.call-done) | copy-start | bytes 147460
  215.6 121.8 %reduce-scatter.17.cloned.1.call-start = ((), (), s32[]{:S(2)}) async-start(), calls=%async_computation.14 | async-start | bytes 278528 | tf_op jit(solution)/shard_map/reduce_scatter | solution.py:64
  269.5 67.8 %copy-start.4 = (f32[2,32,128]{2,1,0:T(8,128)S(1)}, f32[2,32,128]{2,1,0:T(8,128)}, u32[]{:S(2)}) copy-start(f32[2,32,128]{2,1,0:T(8,128)} %reduce-scatter.15.cloned.1.call-done) | copy-start | bytes 98308
Sparse Core Ops, SparseCore 0:
  42.1 7.2 reduce-scatter.6
  78.0 6.2 reduce-scatter.8
  112.6 6.1 reduce-scatter.10
  142.4 56.4 reduce-scatter.12
  215.7 53.8 reduce-scatter.14
  283.9 53.4 reduce-scatter.16
where the time goes:
time: 347 us; the launch traced here: 346 us
  waiting for transfers between devices  182 us (52%)
  blocking collectives  126 us (36%)
  between operations  13.8 us (4%)
  matrix products  9.91 us (3%)
  local copies, waits for them, and re-layouts  8.1 us (2%)
  other arithmetic  6.49 us (2%)
    reduce_scatter x3, waiting for transfers between devices, reduce_backward(): return lax.psum_scatter(traded, 'row', scatter_dimension=2, tiled=True)  164 us
    all_gather x3, blocking collectives, local(): gathered = lax.all_gather(grouped, 'row', axis=1, tiled=True)  66.9 us
    all_to_all x3, blocking collectives, reduce_backward(): lax.all_to_all(stacked, 'col', split_axis=1, concat_axis=2, tiled=True)  31.6 us
    reduce_scatter x3, waiting for transfers between devices, reduce_forward(): return lax.psum_scatter(stacked, 'col', scatter_dimension=1, tiled=True)  17.5 us
    all_gather x3, blocking collectives, local(): grouped = lax.all_gather(rounded, 'col', axis=0, tiled=True)  14 us
    all_gather x3, blocking collectives, local(): lax.all_gather(current.astype(jnp.bfloat16), 'col', axis=0, tiled=True)  13.1 us
  transfers between devices with their start and end apart: 6, of which 6 were waited for; matrix products, arithmetic and copies ran while one was open for 1% of the time, Pallas kernels for 0%

commit v1 on v0

v1 whole, which is shorter than its diff:
```python
import jax
import jax.numpy as jnp
from jax import lax
from jax.experimental import pallas as pl
from jax.experimental.pallas import tpu as pltpu
from jax.sharding import PartitionSpec as P

HIGHEST = lax.Precision.HIGHEST


def pair_lookup(level_count):
    lookup = {}
    for lower_level in range(level_count):
        for above_level in range(lower_level + 1, level_count):
            lookup[above_level, lower_level] = len(lookup)
    return lookup


def call(kernel, outs, *operands):
    return pl.pallas_call(
        kernel,
        out_shape=outs,
        in_specs=[
            pl.BlockSpec(memory_space=pltpu.SMEM if x.ndim == 1 else pltpu.VMEM) for x in operands
        ],
        out_specs=jax.tree.map(lambda _: pl.BlockSpec(memory_space=pltpu.VMEM), outs),
        compiler_params=pltpu.CompilerParams(vmem_limit_bytes=48 * 1024 * 1024),
    )(*operands)


def live_row(widths, level, block_width):
    column = lax.broadcasted_iota(jnp.int32, (1, block_width), 1)
    return (column < widths[level]).astype(jnp.float32)


def join(blocks):
    return jnp.concatenate([blocks[k] for k in range(blocks.shape[0])], axis=1)


def local(parts, right_sides, factors, pattern, live_widths, inverses):
    row_parts, col_parts = parts
    levels, rhs, width = right_sides.shape
    pairs, _, local_cols = factors.shape
    half = local_cols // width
    total_blocks = half * col_parts
    lookup = pair_lookup(levels)
    widths = live_widths.reshape(levels)
    inverses = inverses.reshape(levels, width, width)
    f32, bf16 = jnp.float32, jnp.bfloat16

    with jax.named_scope("mask"):
        kept = pattern.reshape(pairs, 1, half, 1).astype(bf16)
        masked = (factors.reshape(pairs, width, half, width) * kept).reshape(factors.shape)
    held = {}
    for level in range(1, levels):
        with jax.named_scope("exchange"):
            own = jnp.stack([masked[lookup[level, lower]] for lower in range(level)])
            shifted = [own]
            for shift in range(1, col_parts):
                to_lower = [((q + shift) % col_parts, q) for q in range(col_parts)]
                shifted.append(lax.ppermute(own, "col", to_lower))
            held[level] = shifted

    block_f32 = jax.ShapeDtypeStruct((rhs, width), f32)
    block_bf16 = jax.ShapeDtypeStruct((rhs, width), bf16)
    spread_bf16 = jax.ShapeDtypeStruct((total_blocks, rhs, width), bf16)
    spread_f32 = jax.ShapeDtypeStruct((total_blocks, rhs, width), f32)

    def trade(blocks):
        return lax.all_to_all(blocks, "row", 0, 0)

    def solve_forward(level, widths_ref, rhs_ref, inverse_ref, total):
        live = live_row(widths_ref, level, width)
        vector = (rhs_ref[level] - total) * live
        product = lax.dot_general(
            vector, inverse_ref[level], (((1,), (1,)), ((), ())), precision=HIGHEST, preferred_element_type=f32
        )
        return product * live

    def solve_backward(level, widths_ref, inverse_ref, corrected):
        live = live_row(widths_ref, level, width)
        product = lax.dot_general(
            corrected * live, inverse_ref[level], (((1,), (0,)), ((), ())), precision=HIGHEST, preferred_element_type=f32
        )
        return product * live

    def forward_total(gathered, level, matrices):
        mine = lax.axis_index("col")
        total = None
        for shift in range(col_parts):
            start = lax.rem(mine + shift, col_parts) * half
            for lower in range(level):
                left = join(gathered[lower][pl.ds(start, half)])
                term = lax.dot_general(
                    left, matrices[shift][lower], (((1,), (1,)), ((), ())), preferred_element_type=f32
                )
                total = term if total is None else total + term
        return total

    def backward_partials(out_ref, solved, lower, matrices):
        mine = lax.axis_index("col")
        for shift in range(col_parts):
            start = lax.rem(mine + shift, col_parts) * half
            total = None
            for level, vector in solved.items():
                term = lax.dot_general(
                    vector, matrices[level][shift][lower], (((1,), (0,)), ((), ())), preferred_element_type=f32
                )
                total = term if total is None else total + term
            for block in range(half):
                out_ref[start + block] = total[:, block * width : (block + 1) * width]

    def spread(out_ref, value):
        out_ref[...] = jnp.broadcast_to(value.astype(bf16)[None], out_ref.shape)

    def first(widths_ref, rhs_ref, inverse_ref, solved_ref, out_ref):
        value = solve_forward(0, widths_ref, rhs_ref, inverse_ref, jnp.zeros((rhs, width), f32))
        solved_ref[...] = value
        spread(out_ref, value)

    def middle(level):
        def body(widths_ref, rhs_ref, inverse_ref, *refs):
            gathered, matrices = refs[:level], refs[level : level + col_parts]
            solved_ref, out_ref = refs[level + col_parts :]
            total = forward_total(gathered, level, matrices)
            value = solve_forward(level, widths_ref, rhs_ref, inverse_ref, total)
            solved_ref[...] = value
            spread(out_ref, value)

        return body

    def top(widths_ref, rhs_ref, inverse_ref, *refs):
        level = levels - 1
        gathered, matrices = refs[:level], refs[level : level + col_parts]
        result_ref, rounded_ref, out_ref = refs[level + col_parts :]
        total = forward_total(gathered, level, matrices)
        value = solve_forward(level, widths_ref, rhs_ref, inverse_ref, total)
        result = solve_backward(level, widths_ref, inverse_ref, value)
        result_ref[...] = result
        rounded = result.astype(bf16)
        rounded_ref[...] = rounded
        backward_partials(out_ref, {level: rounded}, level - 1, {level: matrices})

    def down(level):
        above = levels - 1 - level

        def body(widths_ref, inverse_ref, solved_ref, sums_ref, *refs):
            rounded_above = refs[:above]
            flat = refs[above : above + (above + 1) * col_parts]
            result_ref, rounded_ref, out_ref = refs[above + (above + 1) * col_parts :]
            corrected = solved_ref[...] - jnp.sum(sums_ref[...], axis=0)
            result = solve_backward(level, widths_ref, inverse_ref, corrected)
            result_ref[...] = result
            rounded = result.astype(bf16)
            rounded_ref[...] = rounded
            solved = {level: rounded}
            for index in range(above):
                solved[level + 1 + index] = rounded_above[index][...]
            matrices = {
                level + index: flat[index * col_parts : (index + 1) * col_parts] for index in range(above + 1)
            }
            backward_partials(out_ref, solved, level - 1, matrices)

        return body

    def last(widths_ref, inverse_ref, solved_ref, sums_ref, *refs):
        out_ref = refs[-1]
        corrected = solved_ref[...] - jnp.sum(sums_ref[...], axis=0)
        out_ref[0] = solve_backward(0, widths_ref, inverse_ref, corrected)
        for level in range(1, levels):
            out_ref[level] = refs[level - 1][...]

    solved, gathered = [], []
    with jax.named_scope("forward_first"):
        value, out = call(first, (block_f32, spread_bf16), widths, right_sides, inverses)
    solved.append(value)
    gathered.append(trade(out))
    for level in range(1, levels - 1):
        with jax.named_scope("forward_level"):
            value, out = call(
                middle(level), (block_f32, spread_bf16), widths, right_sides, inverses, *gathered, *held[level]
            )
        solved.append(value)
        gathered.append(trade(out))
    results, rounded = {}, {}
    level = levels - 1
    with jax.named_scope("top_level"):
        results[level], rounded[level], out = call(
            top, (block_f32, block_bf16, spread_f32), widths, right_sides, inverses, *gathered, *held[level]
        )
    sums = trade(out)
    for level in range(levels - 2, 0, -1):
        with jax.named_scope("backward_level"):
            flat = [m for upper in range(level, levels) for m in held[upper]]
            results[level], rounded[level], out = call(
                down(level),
                (block_f32, block_bf16, spread_f32),
                widths,
                inverses,
                solved[level],
                sums,
                *[rounded[upper] for upper in range(level + 1, levels)],
                *flat,
            )
        sums = trade(out)
    with jax.named_scope("backward_last"):
        return call(
            last,
            jax.ShapeDtypeStruct((levels, rhs, width), f32),
            widths,
            inverses,
            solved[0],
            sums,
            *[results[level] for level in range(1, levels)],
        )


def solution(mesh):
    parts = (mesh.shape["row"], mesh.shape["col"])

    def run(*operands):
        return local(parts, *operands)

    return jax.shard_map(
        run,
        mesh=mesh,
        in_specs=(
            P(None, "col", "row"),
            P(None, "row", "col"),
            P(None, "row", "col"),
            P(None, "row"),
            P(None, "row", None, None),
        ),
        out_specs=P(None, "col", "row"),
        check_vma=False,
    )
```

time: 347 us -> 112 us (0.32)
  waiting for transfers between devices: 182 us -> 17.4 us
  blocking collectives: 126 us -> 76.3 us
  between operations: 13.8 us -> 0.16 us
  matrix products: 9.91 us -> 0 us
  Pallas kernels: 0 us -> 9.07 us
  other arithmetic: 6.49 us -> 0.86 us
  local copies, waits for them, and re-layouts: 8.1 us -> 2.75 us
  starting transfers between devices: 0.21 us -> 5.19 us
    reduce_scatter x6 -> x0, waiting for transfers between devices: 182 us -> none  [the longest x3 164 us: reduce_backward(): return lax.psum_scatter(traded, 'row', scatter_dimension=2, tiled=True)]
    all_gather x9 -> x0, blocking collectives: 94 us -> none  [the longest x3 66.9 us: local(): gathered = lax.all_gather(grouped, 'row', axis=1, tiled=True)]
    all_to_all x3 -> x6, blocking collectives: 31.6 us -> 76.3 us  [trade(): return lax.all_to_all(blocks, 'row', 0, 0)]
    ppermute x0 -> x3, waiting for transfers between devices: none -> 17.4 us  [local(): shifted.append(lax.ppermute(own, 'col', to_lower))]
    dot_general x20 -> x0, matrix products: 9.91 us -> none  [the longest x8 6.83 us: apply_inverse(): jnp.einsum(einsum_form, shaped, inverse, precision=lax.Precision.HIGHEST)]
    pallas_call x0 -> x7, Pallas kernels: none -> 9.07 us  [call(): pl.pallas_call(kernel, out_shape=outs, in_specs=[pl.BlockSpec(memory_spac...]
    ppermute x0 -> x3, starting transfers between devices: none -> 5.19 us  [local(): shifted.append(lax.ppermute(own, 'col', to_lower))]
  transfers between devices with their start and end apart: 6 -> 3, of which waited for: 6 -> 1; matrix products, arithmetic and copies ran while one was open for 1% -> 0% of each run, Pallas kernels for 0% -> 3%
where the time goes in v1:
time: 112 us
  blocking collectives  76.3 us (68%)
  waiting for transfers between devices  17.4 us (16%)
  Pallas kernels  9.07 us (8%)
  starting transfers between devices  5.19 us (5%)
  local copies, waits for them, and re-layouts  2.75 us (2%)
    all_to_all x6, blocking collectives, trade(): return lax.all_to_all(blocks, 'row', 0, 0)  76.3 us
    ppermute x3, waiting for transfers between devices, local(): shifted.append(lax.ppermute(own, 'col', to_lower))  17.4 us
    pallas_call x7, Pallas kernels, call(): pl.pallas_call(kernel, out_shape=outs, in_specs=[pl.BlockSpec(memory_spac...  9.07 us
    ppermute x3, starting transfers between devices, local(): shifted.append(lax.ppermute(own, 'col', to_lower))  5.19 us
  transfers between devices with their start and end apart: 3, of which 1 were waited for; matrix products, arithmetic and copies ran while one was open for 0% of the time, Pallas kernels for 3%

profile of v1, /device:TPU:0, one launch (start us, length us, event | category | flops | bytes accessed | tf_op | source)
XLA Modules:
  0.0 111.7 jit_solution(8141525569021278956)
XLA Ops:
  0.0 0.7 fusion
  0.7 1.8 %copy.7 = bf16[96,8,8,128]{3,2,1,0:T(8,128)(2,1)S(1)} copy(bf16[96,8,8,128]{3,1,2,0:T(8,128)(2,1)} %bitcast.37) | data formatting | bytes 3145728
  2.5 0.2 bitcast_multiply_fusion
  2.7 0.1 fusion.1
  2.8 0.1 slice.47
  3.0 0.1 slice.45
  3.1 0.1 slice.43
  3.3 0.0 copy-start
  3.3 0.0 copy-start.1
  3.3 0.0 copy-start.2
  3.3 3.0 %collective-permute-start.2 = (bf16[3,128,1024]{2,1,0:T(8,128)(2,1)S(1)}, bf16[3,128,1024]{2,1,0:T(8,128)(2,1)S(1)}, u32[]{:S(2)}, u32[]{:S(2)}) collective-permute-start(bf16[3,128,1024]{2,1,0:T(8,128)(2,1)S(1)} %constant_dynamic-update-slice_fusion.2.refs_3_.refs_6_), channel_id=1, source_target_pairs={{1,0},{0,1},{3,2},{2,3},{5,4},{4,5},{7,6},{6,7},{9,8},{8,9},{11,10... | collective-permute-start | bytes 2359304 | tf_op jit(solution)/shard_map/exchange/ppermute | solution.py:61
  6.4 0.1 slice.41
  6.5 0.1 slice.39
  6.6 0.1 collective-permute-start.1
  6.7 0.1 slice.37.refs_1_.refs_2_
  6.8 2.1 %collective-permute-start = (bf16[1,128,1024]{2,1,0:T(8,128)(2,1)S(1)}, bf16[1,128,1024]{2,1,0:T(8,128)(2,1)S(1)}, u32[]{:S(2)}, u32[]{:S(2)}) collective-permute-start(bf16[1,128,1024]{2,1,0:T(8,128)(2,1)S(1)} %slice.37.refs_1_.refs_2_), channel_id=1, source_target_pairs={{1,0},{0,1},{3,2},{2,3},{5,4},{4,5},{7,6},{6,7},{9,8},{8,9},{11,10... | collective-permute-start | bytes 786440 | tf_op jit(solution)/shard_map/exchange/ppermute | solution.py:61
  8.9 0.0 copy-done
  8.9 0.0 copy-done.1
  8.9 0.0 copy-done.2
  8.9 0.8 forward_first.1
  9.7 13.6 %all_to_all.30.refs_0_ = bf16[16,32,128]{2,1,0:T(8,128)(2,1)S(1)} all-to-all(bf16[16,32,128]{2,1,0:T(8,128)(2,1)S(1)} %get-tuple-element.20), channel_id=1, replica_groups=mesh['row'=16,'col'=2] {'row'}, dimensions={0} | all-to-all | bytes 262144 | tf_op jit(solution)/shard_map/all_to_all | solution.py:70
  23.3 17.4 %collective-permute-done.refs_2_.refs_3_ = bf16[1,128,1024]{2,1,0:T(8,128)(2,1)S(1)} collective-permute-done((bf16[1,128,1024]{2,1,0:T(8,128)(2,1)S(1)}, bf16[1,128,1024]{2,1,0:T(8,128)(2,1)S(1)}, u32[]{:S(2)}, u32[]{:S(2)}) %collective-permute-start) | collective-permute-done | bytes 262176 | tf_op jit(solution)/shard_map/exchange/ppermute | solution.py:61
  40.7 1.2 %forward_level.2 = (f32[32,128]{1,0:T(8,128)S(1)}, bf16[16,32,128]{2,1,0:T(8,128)(2,1)S(1)}) custom-call(s32[4]{0:T(128)S(1)} %bitcast.30, f32[4,32,128]{2,1,0:T(8,128)S(1)} %copy-done.1, f32[4,128,128]{2,1,0:T(8,128)S(1)} %bitcast.23, bf16[16,32,128]{2,1,0:T(8,128)(2,1)S(1)} %all_to_all.30.refs_0_, bf16[1,128,1024]{2,1,0:T(8,128)(2,1)S(1)} %slice.37.refs_1_.refs_2_, ...), custom_call_target="tpu_custom_call" | custom-call | tf_op jit(solution)/shard_map/forward_level/pallas_call | solution.py:20
  42.0 13.9 %all_to_all.31.refs_1_ = bf16[16,32,128]{2,1,0:T(8,128)(2,1)S(1)} all-to-all(bf16[16,32,128]{2,1,0:T(8,128)(2,1)S(1)} %get-tuple-element.22), channel_id=1, replica_groups=mesh['row'=16,'col'=2] {'row'}, dimensions={0} | all-to-all | bytes 262144 | tf_op jit(solution)/shard_map/all_to_all | solution.py:70
  55.8 0.0 collective-permute-done.1.refs_3_.refs_2_.refs_5_
  55.8 1.4 %forward_level.3 = (f32[32,128]{1,0:T(8,128)S(1)}, bf16[16,32,128]{2,1,0:T(8,128)(2,1)S(1)}) custom-call(s32[4]{0:T(128)S(1)} %bitcast.31, f32[4,32,128]{2,1,0:T(8,128)S(1)} %copy-done.1, f32[4,128,128]{2,1,0:T(8,128)S(1)} %bitcast.24, bf16[16,32,128]{2,1,0:T(8,128)(2,1)S(1)} %all_to_all.30.refs_0_, bf16[16,32,128]{2,1,0:T(8,128)(2,1)S(1)} %all_to_all.31.refs_1_, ...), custom_call_target="tpu_custom_call" | custom-call | tf_op jit(solution)/shard_map/forward_level/pallas_call | solution.py:20
  57.2 10.5 %all_to_all.32.refs_2_ = bf16[16,32,128]{2,1,0:T(8,128)(2,1)S(1)} all-to-all(bf16[16,32,128]{2,1,0:T(8,128)(2,1)S(1)} %get-tuple-element.24), channel_id=1, replica_groups=mesh['row'=16,'col'=2] {'row'}, dimensions={0} | all-to-all | bytes 262144 | tf_op jit(solution)/shard_map/all_to_all | solution.py:70
  67.7 0.0 collective-permute-done.2.refs_4_.refs_7_
  67.7 2.1 %top_level.1 = (f32[32,128]{1,0:T(8,128)S(1)}, bf16[32,128]{1,0:T(8,128)(2,1)S(1)}, f32[16,32,128]{2,1,0:T(8,128)S(1)}) custom-call(s32[4]{0:T(128)S(1)} %bitcast.32, f32[4,32,128]{2,1,0:T(8,128)S(1)} %copy-done.1, f32[4,128,128]{2,1,0:T(8,128)S(1)} %bitcast.25, bf16[16,32,128]{2,1,0:T(8,128)(2,1)S(1)} %all_to_all.30.refs_0_, ...), custom_call_target="tpu_custom_call" | custom-call | tf_op jit(solution)/shard_map/top_level/pallas_call | solution.py:20
  69.8 12.6 %all_to_all.33.sums_ref = f32[16,32,128]{2,1,0:T(8,128)S(1)} all-to-all(f32[16,32,128]{2,1,0:T(8,128)S(1)} %get-tuple-element.25), channel_id=1, replica_groups=mesh['row'=16,'col'=2] {'row'}, dimensions={0} | all-to-all | bytes 524288 | tf_op jit(solution)/shard_map/all_to_all | solution.py:70
  82.4 1.0 backward_level.2
  83.4 12.8 %all_to_all.34.sums_ref = f32[16,32,128]{2,1,0:T(8,128)S(1)} all-to-all(f32[16,32,128]{2,1,0:T(8,128)S(1)} %get-tuple-element.27), channel_id=1, replica_groups=mesh['row'=16,'col'=2] {'row'}, dimensions={0} | all-to-all | bytes 524288 | tf_op jit(solution)/shard_map/all_to_all | solution.py:70
  96.2 1.4 %backward_level.3 = (f32[32,128]{1,0:T(8,128)S(1)}, bf16[32,128]{1,0:T(8,128)(2,1)}, f32[16,32,128]{2,1,0:T(8,128)S(1)}) custom-call(s32[4]{0:T(128)S(1)} %bitcast.34, f32[4,128,128]{2,1,0:T(8,128)S(1)} %bitcast.27, f32[32,128]{1,0:T(8,128)S(1)} %get-tuple-element.21.solved_ref, f32[16,32,128]{2,1,0:T(8,128)S(1)} %all_to_all.34.sums_ref, ...), custom_call_target="tpu_custom_call" | custom-call | tf_op jit(solution)/shard_map/backward_level/pallas_call | solution.py:20
  97.6 12.8 %all_to_all.35.sums_ref = f32[16,32,128]{2,1,0:T(8,128)S(1)} all-to-all(f32[16,32,128]{2,1,0:T(8,128)S(1)} %get-tuple-element.29), channel_id=1, replica_groups=mesh['row'=16,'col'=2] {'row'}, dimensions={0} | all-to-all | bytes 524288 | tf_op jit(solution)/shard_map/all_to_all | solution.py:70
  110.4 1.3 %backward_last.1 = f32[4,32,128]{2,1,0:T(8,128)} custom-call(s32[4]{0:T(128)S(1)} %bitcast.35, f32[4,128,128]{2,1,0:T(8,128)S(1)} %bitcast.28, f32[32,128]{1,0:T(8,128)S(1)} %get-tuple-element.19.solved_ref, f32[16,32,128]{2,1,0:T(8,128)S(1)} %all_to_all.35.sums_ref, f32[32,128]{1,0:T(8,128)S(1)} %get-tuple-element.30.refs_0_, ...), custom_call_target="tpu_custom_call" | custom-call | tf_op jit(solution)/shard_map/backward_last/pallas_call | solution.py:20
  (5 shorter events, 0.1 us)
Async XLA Ops:
  3.3 5.7 %copy-start = (f32[4,1,128,128]{3,2,1,0:T(8,128)S(1)}, f32[4,1,128,128]{3,2,1,0:T(8,128)}, u32[]{:S(2)}) copy-start(f32[4,1,128,128]{3,2,1,0:T(8,128)} %param.9) | copy-start | bytes 786436
  3.3 5.7 %copy-start.1 = (f32[4,32,128]{2,1,0:T(8,128)S(1)}, f32[4,32,128]{2,1,0:T(8,128)}, u32[]{:S(2)}) copy-start(f32[4,32,128]{2,1,0:T(8,128)} %rhs_ref.7) | copy-start | bytes 196612
  3.3 5.6 %copy-start.2 = (s32[4,1]{0,1:T(1,128)S(1)}, s32[4,1]{0,1:T(1,128)}, u32[]{:S(2)}) copy-start(s32[4,1]{0,1:T(1,128)} %param.8) | copy-start | bytes 52
  3.3 64.4 %collective-permute-start.2 = (bf16[3,128,1024]{2,1,0:T(8,128)(2,1)S(1)}, bf16[3,128,1024]{2,1,0:T(8,128)(2,1)S(1)}, u32[]{:S(2)}, u32[]{:S(2)}) collective-permute-start(bf16[3,128,1024]{2,1,0:T(8,128)(2,1)S(1)} %constant_dynamic-update-slice_fusion.2.refs_3_.refs_6_), channel_id=1, source_target_pairs={{1,0},{0,1},{3,2},{2,3},{5,4},{4,5},{7,6},{6,7},{9,8},{8,9},{11,10... | collective-permute-start | bytes 2359304 | tf_op jit(solution)/shard_map/exchange/ppermute | solution.py:61
  6.6 49.2 %collective-permute-start.1 = (bf16[2,128,1024]{2,1,0:T(8,128)(2,1)S(1)}, bf16[2,128,1024]{2,1,0:T(8,128)(2,1)S(1)}, u32[]{:S(2)}, u32[]{:S(2)}) collective-permute-start(bf16[2,128,1024]{2,1,0:T(8,128)(2,1)S(1)} %constant_dynamic-update-slice_fusion.refs_2_.refs_1_.refs_4_), channel_id=1, source_target_pairs={{1,0},{0,1},{3,2},{2,3},{5,4},{4,5},{7,6},{6,7},{9,8},{8,9},{11,10... | collective-permute-start | bytes 1572872 | tf_op jit(solution)/shard_map/exchange/ppermute | solution.py:61
  6.8 33.9 %collective-permute-start = (bf16[1,128,1024]{2,1,0:T(8,128)(2,1)S(1)}, bf16[1,128,1024]{2,1,0:T(8,128)(2,1)S(1)}, u32[]{:S(2)}, u32[]{:S(2)}) collective-permute-start(bf16[1,128,1024]{2,1,0:T(8,128)(2,1)S(1)} %slice.37.refs_1_.refs_2_), channel_id=1, source_target_pairs={{1,0},{0,1},{3,2},{2,3},{5,4},{4,5},{7,6},{6,7},{9,8},{8,9},{11,10... | collective-permute-start | bytes 786440 | tf_op jit(solution)/shard_map/exchange/ppermute | solution.py:61

commit v2 on v1

v2 whole, which is shorter than its diff:
```python
import jax
import jax.numpy as jnp
from jax import lax
from jax.experimental import pallas as pl
from jax.experimental.pallas import tpu as pltpu
from jax.sharding import PartitionSpec as P

HIGHEST = lax.Precision.HIGHEST


def pair_lookup(level_count):
    lookup = {}
    for lower_level in range(level_count):
        for above_level in range(lower_level + 1, level_count):
            lookup[above_level, lower_level] = len(lookup)
    return lookup


def call(kernel, outs, *operands, space=pltpu.VMEM, scratch=()):
    return pl.pallas_call(
        kernel,
        out_shape=outs,
        in_specs=[pl.BlockSpec(memory_space=space) for x in operands],
        out_specs=jax.tree.map(lambda _: pl.BlockSpec(memory_space=pltpu.VMEM), outs),
        scratch_shapes=scratch,
        compiler_params=pltpu.CompilerParams(vmem_limit_bytes=48 * 1024 * 1024),
    )(*operands)


def join(blocks):
    return jnp.concatenate([blocks[k] for k in range(blocks.shape[0])], axis=1)


def local(parts, right_sides, factors, pattern, live_widths, inverses):
    row_parts, col_parts = parts
    levels, rhs, width = right_sides.shape
    pairs, _, local_cols = factors.shape
    half = local_cols // width
    total_blocks = half * col_parts
    lookup = pair_lookup(levels)
    needed = [lookup[level, lower] for level in range(1, levels) for lower in range(level)]
    group_size = -(-pairs // (levels - 1))
    groups = [needed[k : k + group_size] for k in range(0, pairs, group_size)]
    place_of = {pair: (g, k) for g, group in enumerate(groups) for k, pair in enumerate(group)}
    inverses = inverses.reshape(levels, width, width)
    f32, bf16 = jnp.float32, jnp.bfloat16

    block_f32 = jax.ShapeDtypeStruct((rhs, width), f32)
    block_bf16 = jax.ShapeDtypeStruct((rhs, width), bf16)
    spread_bf16 = jax.ShapeDtypeStruct((total_blocks, rhs, width), bf16)
    spread_f32 = jax.ShapeDtypeStruct((total_blocks, rhs, width), f32)

    def trade(blocks):
        return lax.all_to_all(blocks, "row", 0, 0)

    def solve_forward(level, live_ref, rhs_ref, inverse_ref, total):
        live = live_ref[level]
        vector = (rhs_ref[level] - total) * live
        product = lax.dot_general(
            vector, inverse_ref[level], (((1,), (1,)), ((), ())), precision=HIGHEST, preferred_element_type=f32
        )
        return product * live

    def solve_backward(level, live_ref, inverse_ref, corrected):
        live = live_ref[level]
        product = lax.dot_general(
            corrected * live, inverse_ref[level], (((1,), (0,)), ((), ())), precision=HIGHEST, preferred_element_type=f32
        )
        return product * live

    def forward_total(gathered, level, matrices):
        mine = lax.axis_index("col")
        total = None
        for shift in range(col_parts):
            start = lax.rem(mine + shift, col_parts) * half
            for lower in range(level):
                left = join(gathered[lower][pl.ds(start, half)])
                term = lax.dot_general(
                    left, matrix(matrices, level, lower, shift), (((1,), (1,)), ((), ())), preferred_element_type=f32
                )
                total = term if total is None else total + term
        return total

    def backward_partials(out_ref, solved, lower, matrices):
        mine = lax.axis_index("col")
        for shift in range(col_parts):
            start = lax.rem(mine + shift, col_parts) * half
            total = None
            for level, vector in solved.items():
                term = lax.dot_general(
                    vector, matrix(matrices, level, lower, shift), (((1,), (0,)), ((), ())), preferred_element_type=f32
                )
                total = term if total is None else total + term
            for block in range(half):
                out_ref[start + block] = total[:, block * width : (block + 1) * width]

    def spread(out_ref, value):
        out_ref[...] = jnp.broadcast_to(value.astype(bf16)[None], out_ref.shape)

    def mask_pair(out_ref, place, pattern_ref, factor_ref, pair):
        for block in range(half):
            columns = slice(block * width, (block + 1) * width)
            kept = jnp.broadcast_to(pattern_ref[pair][:, block : block + 1].astype(f32), (width, width))
            out_ref[place, :, columns] = factor_ref[pair, :, columns] * kept.astype(bf16)

    def first(
        rhs_hbm, factor_hbm, pattern_hbm, widths_hbm, inverse_hbm,
        solved_ref, out_ref, rhs_ref, live_ref, inverse_ref, *refs,
    ):
        masked_refs = refs[: len(groups)]
        factor_ref, pattern_ref, widths_ref, sems = refs[len(groups) :]
        order = needed
        small = [
            pltpu.make_async_copy(pattern_hbm, pattern_ref, sems.at[0]),
            pltpu.make_async_copy(widths_hbm, widths_ref, sems.at[1]),
            pltpu.make_async_copy(rhs_hbm, rhs_ref, sems.at[2]),
            pltpu.make_async_copy(inverse_hbm, inverse_ref, sems.at[3]),
        ]
        large = [
            pltpu.make_async_copy(factor_hbm.at[pair], factor_ref.at[pair], sems.at[4 + k])
            for k, pair in enumerate(order)
        ]
        for copy in small + large:
            copy.start()
        for copy in small:
            copy.wait()
        column = lax.broadcasted_iota(jnp.int32, (1, width), 1)
        for level in range(levels):
            live_ref[level] = (column < widths_ref[level]).astype(f32)
        value = solve_forward(0, live_ref, rhs_ref, inverse_ref, jnp.zeros((rhs, width), f32))
        solved_ref[...] = value
        spread(out_ref, value)
        for copy, pair in zip(large, order):
            copy.wait()
            group, place = place_of[pair]
            mask_pair(masked_refs[group], place, pattern_ref, factor_ref, pair)

    def flat(held):
        return [m for moved in held for m in moved]

    def matrix(refs, level, lower, shift):
        group, place = place_of[lookup[level, lower]]
        return refs[group * col_parts + shift][place]

    def middle(level):
        def body(live_ref, rhs_ref, inverse_ref, *refs):
            gathered, matrices = refs[:level], refs[level:-2]
            solved_ref, out_ref = refs[-2:]
            total = forward_total(gathered, level, matrices)
            value = solve_forward(level, live_ref, rhs_ref, inverse_ref, total)
            solved_ref[...] = value
            spread(out_ref, value)

        return body

    def top(live_ref, rhs_ref, inverse_ref, *refs):
        level = levels - 1
        gathered, matrices = refs[:level], refs[level:-3]
        result_ref, rounded_ref, out_ref = refs[-3:]
        total = forward_total(gathered, level, matrices)
        value = solve_forward(level, live_ref, rhs_ref, inverse_ref, total)
        result = solve_backward(level, live_ref, inverse_ref, value)
        result_ref[...] = result
        rounded = result.astype(bf16)
        rounded_ref[...] = rounded
        backward_partials(out_ref, {level: rounded}, level - 1, matrices)

    def down(level):
        above = levels - 1 - level

        def body(live_ref, inverse_ref, solved_ref, sums_ref, *refs):
            rounded_above = refs[:above]
            matrices = refs[above:-3]
            result_ref, rounded_ref, out_ref = refs[-3:]
            corrected = solved_ref[...] - jnp.sum(sums_ref[...], axis=0)
            result = solve_backward(level, live_ref, inverse_ref, corrected)
            result_ref[...] = result
            rounded = result.astype(bf16)
            rounded_ref[...] = rounded
            solved = {level: rounded}
            for index in range(above):
                solved[level + 1 + index] = rounded_above[index][...]
            backward_partials(out_ref, solved, level - 1, matrices)

        return body

    def last(live_ref, inverse_ref, solved_ref, sums_ref, *refs):
        out_ref = refs[-1]
        corrected = solved_ref[...] - jnp.sum(sums_ref[...], axis=0)
        out_ref[0] = solve_backward(0, live_ref, inverse_ref, corrected)
        for level in range(1, levels):
            out_ref[level] = refs[level - 1][...]

    def exchange(own):
        shifted = [own]
        for shift in range(1, col_parts):
            to_lower = [((q + shift) % col_parts, q) for q in range(col_parts)]
            shifted.append(lax.ppermute(own, "col", to_lower))
        return shifted

    def trade_beside(blocks, group):
        moved = exchange(masked[group]) if group < len(groups) else None
        blocks = trade(blocks)
        for later in range(group + 1, len(groups)):
            masked[later], blocks = lax.optimization_barrier((masked[later], blocks))
        return blocks, moved

    solved, gathered, held = [], [], []
    shaped = lambda *shape: jax.ShapeDtypeStruct(shape, f32)
    with jax.named_scope("forward_first"):
        value, out, right_sides, live, inverses, *masked = call(
            first,
            (block_f32, spread_bf16, shaped(levels, rhs, width), shaped(levels, 1, width), shaped(levels, width, width))
            + tuple(jax.ShapeDtypeStruct((len(group), width, local_cols), bf16) for group in groups),
            right_sides, factors, pattern, live_widths.reshape(levels, 1, 1), inverses,
            space=pltpu.HBM,
            scratch=[
                pltpu.VMEM(factors.shape, bf16),
                pltpu.VMEM(pattern.shape, jnp.int32),
                pltpu.VMEM((levels, 1, 1), jnp.int32),
                pltpu.SemaphoreType.DMA((4 + pairs,)),
            ],
        )
    solved.append(value)
    blocks, moved = trade_beside(out, 0)
    gathered.append(blocks)
    held.append(moved)
    for level in range(1, levels - 1):
        with jax.named_scope("forward_level"):
            value, out = call(middle(level), (block_f32, spread_bf16), live, right_sides, inverses, *gathered, *flat(held))
        solved.append(value)
        blocks, moved = trade_beside(out, level)
        gathered.append(blocks)
        if moved is not None:
            held.append(moved)
    results, rounded = {}, {}
    level = levels - 1
    with jax.named_scope("top_level"):
        results[level], rounded[level], out = call(
            top, (block_f32, block_bf16, spread_f32), live, right_sides, inverses, *gathered, *flat(held)
        )
    sums = trade(out)
    for level in range(levels - 2, 0, -1):
        with jax.named_scope("backward_level"):
            results[level], rounded[level], out = call(
                down(level),
                (block_f32, block_bf16, spread_f32),
                live,
                inverses,
                solved[level],
                sums,
                *[rounded[upper] for upper in range(level + 1, levels)],
                *flat(held),
            )
        sums = trade(out)
    with jax.named_scope("backward_last"):
        return call(
            last,
            jax.ShapeDtypeStruct((levels, rhs, width), f32),
            live,
            inverses,
            solved[0],
            sums,
            *[results[level] for level in range(1, levels)],
        )


def solution(mesh):
    parts = (mesh.shape["row"], mesh.shape["col"])

    def run(*operands):
        return local(parts, *operands)

    return jax.shard_map(
        run,
        mesh=mesh,
        in_specs=(
            P(None, "col", "row"),
            P(None, "row", "col"),
            P(None, "row", "col"),
            P(None, "row"),
            P(None, "row", None, None),
        ),
        out_specs=P(None, "col", "row"),
        check_vma=False,
    )
```

time: 112 us -> 91.4 us (0.82)
  waiting for transfers between devices: 17.4 us -> 0.07 us
  Pallas kernels: 9.07 us -> 6.41 us
  blocking collectives: 76.3 us -> 74.4 us
  local copies, waits for them, and re-layouts: 2.75 us -> 4.62 us
    ppermute x3, waiting for transfers between devices: 17.4 us -> 0.07 us  [exchange(): shifted.append(lax.ppermute(own, 'col', to_lower))]
    pallas_call x7, Pallas kernels: 9.07 us -> 6.41 us  [call(): pl.pallas_call(kernel, out_shape=outs, in_specs=[pl.BlockSpec(memory_spac...]
    unnamed x10 -> x8, local copies, waits for them, and re-layouts: 1.92 us -> 3.88 us
    all_to_all x6, blocking collectives: 76.3 us -> 74.4 us  [trade(): return lax.all_to_all(blocks, 'row', 0, 0)]
  transfers between devices with their start and end apart: 3 -> 3, of which waited for: 1 -> 1; matrix products, arithmetic and copies ran while one was open for 0% -> 0% of each run, Pallas kernels for 3% -> 2%
where the time goes in v2:
time: 91.4 us; the launch traced here: 90.9 us
  blocking collectives  74.4 us (81%)
  Pallas kernels  6.41 us (7%)
  starting transfers between devices  5.36 us (6%)
  local copies, waits for them, and re-layouts  4.62 us (5%)
    all_to_all x6, blocking collectives, trade(): return lax.all_to_all(blocks, 'row', 0, 0)  74.4 us
    pallas_call x7, Pallas kernels, call(): pl.pallas_call(kernel, out_shape=outs, in_specs=[pl.BlockSpec(memory_spac...  6.41 us
    ppermute x3, starting transfers between devices, exchange(): shifted.append(lax.ppermute(own, 'col', to_lower))  5.36 us
    unnamed x8, local copies, waits for them, and re-layouts  3.88 us
  transfers between devices with their start and end apart: 3, of which 1 were waited for; matrix products, arithmetic and copies ran while one was open for 0% of the time, Pallas kernels for 2%

profile of v2, /device:TPU:0, one launch (start us, length us, event | category | flops | bytes accessed | tf_op | source)
XLA Modules:
  0.0 90.9 jit_solution(15748402022980226672)
XLA Ops:
  0.0 0.7 copy.6.widths_hbm
  0.7 0.0 copy-start
  0.7 1.4 %copy-done = bf16[6,128,1024]{2,1,0:T(8,128)(2,1)S(1)} copy-done((bf16[6,128,1024]{2,1,0:T(8,128)(2,1)S(1)}, bf16[6,128,1024]{2,1,0:T(8,128)(2,1)}, u32[]{:S(2)}) %copy-start) | copy-done | bytes 1572888
  2.1 0.0 copy-start.1
  2.2 0.9 %copy-done.1 = f32[4,1,128,128]{3,2,1,0:T(8,128)S(1)} copy-done((f32[4,1,128,128]{3,2,1,0:T(8,128)S(1)}, f32[4,1,128,128]{3,2,1,0:T(8,128)}, u32[]{:S(2)}) %copy-start.1) | copy-done | bytes 262168
  3.1 0.0 copy-start.2
  3.1 0.8 copy-done.2
  3.9 0.0 copy-start.3
  3.9 0.7 copy-done.3
  4.6 1.3 %forward_first.1 = (f32[32,128]{1,0:T(8,128)S(1)}, bf16[16,32,128]{2,1,0:T(8,128)(2,1)S(1)}, f32[4,32,128]{2,1,0:T(8,128)S(1)}, f32[4,1,128]{2,1,0:T(1,128)S(1)}...) custom-call(f32[4,32,128]{2,1,0:T(8,128)S(1)} %copy-done.2, ...), custom_call_target="tpu_custom_call" | custom-call | tf_op jit(solution)/shard_map/forward_first/pallas_call | solution.py:20
  6.0 3.0 %collective-permute-start = (bf16[2,128,1024]{2,1,0:T(8,128)(2,1)S(1)}, bf16[2,128,1024]{2,1,0:T(8,128)(2,1)S(1)}, u32[]{:S(2)}, u32[]{:S(2)}) collective-permute-start(bf16[2,128,1024]{2,1,0:T(8,128)(2,1)S(1)} %get-tuple-element.40.refs_1_.refs_2_.refs_3_), channel_id=1, source_target_pairs={{1,0},{0,1},{3,2},{2,3},{5,4},{4,5},{7,6},{6,7},{9,8},{8,9},{11,10... | collective-permute-start | bytes 1572872 | tf_op jit(solution)/shard_map/ppermute | solution.py:198
  9.0 13.6 %all_to_all.30.refs_0_ = bf16[16,32,128]{2,1,0:T(8,128)(2,1)S(1)} all-to-all(bf16[16,32,128]{2,1,0:T(8,128)(2,1)S(1)} %get-tuple-element.37), channel_id=1, replica_groups=mesh['row'=16,'col'=2] {'row'}, dimensions={0} | all-to-all | bytes 262144 | tf_op jit(solution)/shard_map/all_to_all | solution.py:54
  22.6 0.5 collective-permute-start.1
  23.1 0.0 collective-permute-done.refs_2_.refs_3_.refs_4_
  23.1 0.7 forward_level.2
  23.8 11.6 %all_to_all.31.refs_1_ = bf16[16,32,128]{2,1,0:T(8,128)(2,1)S(1)} all-to-all(bf16[16,32,128]{2,1,0:T(8,128)(2,1)S(1)} %get-tuple-element.43), channel_id=1, replica_groups=mesh['row'=16,'col'=2] {'row'}, dimensions={0} | all-to-all | bytes 262144 | tf_op jit(solution)/shard_map/all_to_all | solution.py:54
  35.5 1.8 %collective-permute-start.2 = (bf16[2,128,1024]{2,1,0:T(8,128)(2,1)S(1)}, bf16[2,128,1024]{2,1,0:T(8,128)(2,1)S(1)}, u32[]{:S(2)}, u32[]{:S(2)}) collective-permute-start(bf16[2,128,1024]{2,1,0:T(8,128)(2,1)S(1)} %get-tuple-element.48.refs_7_.refs_5_.refs_6_), channel_id=1, source_target_pairs={{1,0},{0,1},{3,2},{2,3},{5,4},{4,5},{7,6},{6,7},{9,8},{8,9},{11,10... | collective-permute-start | bytes 1572872 | tf_op jit(solution)/shard_map/ppermute | solution.py:198
  37.3 0.0 collective-permute-done.1.refs_5_.refs_6_.refs_4_
  37.3 0.8 forward_level.3
  38.1 10.5 %all_to_all.32.refs_2_ = bf16[16,32,128]{2,1,0:T(8,128)(2,1)S(1)} all-to-all(bf16[16,32,128]{2,1,0:T(8,128)(2,1)S(1)} %get-tuple-element.47), channel_id=1, replica_groups=mesh['row'=16,'col'=2] {'row'}, dimensions={0} | all-to-all | bytes 262144 | tf_op jit(solution)/shard_map/all_to_all | solution.py:54
  48.6 0.1 collective-permute-done.2.refs_8_.refs_6_.refs_7_
  48.7 1.5 %top_level.1 = (f32[32,128]{1,0:T(8,128)S(1)}, bf16[32,128]{1,0:T(8,128)(2,1)S(1)}, f32[16,32,128]{2,1,0:T(8,128)S(1)}) custom-call(f32[4,1,128]{2,1,0:T(1,128)S(1)} %get-tuple-element.31.live_ref, f32[4,32,128]{2,1,0:T(8,128)S(1)} %get-tuple-element.34.rhs_ref, f32[4,128,128]{2,1,0:T(8,128)S(1)} %get-tuple-element.32.inverse_ref, ...), custom_call_target="tpu_custom_call" | custom-call | tf_op jit(solution)/shard_map/top_level/pallas_call | solution.py:20
  50.2 13.0 %all_to_all.33.sums_ref = f32[16,32,128]{2,1,0:T(8,128)S(1)} all-to-all(f32[16,32,128]{2,1,0:T(8,128)S(1)} %get-tuple-element.49), channel_id=1, replica_groups=mesh['row'=16,'col'=2] {'row'}, dimensions={0} | all-to-all | bytes 524288 | tf_op jit(solution)/shard_map/all_to_all | solution.py:54
  63.2 0.4 backward_level.2
  63.6 12.8 %all_to_all.34.sums_ref = f32[16,32,128]{2,1,0:T(8,128)S(1)} all-to-all(f32[16,32,128]{2,1,0:T(8,128)S(1)} %get-tuple-element.51), channel_id=1, replica_groups=mesh['row'=16,'col'=2] {'row'}, dimensions={0} | all-to-all | bytes 524288 | tf_op jit(solution)/shard_map/all_to_all | solution.py:54
  76.4 0.8 backward_level.3
  77.3 12.8 %all_to_all.35.sums_ref = f32[16,32,128]{2,1,0:T(8,128)S(1)} all-to-all(f32[16,32,128]{2,1,0:T(8,128)S(1)} %get-tuple-element.53), channel_id=1, replica_groups=mesh['row'=16,'col'=2] {'row'}, dimensions={0} | all-to-all | bytes 524288 | tf_op jit(solution)/shard_map/all_to_all | solution.py:54
  90.1 0.8 backward_last.1
Async XLA Ops:
  0.7 1.4 %copy-start = (bf16[6,128,1024]{2,1,0:T(8,128)(2,1)S(1)}, bf16[6,128,1024]{2,1,0:T(8,128)(2,1)}, u32[]{:S(2)}) copy-start(bf16[6,128,1024]{2,1,0:T(8,128)(2,1)} %factor_hbm.1) | copy-start | bytes 4718596
  2.1 0.9 %copy-start.1 = (f32[4,1,128,128]{3,2,1,0:T(8,128)S(1)}, f32[4,1,128,128]{3,2,1,0:T(8,128)}, u32[]{:S(2)}) copy-start(f32[4,1,128,128]{3,2,1,0:T(8,128)} %param.9) | copy-start | bytes 786436
  3.1 0.8 copy-start.2
  3.9 0.7 copy-start.3
  6.0 17.2 %collective-permute-start = (bf16[2,128,1024]{2,1,0:T(8,128)(2,1)S(1)}, bf16[2,128,1024]{2,1,0:T(8,128)(2,1)S(1)}, u32[]{:S(2)}, u32[]{:S(2)}) collective-permute-start(bf16[2,128,1024]{2,1,0:T(8,128)(2,1)S(1)} %get-tuple-element.40.refs_1_.refs_2_.refs_3_), channel_id=1, source_target_pairs={{1,0},{0,1},{3,2},{2,3},{5,4},{4,5},{7,6},{6,7},{9,8},{8,9},{11,10... | collective-permute-start | bytes 1572872 | tf_op jit(solution)/shard_map/ppermute | solution.py:198
  22.6 14.7 %collective-permute-start.1 = (bf16[2,128,1024]{2,1,0:T(8,128)(2,1)S(1)}, bf16[2,128,1024]{2,1,0:T(8,128)(2,1)S(1)}, u32[]{:S(2)}, u32[]{:S(2)}) collective-permute-start(bf16[2,128,1024]{2,1,0:T(8,128)(2,1)S(1)} %get-tuple-element.45.refs_4_.refs_5_.refs_3_), channel_id=1, source_target_pairs={{1,0},{0,1},{3,2},{2,3},{5,4},{4,5},{7,6},{6,7},{9,8},{8,9},{11,10... | collective-permute-start | bytes 1572872 | tf_op jit(solution)/shard_map/ppermute | solution.py:198
  35.5 13.3 %collective-permute-start.2 = (bf16[2,128,1024]{2,1,0:T(8,128)(2,1)S(1)}, bf16[2,128,1024]{2,1,0:T(8,128)(2,1)S(1)}, u32[]{:S(2)}, u32[]{:S(2)}) collective-permute-start(bf16[2,128,1024]{2,1,0:T(8,128)(2,1)S(1)} %get-tuple-element.48.refs_7_.refs_5_.refs_6_), channel_id=1, source_target_pairs={{1,0},{0,1},{3,2},{2,3},{5,4},{4,5},{7,6},{6,7},{9,8},{8,9},{11,10... | collective-permute-start | bytes 1572872 | tf_op jit(solution)/shard_map/ppermute | solution.py:198

commit v3 on v2

--- a/solution.py
+++ b/solution.py
@@ -48,10 +48,18 @@
     block_f32 = jax.ShapeDtypeStruct((rhs, width), f32)
     block_bf16 = jax.ShapeDtypeStruct((rhs, width), bf16)
     spread_bf16 = jax.ShapeDtypeStruct((total_blocks, rhs, width), bf16)
-    spread_f32 = jax.ShapeDtypeStruct((total_blocks, rhs, width), f32)
+    twins = row_parts // 2
+    twins_f32 = jax.ShapeDtypeStruct((twins, rhs, width), f32)
 
     def trade(blocks):
         return lax.all_to_all(blocks, "row", 0, 0)
+
+    def scatter(keep, give):
+        taken = lax.ppermute(give, "row", [(k, k ^ 1) for k in range(row_parts)])
+        with jax.named_scope("sum_twins"):
+            sums = call(add, twins_f32, keep, taken)
+        same_side = [[2 * g + side for g in range(twins)] for side in range(2)]
+        return lax.all_to_all(sums, "row", 0, 0, axis_index_groups=same_side)
 
     def solve_forward(level, live_ref, rhs_ref, inverse_ref, total):
         live = live_ref[level]
@@ -81,8 +89,12 @@
                 total = term if total is None else total + term
         return total
 
-    def backward_partials(out_ref, solved, lower, matrices):
+    def add(left_ref, right_ref, out_ref):
+        out_ref[...] = left_ref[...] + right_ref[...]
+
+    def backward_partials(keep_ref, give_ref, solved, lower, matrices):
         mine = lax.axis_index("col")
+        odd = lax.rem(lax.axis_index("row"), 2) == 1
         for shift in range(col_parts):
             start = lax.rem(mine + shift, col_parts) * half
             total = None
@@ -91,8 +103,11 @@
                     vector, matrix(matrices, level, lower, shift), (((1,), (0,)), ((), ())), preferred_element_type=f32
                 )
                 total = term if total is None else total + term
-            for block in range(half):
-                out_ref[start + block] = total[:, block * width : (block + 1) * width]
+            for block in range(0, half, 2):
+                even = total[:, block * width : (block + 1) * width]
+                uneven = total[:, (block + 1) * width : (block + 2) * width]
+                keep_ref[start // 2 + block // 2] = jnp.where(odd, uneven, even)
+                give_ref[start // 2 + block // 2] = jnp.where(odd, even, uneven)
 
     def spread(out_ref, value):
         out_ref[...] = jnp.broadcast_to(value.astype(bf16)[None], out_ref.shape)
@@ -126,7 +141,7 @@
             copy.wait()
         column = lax.broadcasted_iota(jnp.int32, (1, width), 1)
         for level in range(levels):
-            live_ref[level] = (column < widths_ref[level]).astype(f32)
+            live_ref[level] = (column < widths_ref[:, level : level + 1]).astype(f32)
         value = solve_forward(0, live_ref, rhs_ref, inverse_ref, jnp.zeros((rhs, width), f32))
         solved_ref[...] = value
         spread(out_ref, value)
@@ -155,23 +170,23 @@
 
     def top(live_ref, rhs_ref, inverse_ref, *refs):
         level = levels - 1
-        gathered, matrices = refs[:level], refs[level:-3]
-        result_ref, rounded_ref, out_ref = refs[-3:]
+        gathered, matrices = refs[:level], refs[level:-4]
+        result_ref, rounded_ref, keep_ref, give_ref = refs[-4:]
         total = forward_total(gathered, level, matrices)
         value = solve_forward(level, live_ref, rhs_ref, inverse_ref, total)
         result = solve_backward(level, live_ref, inverse_ref, value)
         result_ref[...] = result
         rounded = result.astype(bf16)
         rounded_ref[...] = rounded
-        backward_partials(out_ref, {level: rounded}, level - 1, matrices)
+        backward_partials(keep_ref, give_ref, {level: rounded}, level - 1, matrices)
 
     def down(level):
         above = levels - 1 - level
 
         def body(live_ref, inverse_ref, solved_ref, sums_ref, *refs):
             rounded_above = refs[:above]
-            matrices = refs[above:-3]
-            result_ref, rounded_ref, out_ref = refs[-3:]
+            matrices = refs[above:-4]
+            result_ref, rounded_ref, keep_ref, give_ref = refs[-4:]
             corrected = solved_ref[...] - jnp.sum(sums_ref[...], axis=0)
             result = solve_backward(level, live_ref, inverse_ref, corrected)
             result_ref[...] = result
@@ -180,7 +195,7 @@
             solved = {level: rounded}
             for index in range(above):
                 solved[level + 1 + index] = rounded_above[index][...]
-            backward_partials(out_ref, solved, level - 1, matrices)
+            backward_partials(keep_ref, give_ref, solved, level - 1, matrices)
 
         return body
 
@@ -208,16 +223,20 @@
     solved, gathered, held = [], [], []
     shaped = lambda *shape: jax.ShapeDtypeStruct(shape, f32)
     with jax.named_scope("forward_first"):
+        operands = [
+            pltpu.with_memory_space_constraint(x, pltpu.HBM)
+            for x in (right_sides, factors, pattern, live_widths.reshape(1, levels), inverses)
+        ]
         value, out, right_sides, live, inverses, *masked = call(
             first,
             (block_f32, spread_bf16, shaped(levels, rhs, width), shaped(levels, 1, width), shaped(levels, width, width))
             + tuple(jax.ShapeDtypeStruct((len(group), width, local_cols), bf16) for group in groups),
-            right_sides, factors, pattern, live_widths.reshape(levels, 1, 1), inverses,
+            *operands,
             space=pltpu.HBM,
             scratch=[
                 pltpu.VMEM(factors.shape, bf16),
                 pltpu.VMEM(pattern.shape, jnp.int32),
-                pltpu.VMEM((levels, 1, 1), jnp.int32),
+                pltpu.VMEM((1, levels), jnp.int32),
                 pltpu.SemaphoreType.DMA((4 + pairs,)),
             ],
         )
@@ -236,15 +255,15 @@
     results, rounded = {}, {}
     level = levels - 1
     with jax.named_scope("top_level"):
-        results[level], rounded[level], out = call(
-            top, (block_f32, block_bf16, spread_f32), live, right_sides, inverses, *gathered, *flat(held)
-        )
-    sums = trade(out)
+        results[level], rounded[level], *halves = call(
+            top, (block_f32, block_bf16, twins_f32, twins_f32), live, right_sides, inverses, *gathered, *flat(held)
+        )
+    sums = scatter(*halves)
     for level in range(levels - 2, 0, -1):
         with jax.named_scope("backward_level"):
-            results[level], rounded[level], out = call(
+            results[level], rounded[level], *halves = call(
                 down(level),
-                (block_f32, block_bf16, spread_f32),
+                (block_f32, block_bf16, twins_f32, twins_f32),
                 live,
                 inverses,
                 solved[level],
@@ -252,7 +271,7 @@
                 *[rounded[upper] for upper in range(level + 1, levels)],
                 *flat(held),
             )
-        sums = trade(out)
+        sums = scatter(*halves)
     with jax.named_scope("backward_last"):
         return call(
             last,

time: 91.4 us -> 83.2 us (0.910)
  blocking collectives: 74.4 us -> 65.9 us
  local copies, waits for them, and re-layouts: 4.62 us -> 0 us
  waiting for transfers between devices: 0.07 us -> 4.09 us
  Pallas kernels: 6.41 us -> 7.33 us
    all_to_all x6 -> x3, blocking collectives: 74.4 us -> 35.8 us  [trade(): return lax.all_to_all(blocks, 'row', 0, 0)]
    all_to_all x0 -> x3, blocking collectives: none -> 30.1 us  [scatter(): return lax.all_to_all(sums, 'row', 0, 0, axis_index_groups=same_side)]
    ppermute x0 -> x3, waiting for transfers between devices: none -> 4.01 us  [scatter(): taken = lax.ppermute(give, 'row', [(k, k ^ 1) for k in range(row_parts)])]
    unnamed x8 -> x0, local copies, waits for them, and re-layouts: 3.88 us -> none
    pallas_call x7 -> x10, Pallas kernels: 6.41 us -> 7.33 us  [call(): pl.pallas_call(kernel, out_shape=outs, in_specs=[pl.BlockSpec(memory_spac...]
  transfers between devices with their start and end apart: 3 -> 6, of which waited for: 1 -> 4; matrix products, arithmetic and copies ran while one was open for 0% -> 0% of each run, Pallas kernels for 2% -> 2%
where the time goes in v3:
time: 83.2 us; the launch traced here: 82.9 us
  blocking collectives  65.9 us (79%)
  Pallas kernels  7.33 us (9%)
  starting transfers between devices  5.5 us (7%)
  waiting for transfers between devices  4.09 us (5%)
    all_to_all x3, blocking collectives, trade(): return lax.all_to_all(blocks, 'row', 0, 0)  35.8 us
    all_to_all x3, blocking collectives, scatter(): return lax.all_to_all(sums, 'row', 0, 0, axis_index_groups=same_side)  30.1 us
    pallas_call x10, Pallas kernels, call(): pl.pallas_call(kernel, out_shape=outs, in_specs=[pl.BlockSpec(memory_spac...  7.33 us
    ppermute x3, starting transfers between devices, exchange(): shifted.append(lax.ppermute(own, 'col', to_lower))  5.36 us
    ppermute x3, waiting for transfers between devices, scatter(): taken = lax.ppermute(give, 'row', [(k, k ^ 1) for k in range(row_parts)])  4.01 us
  transfers between devices with their start and end apart: 6, of which 4 were waited for; matrix products, arithmetic and copies ran while one was open for 0% of the time, Pallas kernels for 2%

profile of v3, /device:TPU:0, one launch (start us, length us, event | category | flops | bytes accessed | tf_op | source)
XLA Modules:
  0.0 82.9 jit_solution(14837970633247667715)
XLA Ops:
  0.0 2.2 %forward_first.1 = (f32[32,128]{1,0:T(8,128)S(1)}, bf16[16,32,128]{2,1,0:T(8,128)(2,1)S(1)}, f32[4,32,128]{2,1,0:T(8,128)S(1)}, f32[4,1,128]{2,1,0:T(1,128)S(1)}...) custom-call(f32[4,32,128]{2,1,0:T(8,128)} %rhs_hbm.1, ...), custom_call_target="tpu_custom_call" | custom-call | tf_op jit(solution)/shard_map/forward_first/pallas_call | solution.py:20
  2.2 3.0 %collective-permute-start = (bf16[2,128,1024]{2,1,0:T(8,128)(2,1)S(1)}, bf16[2,128,1024]{2,1,0:T(8,128)(2,1)S(1)}, u32[]{:S(2)}, u32[]{:S(2)}) collective-permute-start(bf16[2,128,1024]{2,1,0:T(8,128)(2,1)S(1)} %get-tuple-element.43.refs_1_.refs_2_.refs_3_), channel_id=1, source_target_pairs={{1,0},{0,1},{3,2},{2,3},{5,4},{4,5},{7,6},{6,7},{9,8},{8,9},{11,10... | collective-permute-start | bytes 1572872 | tf_op jit(solution)/shard_map/ppermute | solution.py:213
  5.2 13.6 %all_to_all.30.refs_0_ = bf16[16,32,128]{2,1,0:T(8,128)(2,1)S(1)} all-to-all(bf16[16,32,128]{2,1,0:T(8,128)(2,1)S(1)} %get-tuple-element.40), channel_id=1, replica_groups=mesh['row'=16,'col'=2] {'row'}, dimensions={0} | all-to-all | bytes 262144 | tf_op jit(solution)/shard_map/all_to_all | solution.py:55
  18.8 0.5 collective-permute-start.1
  19.3 0.0 collective-permute-done.refs_2_.refs_3_.refs_4_
  19.3 0.7 forward_level.2
  20.0 11.6 %all_to_all.31.refs_1_ = bf16[16,32,128]{2,1,0:T(8,128)(2,1)S(1)} all-to-all(bf16[16,32,128]{2,1,0:T(8,128)(2,1)S(1)} %get-tuple-element.46), channel_id=1, replica_groups=mesh['row'=16,'col'=2] {'row'}, dimensions={0} | all-to-all | bytes 262144 | tf_op jit(solution)/shard_map/all_to_all | solution.py:55
  31.7 1.8 %collective-permute-start.2 = (bf16[2,128,1024]{2,1,0:T(8,128)(2,1)S(1)}, bf16[2,128,1024]{2,1,0:T(8,128)(2,1)S(1)}, u32[]{:S(2)}, u32[]{:S(2)}) collective-permute-start(bf16[2,128,1024]{2,1,0:T(8,128)(2,1)S(1)} %get-tuple-element.51.refs_7_.refs_5_.refs_6_), channel_id=1, source_target_pairs={{1,0},{0,1},{3,2},{2,3},{5,4},{4,5},{7,6},{6,7},{9,8},{8,9},{11,10... | collective-permute-start | bytes 1572872 | tf_op jit(solution)/shard_map/ppermute | solution.py:213
  33.5 0.0 collective-permute-done.1.refs_5_.refs_6_.refs_4_
  33.5 0.8 forward_level.3
  34.3 10.5 %all_to_all.32.refs_2_ = bf16[16,32,128]{2,1,0:T(8,128)(2,1)S(1)} all-to-all(bf16[16,32,128]{2,1,0:T(8,128)(2,1)S(1)} %get-tuple-element.50), channel_id=1, replica_groups=mesh['row'=16,'col'=2] {'row'}, dimensions={0} | all-to-all | bytes 262144 | tf_op jit(solution)/shard_map/all_to_all | solution.py:55
  44.8 0.1 collective-permute-done.2.refs_8_.refs_6_.refs_7_
  44.9 1.5 %top_level.1 = (f32[32,128]{1,0:T(8,128)S(1)}, bf16[32,128]{1,0:T(8,128)(2,1)S(1)}, f32[8,32,128]{2,1,0:T(8,128)S(1)}, f32[8,32,128]{2,1,0:T(8,128)S(1)}) custom-call(f32[4,1,128]{2,1,0:T(1,128)S(1)} %get-tuple-element.34.live_ref, f32[4,32,128]{2,1,0:T(8,128)S(1)} %get-tuple-element.37.rhs_ref, f32[4,128,128]{2,1,0:T(8,128)S(1)} %get-tuple-element.35.inverse_ref, ...), custom_call_target="tpu_custom_call" | custom-call | tf_op jit(solution)/shard_map/top_level/pallas_call | solution.py:20
  46.4 0.1 collective-permute-start.3
  46.5 1.3 %collective-permute-done.3.right_ref = f32[8,32,128]{2,1,0:T(8,128)S(1)} collective-permute-done((f32[8,32,128]{2,1,0:T(8,128)S(1)}, f32[8,32,128]{2,1,0:T(8,128)S(1)}, u32[]{:S(2)}, u32[]{:S(2)}) %collective-permute-start.3) | collective-permute-done | bytes 131104 | tf_op jit(solution)/shard_map/ppermute | solution.py:58
  47.9 10.2 %all_to_all.33.sums_ref = f32[8,32,128]{2,1,0:T(8,128)S(1)} all-to-all(f32[8,32,128]{2,1,0:T(8,128)S(1)} %sum_twins.3), channel_id=1, replica_groups={{0,4,8,12,16,20,24,28},{2,6,10,14,18,22,26,30},{1,5,9,13,17,21,25,29},{..., dimensions={0} | all-to-all | bytes 262144 | tf_op jit(solution)/shard_map/all_to_all | solution.py:62
  58.0 0.4 backward_level.2
  58.4 0.1 collective-permute-start.4
  58.5 1.3 %collective-permute-done.4.right_ref = f32[8,32,128]{2,1,0:T(8,128)S(1)} collective-permute-done((f32[8,32,128]{2,1,0:T(8,128)S(1)}, f32[8,32,128]{2,1,0:T(8,128)S(1)}, u32[]{:S(2)}, u32[]{:S(2)}) %collective-permute-start.4) | collective-permute-done | bytes 131104 | tf_op jit(solution)/shard_map/ppermute | solution.py:58
  59.9 10.0 %all_to_all.34.sums_ref = f32[8,32,128]{2,1,0:T(8,128)S(1)} all-to-all(f32[8,32,128]{2,1,0:T(8,128)S(1)} %sum_twins.4), channel_id=1, replica_groups={{0,4,8,12,16,20,24,28},{2,6,10,14,18,22,26,30},{1,5,9,13,17,21,25,29},{..., dimensions={0} | all-to-all | bytes 262144 | tf_op jit(solution)/shard_map/all_to_all | solution.py:62
  69.8 0.9 %backward_level.3 = (f32[32,128]{1,0:T(8,128)S(1)}, bf16[32,128]{1,0:T(8,128)(2,1)}, f32[8,32,128]{2,1,0:T(8,128)S(1)}, f32[8,32,128]{2,1,0:T(8,128)S(1)}) custom-call(f32[4,1,128]{2,1,0:T(1,128)S(1)} %get-tuple-element.34.live_ref, f32[4,128,128]{2,1,0:T(8,128)S(1)} %get-tuple-element.35.inverse_ref, f32[32,128]{1,0:T(8,128)S(1)} %get-tuple-element.44.solved_ref, ...), custom_call_target="tpu_custom_call" | custom-call | tf_op jit(solution)/shard_map/backward_level/pallas_call | solution.py:20
  70.7 0.0 collective-permute-start.5
  70.7 1.3 %collective-permute-done.5.right_ref = f32[8,32,128]{2,1,0:T(8,128)S(1)} collective-permute-done((f32[8,32,128]{2,1,0:T(8,128)S(1)}, f32[8,32,128]{2,1,0:T(8,128)S(1)}, u32[]{:S(2)}, u32[]{:S(2)}) %collective-permute-start.5) | collective-permute-done | bytes 131104 | tf_op jit(solution)/shard_map/ppermute | solution.py:58
  72.1 10.0 %all_to_all.35.sums_ref = f32[8,32,128]{2,1,0:T(8,128)S(1)} all-to-all(f32[8,32,128]{2,1,0:T(8,128)S(1)} %sum_twins.5), channel_id=1, replica_groups={{0,4,8,12,16,20,24,28},{2,6,10,14,18,22,26,30},{1,5,9,13,17,21,25,29},{..., dimensions={0} | all-to-all | bytes 262144 | tf_op jit(solution)/shard_map/all_to_all | solution.py:62
  82.1 0.8 backward_last.1
  (3 shorter events, 0.1 us)
Async XLA Ops:
  2.2 17.2 %collective-permute-start = (bf16[2,128,1024]{2,1,0:T(8,128)(2,1)S(1)}, bf16[2,128,1024]{2,1,0:T(8,128)(2,1)S(1)}, u32[]{:S(2)}, u32[]{:S(2)}) collective-permute-start(bf16[2,128,1024]{2,1,0:T(8,128)(2,1)S(1)} %get-tuple-element.43.refs_1_.refs_2_.refs_3_), channel_id=1, source_target_pairs={{1,0},{0,1},{3,2},{2,3},{5,4},{4,5},{7,6},{6,7},{9,8},{8,9},{11,10... | collective-permute-start | bytes 1572872 | tf_op jit(solution)/shard_map/ppermute | solution.py:213
  18.8 14.7 %collective-permute-start.1 = (bf16[2,128,1024]{2,1,0:T(8,128)(2,1)S(1)}, bf16[2,128,1024]{2,1,0:T(8,128)(2,1)S(1)}, u32[]{:S(2)}, u32[]{:S(2)}) collective-permute-start(bf16[2,128,1024]{2,1,0:T(8,128)(2,1)S(1)} %get-tuple-element.48.refs_4_.refs_5_.refs_3_), channel_id=1, source_target_pairs={{1,0},{0,1},{3,2},{2,3},{5,4},{4,5},{7,6},{6,7},{9,8},{8,9},{11,10... | collective-permute-start | bytes 1572872 | tf_op jit(solution)/shard_map/ppermute | solution.py:213
  31.7 13.3 %collective-permute-start.2 = (bf16[2,128,1024]{2,1,0:T(8,128)(2,1)S(1)}, bf16[2,128,1024]{2,1,0:T(8,128)(2,1)S(1)}, u32[]{:S(2)}, u32[]{:S(2)}) collective-permute-start(bf16[2,128,1024]{2,1,0:T(8,128)(2,1)S(1)} %get-tuple-element.51.refs_7_.refs_5_.refs_6_), channel_id=1, source_target_pairs={{1,0},{0,1},{3,2},{2,3},{5,4},{4,5},{7,6},{6,7},{9,8},{8,9},{11,10... | collective-permute-start | bytes 1572872 | tf_op jit(solution)/shard_map/ppermute | solution.py:213
  46.4 1.4 %collective-permute-start.3 = (f32[8,32,128]{2,1,0:T(8,128)S(1)}, f32[8,32,128]{2,1,0:T(8,128)S(1)}, u32[]{:S(2)}, u32[]{:S(2)}) collective-permute-start(f32[8,32,128]{2,1,0:T(8,128)S(1)} %get-tuple-element.53), channel_id=1, source_target_pairs={{0,2},{2,0},{4,6},{6,4},{8,10},{10,8},{12,14},{14,12},{16,18},{18,... | collective-permute-start | bytes 393224 | tf_op jit(solution)/shard_map/ppermute | solution.py:58
  58.4 1.4 %collective-permute-start.4 = (f32[8,32,128]{2,1,0:T(8,128)S(1)}, f32[8,32,128]{2,1,0:T(8,128)S(1)}, u32[]{:S(2)}, u32[]{:S(2)}) collective-permute-start(f32[8,32,128]{2,1,0:T(8,128)S(1)} %get-tuple-element.56), channel_id=1, source_target_pairs={{0,2},{2,0},{4,6},{6,4},{8,10},{10,8},{12,14},{14,12},{16,18},{18,... | collective-permute-start | bytes 393224 | tf_op jit(solution)/shard_map/ppermute | solution.py:58
  70.7 1.3 %collective-permute-start.5 = (f32[8,32,128]{2,1,0:T(8,128)S(1)}, f32[8,32,128]{2,1,0:T(8,128)S(1)}, u32[]{:S(2)}, u32[]{:S(2)}) collective-permute-start(f32[8,32,128]{2,1,0:T(8,128)S(1)} %get-tuple-element.59), channel_id=1, source_target_pairs={{0,2},{2,0},{4,6},{6,4},{8,10},{10,8},{12,14},{14,12},{16,18},{18,... | collective-permute-start | bytes 393224 | tf_op jit(solution)/shard_map/ppermute | solution.py:58

commit v4 on v3

--- a/solution.py
+++ b/solution.py
@@ -1,3 +1,5 @@
+import math
+
 import jax
 import jax.numpy as jnp
 from jax import lax
@@ -25,10 +27,6 @@
         scratch_shapes=scratch,
         compiler_params=pltpu.CompilerParams(vmem_limit_bytes=48 * 1024 * 1024),
     )(*operands)
-
-
-def join(blocks):
-    return jnp.concatenate([blocks[k] for k in range(blocks.shape[0])], axis=1)
 
 
 def local(parts, right_sides, factors, pattern, live_widths, inverses):
@@ -51,15 +49,25 @@
     twins = row_parts // 2
     twins_f32 = jax.ShapeDtypeStruct((twins, rhs, width), f32)
 
+    middle_row = row_parts // 2 + 1
+    row_order = [middle_row] + [k for k in range(0, row_parts, 2)] + [k for k in range(1, row_parts, 2) if k != middle_row]
+    step = next(s for s in range(5, 5 + twins) if math.gcd(s, twins) == 1)
+    twin_order = [(twins // 2 + step * k) % twins for k in range(twins)]
+
+    def row_place(index):
+        odd_place = twins + index // 2 + jnp.where(index < middle_row, 1, 0)
+        odd_place = jnp.where(index == middle_row, 0, odd_place)
+        return jnp.where(lax.rem(index, 2) == 0, 1 + index // 2, odd_place)
+
     def trade(blocks):
-        return lax.all_to_all(blocks, "row", 0, 0)
+        return lax.all_to_all(blocks, "row", 0, 0, axis_index_groups=[row_order])
 
     def scatter(keep, give):
         taken = lax.ppermute(give, "row", [(k, k ^ 1) for k in range(row_parts)])
         with jax.named_scope("sum_twins"):
             sums = call(add, twins_f32, keep, taken)
-        same_side = [[2 * g + side for g in range(twins)] for side in range(2)]
-        return lax.all_to_all(sums, "row", 0, 0, axis_index_groups=same_side)
+        one_of_each = [[2 * g + (g + side) % 2 for g in twin_order] for side in (1, 0)]
+        return lax.all_to_all(sums, "row", 0, 0, axis_index_groups=one_of_each)
 
     def solve_forward(level, live_ref, rhs_ref, inverse_ref, total):
         live = live_ref[level]
@@ -82,7 +90,7 @@
         for shift in range(col_parts):
             start = lax.rem(mine + shift, col_parts) * half
             for lower in range(level):
-                left = join(gathered[lower][pl.ds(start, half)])
+                left = jnp.concatenate([gathered[lower][row_place(start + k)] for k in range(half)], axis=1)
                 term = lax.dot_general(
                     left, matrix(matrices, level, lower, shift), (((1,), (1,)), ((), ())), preferred_element_type=f32
                 )
@@ -90,11 +98,12 @@
         return total
 
     def add(left_ref, right_ref, out_ref):
-        out_ref[...] = left_ref[...] + right_ref[...]
+        for place, g in enumerate(twin_order):
+            out_ref[place] = left_ref[g] + right_ref[g]
 
     def backward_partials(keep_ref, give_ref, solved, lower, matrices):
         mine = lax.axis_index("col")
-        odd = lax.rem(lax.axis_index("row"), 2) == 1
+        index = lax.axis_index("row")
         for shift in range(col_parts):
             start = lax.rem(mine + shift, col_parts) * half
             total = None
@@ -106,8 +115,10 @@
             for block in range(0, half, 2):
                 even = total[:, block * width : (block + 1) * width]
                 uneven = total[:, (block + 1) * width : (block + 2) * width]
-                keep_ref[start // 2 + block // 2] = jnp.where(odd, uneven, even)
-                give_ref[start // 2 + block // 2] = jnp.where(odd, even, uneven)
+                g = start // 2 + block // 2
+                odd = lax.rem(index + index // 2 + g, 2) == 1
+                keep_ref[g] = jnp.where(odd, uneven, even)
+                give_ref[g] = jnp.where(odd, even, uneven)
 
     def spread(out_ref, value):
         out_ref[...] = jnp.broadcast_to(value.astype(bf16)[None], out_ref.shape)

time: 83.2 us -> 78.8 us (0.947)
  blocking collectives: 65.9 us -> 58.6 us
  starting transfers between devices: 5.5 us -> 7.08 us
  waiting for transfers between devices: 4.09 us -> 5.38 us
    all_to_all x6, blocking collectives: 65.9 us -> 58.6 us  [the longest x3 32.3 us: trade(): return lax.all_to_all(blocks, 'row', 0, 0, axis_index_groups=[row_order])]
    ppermute x3, waiting for transfers between devices: 0.07 us -> 2.08 us  [exchange(): shifted.append(lax.ppermute(own, 'col', to_lower))]
    ppermute x3, starting transfers between devices: 0.14 us -> 1.21 us  [scatter(): taken = lax.ppermute(give, 'row', [(k, k ^ 1) for k in range(row_parts)])]
  transfers between devices with their start and end apart: 6 -> 6, of which waited for: 4 -> 5; matrix products, arithmetic and copies ran while one was open for 0% -> 0% of each run, Pallas kernels for 2% -> 2%
where the time goes in v4:
time: 78.8 us; the launch traced here: 78.4 us
  blocking collectives  58.6 us (74%)
  Pallas kernels  7.3 us (9%)
  starting transfers between devices  7.08 us (9%)
  waiting for transfers between devices  5.38 us (7%)
    all_to_all x3, blocking collectives, trade(): return lax.all_to_all(blocks, 'row', 0, 0, axis_index_groups=[row_order])  32.3 us
    all_to_all x3, blocking collectives, scatter(): return lax.all_to_all(sums, 'row', 0, 0, axis_index_groups=one_of_each)  26.3 us
    pallas_call x10, Pallas kernels, call(): pl.pallas_call(kernel, out_shape=outs, in_specs=[pl.BlockSpec(memory_spac...  7.3 us
    ppermute x3, starting transfers between devices, exchange(): shifted.append(lax.ppermute(own, 'col', to_lower))  5.87 us
    ppermute x3, waiting for transfers between devices, scatter(): taken = lax.ppermute(give, 'row', [(k, k ^ 1) for k in range(row_parts)])  3.31 us
    ppermute x3, waiting for transfers between devices, exchange(): shifted.append(lax.ppermute(own, 'col', to_lower))  2.08 us
  transfers between devices with their start and end apart: 6, of which 5 were waited for; matrix products, arithmetic and copies ran while one was open for 0% of the time, Pallas kernels for 2%

profile of v4, /device:TPU:0, one launch (start us, length us, event | category | flops | bytes accessed | tf_op | source)
XLA Modules:
  0.0 78.4 jit_solution(5199208730960989778)
XLA Ops:
  0.0 2.2 %forward_first.1 = (f32[32,128]{1,0:T(8,128)S(1)}, bf16[16,32,128]{2,1,0:T(8,128)(2,1)S(1)}, f32[4,32,128]{2,1,0:T(8,128)S(1)}, f32[4,1,128]{2,1,0:T(1,128)S(1)}...) custom-call(f32[4,32,128]{2,1,0:T(8,128)} %rhs_hbm.1, ...), custom_call_target="tpu_custom_call" | custom-call | tf_op jit(solution)/shard_map/forward_first/pallas_call | solution.py:22
  2.2 3.0 %collective-permute-start = (bf16[2,128,1024]{2,1,0:T(8,128)(2,1)S(1)}, bf16[2,128,1024]{2,1,0:T(8,128)(2,1)S(1)}, u32[]{:S(2)}, u32[]{:S(2)}) collective-permute-start(bf16[2,128,1024]{2,1,0:T(8,128)(2,1)S(1)} %get-tuple-element.43.refs_1_.refs_2_.refs_3_), channel_id=1, source_target_pairs={{1,0},{0,1},{3,2},{2,3},{5,4},{4,5},{7,6},{6,7},{9,8},{8,9},{11,10... | collective-permute-start | bytes 1572872 | tf_op jit(solution)/shard_map/ppermute | solution.py:224
  5.2 11.3 %all_to_all.30.refs_0_ = bf16[16,32,128]{2,1,0:T(8,128)(2,1)S(1)} all-to-all(bf16[16,32,128]{2,1,0:T(8,128)(2,1)S(1)} %get-tuple-element.40), channel_id=1, replica_groups={{18,0,4,8,12,16,20,24,28,2,6,10,14,22,26,30},{19,1,5,9,13,17,21,25,29,3..., dimensions={0} | all-to-all | bytes 262144 | tf_op jit(solution)/shard_map/all_to_all | solution.py:63
  16.5 0.5 collective-permute-start.1
  17.0 0.1 collective-permute-done.refs_2_.refs_3_.refs_4_
  17.1 0.7 forward_level.2
  17.8 11.9 %all_to_all.31.refs_1_ = bf16[16,32,128]{2,1,0:T(8,128)(2,1)S(1)} all-to-all(bf16[16,32,128]{2,1,0:T(8,128)(2,1)S(1)} %get-tuple-element.46), channel_id=1, replica_groups={{18,0,4,8,12,16,20,24,28,2,6,10,14,22,26,30},{19,1,5,9,13,17,21,25,29,3..., dimensions={0} | all-to-all | bytes 262144 | tf_op jit(solution)/shard_map/all_to_all | solution.py:63
  29.6 2.3 %collective-permute-start.2 = (bf16[2,128,1024]{2,1,0:T(8,128)(2,1)S(1)}, bf16[2,128,1024]{2,1,0:T(8,128)(2,1)S(1)}, u32[]{:S(2)}, u32[]{:S(2)}) collective-permute-start(bf16[2,128,1024]{2,1,0:T(8,128)(2,1)S(1)} %get-tuple-element.51.refs_7_.refs_5_.refs_6_), channel_id=1, source_target_pairs={{1,0},{0,1},{3,2},{2,3},{5,4},{4,5},{7,6},{6,7},{9,8},{8,9},{11,10... | collective-permute-start | bytes 1572872 | tf_op jit(solution)/shard_map/ppermute | solution.py:224
  32.0 0.0 collective-permute-done.1.refs_5_.refs_6_.refs_4_
  32.0 0.8 %forward_level.3 = (f32[32,128]{1,0:T(8,128)S(1)}, bf16[16,32,128]{2,1,0:T(8,128)(2,1)S(1)}) custom-call(f32[4,1,128]{2,1,0:T(1,128)S(1)} %get-tuple-element.34.live_ref, f32[4,32,128]{2,1,0:T(8,128)S(1)} %get-tuple-element.37.rhs_ref, f32[4,128,128]{2,1,0:T(8,128)S(1)} %get-tuple-element.35.inverse_ref, bf16[16,32,128]{2,1,0:T(8,128)(2,1)S(1)} %all_to_all.30.refs_0_, ...), custom_call_target="tpu_custom_call" | custom-call | tf_op jit(solution)/shard_map/forward_level/pallas_call | solution.py:22
  32.8 9.1 %all_to_all.32.refs_2_ = bf16[16,32,128]{2,1,0:T(8,128)(2,1)S(1)} all-to-all(bf16[16,32,128]{2,1,0:T(8,128)(2,1)S(1)} %get-tuple-element.50), channel_id=1, replica_groups={{18,0,4,8,12,16,20,24,28,2,6,10,14,22,26,30},{19,1,5,9,13,17,21,25,29,3..., dimensions={0} | all-to-all | bytes 262144 | tf_op jit(solution)/shard_map/all_to_all | solution.py:63
  41.9 1.9 %collective-permute-done.2.refs_8_.refs_6_.refs_7_ = bf16[2,128,1024]{2,1,0:T(8,128)(2,1)S(1)} collective-permute-done((bf16[2,128,1024]{2,1,0:T(8,128)(2,1)S(1)}, bf16[2,128,1024]{2,1,0:T(8,128)(2,1)S(1)}, u32[]{:S(2)}, u32[]{:S(2)}) %collective-permute-start.2) | collective-permute-done | bytes 524320 | tf_op jit(solution)/shard_map/ppermute | solution.py:224
  43.9 1.5 %top_level.1 = (f32[32,128]{1,0:T(8,128)S(1)}, bf16[32,128]{1,0:T(8,128)(2,1)S(1)}, f32[8,32,128]{2,1,0:T(8,128)S(1)}, f32[8,32,128]{2,1,0:T(8,128)S(1)}) custom-call(f32[4,1,128]{2,1,0:T(1,128)S(1)} %get-tuple-element.34.live_ref, f32[4,32,128]{2,1,0:T(8,128)S(1)} %get-tuple-element.37.rhs_ref, f32[4,128,128]{2,1,0:T(8,128)S(1)} %get-tuple-element.35.inverse_ref, ...), custom_call_target="tpu_custom_call" | custom-call | tf_op jit(solution)/shard_map/top_level/pallas_call | solution.py:22
  45.4 0.1 collective-permute-start.3
  45.4 1.3 %collective-permute-done.3.right_ref = f32[8,32,128]{2,1,0:T(8,128)S(1)} collective-permute-done((f32[8,32,128]{2,1,0:T(8,128)S(1)}, f32[8,32,128]{2,1,0:T(8,128)S(1)}, u32[]{:S(2)}, u32[]{:S(2)}) %collective-permute-start.3) | collective-permute-done | bytes 131104 | tf_op jit(solution)/shard_map/ppermute | solution.py:66
  46.8 8.6 %all_to_all.33.sums_ref = f32[8,32,128]{2,1,0:T(8,128)S(1)} all-to-all(f32[8,32,128]{2,1,0:T(8,128)S(1)} %sum_twins.3), channel_id=1, replica_groups={{18,4,26,12,2,20,10,28},{16,6,24,14,0,22,8,30},{19,5,27,13,3,21,11,29},..., dimensions={0} | all-to-all | bytes 262144 | tf_op jit(solution)/shard_map/all_to_all | solution.py:70
  55.4 0.4 backward_level.2
  55.8 0.7 collective-permute-start.4
  56.5 1.0 %collective-permute-done.4.right_ref = f32[8,32,128]{2,1,0:T(8,128)S(1)} collective-permute-done((f32[8,32,128]{2,1,0:T(8,128)S(1)}, f32[8,32,128]{2,1,0:T(8,128)S(1)}, u32[]{:S(2)}, u32[]{:S(2)}) %collective-permute-start.4) | collective-permute-done | bytes 131104 | tf_op jit(solution)/shard_map/ppermute | solution.py:66
  57.5 8.8 %all_to_all.34.sums_ref = f32[8,32,128]{2,1,0:T(8,128)S(1)} all-to-all(f32[8,32,128]{2,1,0:T(8,128)S(1)} %sum_twins.4), channel_id=1, replica_groups={{18,4,26,12,2,20,10,28},{16,6,24,14,0,22,8,30},{19,5,27,13,3,21,11,29},..., dimensions={0} | all-to-all | bytes 262144 | tf_op jit(solution)/shard_map/all_to_all | solution.py:70
  66.3 0.9 %backward_level.3 = (f32[32,128]{1,0:T(8,128)S(1)}, bf16[32,128]{1,0:T(8,128)(2,1)}, f32[8,32,128]{2,1,0:T(8,128)S(1)}, f32[8,32,128]{2,1,0:T(8,128)S(1)}) custom-call(f32[4,1,128]{2,1,0:T(1,128)S(1)} %get-tuple-element.34.live_ref, f32[4,128,128]{2,1,0:T(8,128)S(1)} %get-tuple-element.35.inverse_ref, f32[32,128]{1,0:T(8,128)S(1)} %get-tuple-element.44.solved_ref, ...), custom_call_target="tpu_custom_call" | custom-call | tf_op jit(solution)/shard_map/backward_level/pallas_call | solution.py:22
  67.2 0.5 collective-permute-start.5
  67.7 1.0 %collective-permute-done.5.right_ref = f32[8,32,128]{2,1,0:T(8,128)S(1)} collective-permute-done((f32[8,32,128]{2,1,0:T(8,128)S(1)}, f32[8,32,128]{2,1,0:T(8,128)S(1)}, u32[]{:S(2)}, u32[]{:S(2)}) %collective-permute-start.5) | collective-permute-done | bytes 131104 | tf_op jit(solution)/shard_map/ppermute | solution.py:66
  68.7 8.9 %all_to_all.35.sums_ref = f32[8,32,128]{2,1,0:T(8,128)S(1)} all-to-all(f32[8,32,128]{2,1,0:T(8,128)S(1)} %sum_twins.5), channel_id=1, replica_groups={{18,4,26,12,2,20,10,28},{16,6,24,14,0,22,8,30},{19,5,27,13,3,21,11,29},..., dimensions={0} | all-to-all | bytes 262144 | tf_op jit(solution)/shard_map/all_to_all | solution.py:70
  77.6 0.8 %backward_last.1 = f32[4,32,128]{2,1,0:T(8,128)} custom-call(f32[4,1,128]{2,1,0:T(1,128)S(1)} %get-tuple-element.34.live_ref, f32[4,128,128]{2,1,0:T(8,128)S(1)} %get-tuple-element.35.inverse_ref, f32[32,128]{1,0:T(8,128)S(1)} %get-tuple-element.36.solved_ref, f32[8,32,128]{2,1,0:T(8,128)S(1)} %all_to_all.35.sums_ref, ...), custom_call_target="tpu_custom_call" | custom-call | tf_op jit(solution)/shard_map/backward_last/pallas_call | solution.py:22
  (3 shorter events, 0.1 us)
Async XLA Ops:
  2.2 15.0 %collective-permute-start = (bf16[2,128,1024]{2,1,0:T(8,128)(2,1)S(1)}, bf16[2,128,1024]{2,1,0:T(8,128)(2,1)S(1)}, u32[]{:S(2)}, u32[]{:S(2)}) collective-permute-start(bf16[2,128,1024]{2,1,0:T(8,128)(2,1)S(1)} %get-tuple-element.43.refs_1_.refs_2_.refs_3_), channel_id=1, source_target_pairs={{1,0},{0,1},{3,2},{2,3},{5,4},{4,5},{7,6},{6,7},{9,8},{8,9},{11,10... | collective-permute-start | bytes 1572872 | tf_op jit(solution)/shard_map/ppermute | solution.py:224
  16.5 15.5 %collective-permute-start.1 = (bf16[2,128,1024]{2,1,0:T(8,128)(2,1)S(1)}, bf16[2,128,1024]{2,1,0:T(8,128)(2,1)S(1)}, u32[]{:S(2)}, u32[]{:S(2)}) collective-permute-start(bf16[2,128,1024]{2,1,0:T(8,128)(2,1)S(1)} %get-tuple-element.48.refs_4_.refs_5_.refs_3_), channel_id=1, source_target_pairs={{1,0},{0,1},{3,2},{2,3},{5,4},{4,5},{7,6},{6,7},{9,8},{8,9},{11,10... | collective-permute-start | bytes 1572872 | tf_op jit(solution)/shard_map/ppermute | solution.py:224
  29.6 14.2 %collective-permute-start.2 = (bf16[2,128,1024]{2,1,0:T(8,128)(2,1)S(1)}, bf16[2,128,1024]{2,1,0:T(8,128)(2,1)S(1)}, u32[]{:S(2)}, u32[]{:S(2)}) collective-permute-start(bf16[2,128,1024]{2,1,0:T(8,128)(2,1)S(1)} %get-tuple-element.51.refs_7_.refs_5_.refs_6_), channel_id=1, source_target_pairs={{1,0},{0,1},{3,2},{2,3},{5,4},{4,5},{7,6},{6,7},{9,8},{8,9},{11,10... | collective-permute-start | bytes 1572872 | tf_op jit(solution)/shard_map/ppermute | solution.py:224
  45.4 1.4 %collective-permute-start.3 = (f32[8,32,128]{2,1,0:T(8,128)S(1)}, f32[8,32,128]{2,1,0:T(8,128)S(1)}, u32[]{:S(2)}, u32[]{:S(2)}) collective-permute-start(f32[8,32,128]{2,1,0:T(8,128)S(1)} %get-tuple-element.53), channel_id=1, source_target_pairs={{0,2},{2,0},{4,6},{6,4},{8,10},{10,8},{12,14},{14,12},{16,18},{18,... | collective-permute-start | bytes 393224 | tf_op jit(solution)/shard_map/ppermute | solution.py:66
  55.8 1.7 %collective-permute-start.4 = (f32[8,32,128]{2,1,0:T(8,128)S(1)}, f32[8,32,128]{2,1,0:T(8,128)S(1)}, u32[]{:S(2)}, u32[]{:S(2)}) collective-permute-start(f32[8,32,128]{2,1,0:T(8,128)S(1)} %get-tuple-element.56), channel_id=1, source_target_pairs={{0,2},{2,0},{4,6},{6,4},{8,10},{10,8},{12,14},{14,12},{16,18},{18,... | collective-permute-start | bytes 393224 | tf_op jit(solution)/shard_map/ppermute | solution.py:66
  67.2 1.4 %collective-permute-start.5 = (f32[8,32,128]{2,1,0:T(8,128)S(1)}, f32[8,32,128]{2,1,0:T(8,128)S(1)}, u32[]{:S(2)}, u32[]{:S(2)}) collective-permute-start(f32[8,32,128]{2,1,0:T(8,128)S(1)} %get-tuple-element.59), channel_id=1, source_target_pairs={{0,2},{2,0},{4,6},{6,4},{8,10},{10,8},{12,14},{14,12},{16,18},{18,... | collective-permute-start | bytes 393224 | tf_op jit(solution)/shard_map/ppermute | solution.py:66

commit v5 on v4

--- a/solution.py
+++ b/solution.py
@@ -18,11 +18,11 @@
     return lookup
 
 
-def call(kernel, outs, *operands, space=pltpu.VMEM, scratch=()):
+def call(kernel, outs, *operands, space=pltpu.VMEM, spaces=None, scratch=()):
     return pl.pallas_call(
         kernel,
         out_shape=outs,
-        in_specs=[pl.BlockSpec(memory_space=space) for x in operands],
+        in_specs=[pl.BlockSpec(memory_space=s) for s in (spaces or [space] * len(operands))],
         out_specs=jax.tree.map(lambda _: pl.BlockSpec(memory_space=pltpu.VMEM), outs),
         scratch_shapes=scratch,
         compiler_params=pltpu.CompilerParams(vmem_limit_bytes=48 * 1024 * 1024),
@@ -129,15 +129,31 @@
             kept = jnp.broadcast_to(pattern_ref[pair][:, block : block + 1].astype(f32), (width, width))
             out_ref[place, :, columns] = factor_ref[pair, :, columns] * kept.astype(bf16)
 
+    def first_mask(factor_hbm, pattern_hbm, masked_ref, pattern_out, factor_ref, pattern_ref, sems):
+        order = groups[0]
+        small = [pltpu.make_async_copy(pattern_hbm, pattern_ref, sems.at[0])]
+        large = [
+            pltpu.make_async_copy(factor_hbm.at[pair], factor_ref.at[pair], sems.at[1 + k])
+            for k, pair in enumerate(order)
+        ]
+        for copy in small + large:
+            copy.start()
+        for copy in small:
+            copy.wait()
+        pattern_out[...] = pattern_ref[...]
+        for copy, pair in zip(large, order):
+            copy.wait()
+            group, place = place_of[pair]
+            mask_pair(masked_ref, place, pattern_ref, factor_ref, pair)
+
     def first(
-        rhs_hbm, factor_hbm, pattern_hbm, widths_hbm, inverse_hbm,
+        rhs_hbm, factor_hbm, pattern_ref, widths_hbm, inverse_hbm,
         solved_ref, out_ref, rhs_ref, live_ref, inverse_ref, *refs,
     ):
-        masked_refs = refs[: len(groups)]
-        factor_ref, pattern_ref, widths_ref, sems = refs[len(groups) :]
-        order = needed
+        masked_refs = [None, *refs[: len(groups) - 1]]
+        factor_ref, widths_ref, sems = refs[len(groups) - 1 :]
+        order = needed[len(groups[0]) :]
         small = [
-            pltpu.make_async_copy(pattern_hbm, pattern_ref, sems.at[0]),
             pltpu.make_async_copy(widths_hbm, widths_ref, sems.at[1]),
             pltpu.make_async_copy(rhs_hbm, rhs_ref, sems.at[2]),
             pltpu.make_async_copy(inverse_hbm, inverse_ref, sems.at[3]),
@@ -238,19 +254,29 @@
             pltpu.with_memory_space_constraint(x, pltpu.HBM)
             for x in (right_sides, factors, pattern, live_widths.reshape(1, levels), inverses)
         ]
+        masked0, pattern_vmem = call(first_mask,
+            (jax.ShapeDtypeStruct((len(groups[0]), width, local_cols), bf16), jax.ShapeDtypeStruct(pattern.shape, jnp.int32)),
+            operands[1], operands[2], space=pltpu.HBM,
+            scratch=[
+                pltpu.VMEM(factors.shape, bf16),
+                pltpu.VMEM(pattern.shape, jnp.int32),
+                pltpu.SemaphoreType.DMA((1 + pairs,)),
+            ],
+        )
+        operands[2] = pattern_vmem
         value, out, right_sides, live, inverses, *masked = call(
             first,
             (block_f32, spread_bf16, shaped(levels, rhs, width), shaped(levels, 1, width), shaped(levels, width, width))
-            + tuple(jax.ShapeDtypeStruct((len(group), width, local_cols), bf16) for group in groups),
+            + tuple(jax.ShapeDtypeStruct((len(group), width, local_cols), bf16) for group in groups[1:]),
             *operands,
-            space=pltpu.HBM,
+            spaces=[pltpu.HBM, pltpu.HBM, pltpu.VMEM, pltpu.HBM, pltpu.HBM],
             scratch=[
                 pltpu.VMEM(factors.shape, bf16),
-                pltpu.VMEM(pattern.shape, jnp.int32),
                 pltpu.VMEM((1, levels), jnp.int32),
                 pltpu.SemaphoreType.DMA((4 + pairs,)),
             ],
         )
+        masked = [masked0, *masked]
     solved.append(value)
     blocks, moved = trade_beside(out, 0)
     gathered.append(blocks)

time: 78.8 us -> 77.3 us (0.981)
  blocking collectives: 58.6 us -> 56.8 us
  Pallas kernels: 7.3 us -> 8.31 us
  starting transfers between devices: 7.08 us -> 6.27 us
    all_to_all x3, blocking collectives: 32.3 us -> 30.5 us  [trade(): return lax.all_to_all(blocks, 'row', 0, 0, axis_index_groups=[row_order])]
    pallas_call x10 -> x11, Pallas kernels: 7.3 us -> 8.31 us  [call(): pl.pallas_call(kernel, out_shape=outs, in_specs=[pl.BlockSpec(memory_spac...]
    ppermute x3, starting transfers between devices: 5.87 us -> 5.06 us  [exchange(): shifted.append(lax.ppermute(own, 'col', to_lower))]
  transfers between devices with their start and end apart: 6 -> 6, of which waited for: 5 -> 5; matrix products, arithmetic and copies ran while one was open for 0% -> 0% of each run, Pallas kernels for 2% -> 4%
where the time goes in v5:
time: 77.3 us; the launch traced here: 76.9 us
  blocking collectives  56.8 us (73%)
  Pallas kernels  8.31 us (11%)
  starting transfers between devices  6.27 us (8%)
  waiting for transfers between devices  5.48 us (7%)
    all_to_all x3, blocking collectives, trade(): return lax.all_to_all(blocks, 'row', 0, 0, axis_index_groups=[row_order])  30.5 us
    all_to_all x3, blocking collectives, scatter(): return lax.all_to_all(sums, 'row', 0, 0, axis_index_groups=one_of_each)  26.3 us
    pallas_call x11, Pallas kernels, call(): pl.pallas_call(kernel, out_shape=outs, in_specs=[pl.BlockSpec(memory_spac...  8.31 us
    ppermute x3, starting transfers between devices, exchange(): shifted.append(lax.ppermute(own, 'col', to_lower))  5.06 us
    ppermute x3, waiting for transfers between devices, scatter(): taken = lax.ppermute(give, 'row', [(k, k ^ 1) for k in range(row_parts)])  3.31 us
    ppermute x3, waiting for transfers between devices, exchange(): shifted.append(lax.ppermute(own, 'col', to_lower))  2.17 us
  transfers between devices with their start and end apart: 6, of which 5 were waited for; matrix products, arithmetic and copies ran while one was open for 0% of the time, Pallas kernels for 4%

profile of v5, /device:TPU:0, one launch (start us, length us, event | category | flops | bytes accessed | tf_op | source)
XLA Modules:
  0.0 76.9 jit_solution(48965610432029910)
XLA Ops:
  0.0 1.3 %forward_first.2 = (bf16[2,128,1024]{2,1,0:T(8,128)(2,1)S(1)}, s32[6,1,8]{2,1,0:T(1,128)S(1)}) custom-call(bf16[6,128,1024]{2,1,0:T(8,128)(2,1)} %factor_hbm.3, s32[6,1,8]{2,1,0:T(1,128)} %pattern_hbm.1), custom_call_target="tpu_custom_call" | custom-call | tf_op jit(solution)/shard_map/forward_first/pallas_call | solution.py:22
  1.3 3.0 %collective-permute-start = (bf16[2,128,1024]{2,1,0:T(8,128)(2,1)S(1)}, bf16[2,128,1024]{2,1,0:T(8,128)(2,1)S(1)}, u32[]{:S(2)}, u32[]{:S(2)}) collective-permute-start(bf16[2,128,1024]{2,1,0:T(8,128)(2,1)S(1)} %get-tuple-element.45.refs_1_.refs_2_.refs_3_), channel_id=1, source_target_pairs={{1,0},{0,1},{3,2},{2,3},{5,4},{4,5},{7,6},{6,7},{9,8},{8,9},{11,10... | collective-permute-start | bytes 1572872 | tf_op jit(solution)/shard_map/ppermute | solution.py:240
  4.3 1.9 %forward_first.3 = (f32[32,128]{1,0:T(8,128)S(1)}, bf16[16,32,128]{2,1,0:T(8,128)(2,1)S(1)}, f32[4,32,128]{2,1,0:T(8,128)S(1)}, f32[4,1,128]{2,1,0:T(1,128)S(1)}...) custom-call(f32[4,32,128]{2,1,0:T(8,128)} %rhs_hbm.1, ...), custom_call_target="tpu_custom_call" | custom-call | tf_op jit(solution)/shard_map/forward_first/pallas_call | solution.py:22
  6.2 11.3 %all_to_all.30.refs_0_ = bf16[16,32,128]{2,1,0:T(8,128)(2,1)S(1)} all-to-all(bf16[16,32,128]{2,1,0:T(8,128)(2,1)S(1)} %get-tuple-element.42), channel_id=1, replica_groups={{18,0,4,8,12,16,20,24,28,2,6,10,14,22,26,30},{19,1,5,9,13,17,21,25,29,3..., dimensions={0} | all-to-all | bytes 262144 | tf_op jit(solution)/shard_map/all_to_all | solution.py:63
  17.5 0.5 collective-permute-start.1
  18.0 0.0 collective-permute-done.refs_2_.refs_3_.refs_4_
  18.0 0.7 forward_level.2
  18.7 9.7 %all_to_all.31.refs_1_ = bf16[16,32,128]{2,1,0:T(8,128)(2,1)S(1)} all-to-all(bf16[16,32,128]{2,1,0:T(8,128)(2,1)S(1)} %get-tuple-element.48), channel_id=1, replica_groups={{18,0,4,8,12,16,20,24,28,2,6,10,14,22,26,30},{19,1,5,9,13,17,21,25,29,3..., dimensions={0} | all-to-all | bytes 262144 | tf_op jit(solution)/shard_map/all_to_all | solution.py:63
  28.4 1.5 %collective-permute-start.2 = (bf16[2,128,1024]{2,1,0:T(8,128)(2,1)S(1)}, bf16[2,128,1024]{2,1,0:T(8,128)(2,1)S(1)}, u32[]{:S(2)}, u32[]{:S(2)}) collective-permute-start(bf16[2,128,1024]{2,1,0:T(8,128)(2,1)S(1)} %get-tuple-element.53.refs_7_.refs_5_.refs_6_), channel_id=1, source_target_pairs={{1,0},{0,1},{3,2},{2,3},{5,4},{4,5},{7,6},{6,7},{9,8},{8,9},{11,10... | collective-permute-start | bytes 1572872 | tf_op jit(solution)/shard_map/ppermute | solution.py:240
  30.0 1.4 %collective-permute-done.1.refs_5_.refs_6_.refs_4_ = bf16[2,128,1024]{2,1,0:T(8,128)(2,1)S(1)} collective-permute-done((bf16[2,128,1024]{2,1,0:T(8,128)(2,1)S(1)}, bf16[2,128,1024]{2,1,0:T(8,128)(2,1)S(1)}, u32[]{:S(2)}, u32[]{:S(2)}) %collective-permute-start.1) | collective-permute-done | bytes 524320 | tf_op jit(solution)/shard_map/ppermute | solution.py:240
  31.4 0.8 %forward_level.3 = (f32[32,128]{1,0:T(8,128)S(1)}, bf16[16,32,128]{2,1,0:T(8,128)(2,1)S(1)}) custom-call(f32[4,1,128]{2,1,0:T(1,128)S(1)} %get-tuple-element.36.live_ref, f32[4,32,128]{2,1,0:T(8,128)S(1)} %get-tuple-element.39.rhs_ref, f32[4,128,128]{2,1,0:T(8,128)S(1)} %get-tuple-element.37.inverse_ref, bf16[16,32,128]{2,1,0:T(8,128)(2,1)S(1)} %all_to_all.30.refs_0_, ...), custom_call_target="tpu_custom_call" | custom-call | tf_op jit(solution)/shard_map/forward_level/pallas_call | solution.py:22
  32.2 9.5 %all_to_all.32.refs_2_ = bf16[16,32,128]{2,1,0:T(8,128)(2,1)S(1)} all-to-all(bf16[16,32,128]{2,1,0:T(8,128)(2,1)S(1)} %get-tuple-element.52), channel_id=1, replica_groups={{18,0,4,8,12,16,20,24,28,2,6,10,14,22,26,30},{19,1,5,9,13,17,21,25,29,3..., dimensions={0} | all-to-all | bytes 262144 | tf_op jit(solution)/shard_map/all_to_all | solution.py:63
  41.6 0.7 collective-permute-done.2.refs_8_.refs_6_.refs_7_
  42.4 1.5 %top_level.1 = (f32[32,128]{1,0:T(8,128)S(1)}, bf16[32,128]{1,0:T(8,128)(2,1)S(1)}, f32[8,32,128]{2,1,0:T(8,128)S(1)}, f32[8,32,128]{2,1,0:T(8,128)S(1)}) custom-call(f32[4,1,128]{2,1,0:T(1,128)S(1)} %get-tuple-element.36.live_ref, f32[4,32,128]{2,1,0:T(8,128)S(1)} %get-tuple-element.39.rhs_ref, f32[4,128,128]{2,1,0:T(8,128)S(1)} %get-tuple-element.37.inverse_ref, ...), custom_call_target="tpu_custom_call" | custom-call | tf_op jit(solution)/shard_map/top_level/pallas_call | solution.py:22
  43.9 0.1 collective-permute-start.3
  44.0 1.3 %collective-permute-done.3.right_ref = f32[8,32,128]{2,1,0:T(8,128)S(1)} collective-permute-done((f32[8,32,128]{2,1,0:T(8,128)S(1)}, f32[8,32,128]{2,1,0:T(8,128)S(1)}, u32[]{:S(2)}, u32[]{:S(2)}) %collective-permute-start.3) | collective-permute-done | bytes 131104 | tf_op jit(solution)/shard_map/ppermute | solution.py:66
  45.3 8.6 %all_to_all.33.sums_ref = f32[8,32,128]{2,1,0:T(8,128)S(1)} all-to-all(f32[8,32,128]{2,1,0:T(8,128)S(1)} %sum_twins.3), channel_id=1, replica_groups={{18,4,26,12,2,20,10,28},{16,6,24,14,0,22,8,30},{19,5,27,13,3,21,11,29},..., dimensions={0} | all-to-all | bytes 262144 | tf_op jit(solution)/shard_map/all_to_all | solution.py:70
  53.9 0.4 backward_level.2
  54.3 0.7 collective-permute-start.4
  55.0 1.0 %collective-permute-done.4.right_ref = f32[8,32,128]{2,1,0:T(8,128)S(1)} collective-permute-done((f32[8,32,128]{2,1,0:T(8,128)S(1)}, f32[8,32,128]{2,1,0:T(8,128)S(1)}, u32[]{:S(2)}, u32[]{:S(2)}) %collective-permute-start.4) | collective-permute-done | bytes 131104 | tf_op jit(solution)/shard_map/ppermute | solution.py:66
  56.0 8.8 %all_to_all.34.sums_ref = f32[8,32,128]{2,1,0:T(8,128)S(1)} all-to-all(f32[8,32,128]{2,1,0:T(8,128)S(1)} %sum_twins.4), channel_id=1, replica_groups={{18,4,26,12,2,20,10,28},{16,6,24,14,0,22,8,30},{19,5,27,13,3,21,11,29},..., dimensions={0} | all-to-all | bytes 262144 | tf_op jit(solution)/shard_map/all_to_all | solution.py:70
  64.8 0.9 %backward_level.3 = (f32[32,128]{1,0:T(8,128)S(1)}, bf16[32,128]{1,0:T(8,128)(2,1)}, f32[8,32,128]{2,1,0:T(8,128)S(1)}, f32[8,32,128]{2,1,0:T(8,128)S(1)}) custom-call(f32[4,1,128]{2,1,0:T(1,128)S(1)} %get-tuple-element.36.live_ref, f32[4,128,128]{2,1,0:T(8,128)S(1)} %get-tuple-element.37.inverse_ref, f32[32,128]{1,0:T(8,128)S(1)} %get-tuple-element.46.solved_ref, ...), custom_call_target="tpu_custom_call" | custom-call | tf_op jit(solution)/shard_map/backward_level/pallas_call | solution.py:22
  65.7 0.5 collective-permute-start.5
  66.2 1.0 %collective-permute-done.5.right_ref = f32[8,32,128]{2,1,0:T(8,128)S(1)} collective-permute-done((f32[8,32,128]{2,1,0:T(8,128)S(1)}, f32[8,32,128]{2,1,0:T(8,128)S(1)}, u32[]{:S(2)}, u32[]{:S(2)}) %collective-permute-start.5) | collective-permute-done | bytes 131104 | tf_op jit(solution)/shard_map/ppermute | solution.py:66
  67.2 8.9 %all_to_all.35.sums_ref = f32[8,32,128]{2,1,0:T(8,128)S(1)} all-to-all(f32[8,32,128]{2,1,0:T(8,128)S(1)} %sum_twins.5), channel_id=1, replica_groups={{18,4,26,12,2,20,10,28},{16,6,24,14,0,22,8,30},{19,5,27,13,3,21,11,29},..., dimensions={0} | all-to-all | bytes 262144 | tf_op jit(solution)/shard_map/all_to_all | solution.py:70
  76.1 0.8 %backward_last.1 = f32[4,32,128]{2,1,0:T(8,128)} custom-call(f32[4,1,128]{2,1,0:T(1,128)S(1)} %get-tuple-element.36.live_ref, f32[4,128,128]{2,1,0:T(8,128)S(1)} %get-tuple-element.37.inverse_ref, f32[32,128]{1,0:T(8,128)S(1)} %get-tuple-element.38.solved_ref, f32[8,32,128]{2,1,0:T(8,128)S(1)} %all_to_all.35.sums_ref, ...), custom_call_target="tpu_custom_call" | custom-call | tf_op jit(solution)/shard_map/backward_last/pallas_call | solution.py:22
  (3 shorter events, 0.1 us)
Async XLA Ops:
  1.3 16.7 %collective-permute-start = (bf16[2,128,1024]{2,1,0:T(8,128)(2,1)S(1)}, bf16[2,128,1024]{2,1,0:T(8,128)(2,1)S(1)}, u32[]{:S(2)}, u32[]{:S(2)}) collective-permute-start(bf16[2,128,1024]{2,1,0:T(8,128)(2,1)S(1)} %get-tuple-element.45.refs_1_.refs_2_.refs_3_), channel_id=1, source_target_pairs={{1,0},{0,1},{3,2},{2,3},{5,4},{4,5},{7,6},{6,7},{9,8},{8,9},{11,10... | collective-permute-start | bytes 1572872 | tf_op jit(solution)/shard_map/ppermute | solution.py:240
  17.5 13.9 %collective-permute-start.1 = (bf16[2,128,1024]{2,1,0:T(8,128)(2,1)S(1)}, bf16[2,128,1024]{2,1,0:T(8,128)(2,1)S(1)}, u32[]{:S(2)}, u32[]{:S(2)}) collective-permute-start(bf16[2,128,1024]{2,1,0:T(8,128)(2,1)S(1)} %get-tuple-element.50.refs_4_.refs_5_.refs_3_), channel_id=1, source_target_pairs={{1,0},{0,1},{3,2},{2,3},{5,4},{4,5},{7,6},{6,7},{9,8},{8,9},{11,10... | collective-permute-start | bytes 1572872 | tf_op jit(solution)/shard_map/ppermute | solution.py:240
  28.4 13.9 %collective-permute-start.2 = (bf16[2,128,1024]{2,1,0:T(8,128)(2,1)S(1)}, bf16[2,128,1024]{2,1,0:T(8,128)(2,1)S(1)}, u32[]{:S(2)}, u32[]{:S(2)}) collective-permute-start(bf16[2,128,1024]{2,1,0:T(8,128)(2,1)S(1)} %get-tuple-element.53.refs_7_.refs_5_.refs_6_), channel_id=1, source_target_pairs={{1,0},{0,1},{3,2},{2,3},{5,4},{4,5},{7,6},{6,7},{9,8},{8,9},{11,10... | collective-permute-start | bytes 1572872 | tf_op jit(solution)/shard_map/ppermute | solution.py:240
  43.9 1.4 %collective-permute-start.3 = (f32[8,32,128]{2,1,0:T(8,128)S(1)}, f32[8,32,128]{2,1,0:T(8,128)S(1)}, u32[]{:S(2)}, u32[]{:S(2)}) collective-permute-start(f32[8,32,128]{2,1,0:T(8,128)S(1)} %get-tuple-element.55), channel_id=1, source_target_pairs={{0,2},{2,0},{4,6},{6,4},{8,10},{10,8},{12,14},{14,12},{16,18},{18,... | collective-permute-start | bytes 393224 | tf_op jit(solution)/shard_map/ppermute | solution.py:66
  54.3 1.7 %collective-permute-start.4 = (f32[8,32,128]{2,1,0:T(8,128)S(1)}, f32[8,32,128]{2,1,0:T(8,128)S(1)}, u32[]{:S(2)}, u32[]{:S(2)}) collective-permute-start(f32[8,32,128]{2,1,0:T(8,128)S(1)} %get-tuple-element.58), channel_id=1, source_target_pairs={{0,2},{2,0},{4,6},{6,4},{8,10},{10,8},{12,14},{14,12},{16,18},{18,... | collective-permute-start | bytes 393224 | tf_op jit(solution)/shard_map/ppermute | solution.py:66
  65.7 1.4 %collective-permute-start.5 = (f32[8,32,128]{2,1,0:T(8,128)S(1)}, f32[8,32,128]{2,1,0:T(8,128)S(1)}, u32[]{:S(2)}, u32[]{:S(2)}) collective-permute-start(f32[8,32,128]{2,1,0:T(8,128)S(1)} %get-tuple-element.61), channel_id=1, source_target_pairs={{0,2},{2,0},{4,6},{6,4},{8,10},{10,8},{12,14},{14,12},{16,18},{18,... | collective-permute-start | bytes 393224 | tf_op jit(solution)/shard_map/ppermute | solution.py:66

commit v6 on v5

--- a/solution.py
+++ b/solution.py
@@ -62,12 +62,14 @@
     def trade(blocks):
         return lax.all_to_all(blocks, "row", 0, 0, axis_index_groups=[row_order])
 
-    def scatter(keep, give):
+    def scatter(keep, give, early=None):
         taken = lax.ppermute(give, "row", [(k, k ^ 1) for k in range(row_parts)])
+        begun = early() if early else ()
         with jax.named_scope("sum_twins"):
             sums = call(add, twins_f32, keep, taken)
+        sums, begun = lax.optimization_barrier((sums, begun))
         one_of_each = [[2 * g + (g + side) % 2 for g in twin_order] for side in (1, 0)]
-        return lax.all_to_all(sums, "row", 0, 0, axis_index_groups=one_of_each)
+        return lax.all_to_all(sums, "row", 0, 0, axis_index_groups=one_of_each), begun
 
     def solve_forward(level, live_ref, rhs_ref, inverse_ref, total):
         live = live_ref[level]
@@ -101,7 +103,7 @@
         for place, g in enumerate(twin_order):
             out_ref[place] = left_ref[g] + right_ref[g]
 
-    def backward_partials(keep_ref, give_ref, solved, lower, matrices):
+    def backward_partials(keep_ref, give_ref, solved, lower, matrices, begun=None):
         mine = lax.axis_index("col")
         index = lax.axis_index("row")
         for shift in range(col_parts):
@@ -116,9 +118,10 @@
                 even = total[:, block * width : (block + 1) * width]
                 uneven = total[:, (block + 1) * width : (block + 2) * width]
                 g = start // 2 + block // 2
+                kept, given = (0.0, 0.0) if begun is None else (begun[0][g], begun[1][g])
                 odd = lax.rem(index + index // 2 + g, 2) == 1
-                keep_ref[g] = jnp.where(odd, uneven, even)
-                give_ref[g] = jnp.where(odd, even, uneven)
+                keep_ref[g] = jnp.where(odd, uneven, even) + kept
+                give_ref[g] = jnp.where(odd, even, uneven) + given
 
     def spread(out_ref, value):
         out_ref[...] = jnp.broadcast_to(value.astype(bf16)[None], out_ref.shape)
@@ -207,22 +210,29 @@
         rounded_ref[...] = rounded
         backward_partials(keep_ref, give_ref, {level: rounded}, level - 1, matrices)
 
+    def backward_early(lower):
+        known = range(lower + 2, levels)
+
+        def body(*refs):
+            solved = {level: refs[k][...] for k, level in enumerate(known)}
+            matrices, (keep_ref, give_ref) = refs[len(known) : -2], refs[-2:]
+            backward_partials(keep_ref, give_ref, solved, lower, matrices)
+
+        return body
+
     def down(level):
-        above = levels - 1 - level
-
-        def body(live_ref, inverse_ref, solved_ref, sums_ref, *refs):
-            rounded_above = refs[:above]
-            matrices = refs[above:-4]
-            result_ref, rounded_ref, keep_ref, give_ref = refs[-4:]
+        def body(live_ref, inverse_ref, solved_ref, sums_ref, early_keep_ref, early_give_ref, *refs):
+            outs = 3 + (level > 1)
+            matrices = refs[:-outs]
+            keep_ref, give_ref, result_ref = refs[-outs:][:3]
             corrected = solved_ref[...] - jnp.sum(sums_ref[...], axis=0)
             result = solve_backward(level, live_ref, inverse_ref, corrected)
             result_ref[...] = result
             rounded = result.astype(bf16)
-            rounded_ref[...] = rounded
-            solved = {level: rounded}
-            for index in range(above):
-                solved[level + 1 + index] = rounded_above[index][...]
-            backward_partials(keep_ref, give_ref, solved, level - 1, matrices)
+            if level > 1:
+                refs[-1][...] = rounded
+            begun = early_keep_ref, early_give_ref
+            backward_partials(keep_ref, give_ref, {level: rounded}, level - 1, matrices, begun)
 
         return body
 
@@ -289,26 +299,35 @@
         gathered.append(blocks)
         if moved is not None:
             held.append(moved)
+    factors = flat(held)
     results, rounded = {}, {}
     level = levels - 1
     with jax.named_scope("top_level"):
         results[level], rounded[level], *halves = call(
-            top, (block_f32, block_bf16, twins_f32, twins_f32), live, right_sides, inverses, *gathered, *flat(held)
-        )
-    sums = scatter(*halves)
+            top, (block_f32, block_bf16, twins_f32, twins_f32), live, right_sides, inverses, *gathered, *factors
+        )
+
+    def begin(lower):
+        with jax.named_scope("backward_early"):
+            known = [rounded[level] for level in range(lower + 2, levels)]
+            return call(backward_early(lower), (twins_f32, twins_f32), *known, *factors)
+
     for level in range(levels - 2, 0, -1):
+        sums, begun = scatter(*halves, lambda: begin(level - 1))
         with jax.named_scope("backward_level"):
-            results[level], rounded[level], *halves = call(
+            keep, give, results[level], *rest = call(
                 down(level),
-                (block_f32, block_bf16, twins_f32, twins_f32),
+                (twins_f32, twins_f32, block_f32) + (block_bf16,) * (level > 1),
                 live,
                 inverses,
                 solved[level],
                 sums,
-                *[rounded[upper] for upper in range(level + 1, levels)],
-                *flat(held),
+                *begun,
+                *factors,
             )
-        sums = scatter(*halves)
+        halves = keep, give
+        rounded[level] = rest[0] if rest else None
+    sums, _ = scatter(*halves)
     with jax.named_scope("backward_last"):
         return call(
             last,

time: 77.3 us -> 76.9 us (level)
    pallas_call x11 -> x13, Pallas kernels: 8.31 us -> 8.35 us  [call(): pl.pallas_call(kernel, out_shape=outs, in_specs=[pl.BlockSpec(memory_spac...]
  transfers between devices with their start and end apart: 6 -> 6, of which waited for: 5 -> 5; matrix products, arithmetic and copies ran while one was open for 0% -> 0% of each run, Pallas kernels for 4% -> 5%
where the time goes in v6:
time: 76.9 us; the launch traced here: 76.5 us
  blocking collectives  56.8 us (74%)
  Pallas kernels  8.35 us (11%)
  starting transfers between devices  6.35 us (8%)
  waiting for transfers between devices  5 us (7%)
    all_to_all x3, blocking collectives, trade(): return lax.all_to_all(blocks, 'row', 0, 0, axis_index_groups=[row_order])  30.5 us
    all_to_all x3, blocking collectives, scatter(): lax.all_to_all(sums, 'row', 0, 0, axis_index_groups=one_of_each)  26.3 us
    pallas_call x13, Pallas kernels, call(): pl.pallas_call(kernel, out_shape=outs, in_specs=[pl.BlockSpec(memory_spac...  8.35 us
    ppermute x3, starting transfers between devices, exchange(): shifted.append(lax.ppermute(own, 'col', to_lower))  5.06 us
    ppermute x3, waiting for transfers between devices, scatter(): taken = lax.ppermute(give, 'row', [(k, k ^ 1) for k in range(row_parts)])  2.83 us
    ppermute x3, waiting for transfers between devices, exchange(): shifted.append(lax.ppermute(own, 'col', to_lower))  2.17 us
  transfers between devices with their start and end apart: 6, of which 5 were waited for; matrix products, arithmetic and copies ran while one was open for 0% of the time, Pallas kernels for 5%

profile of v6, /device:TPU:0, one launch (start us, length us, event | category | flops | bytes accessed | tf_op | source)
XLA Modules:
  0.0 76.5 jit_solution(17836618619068390628)
XLA Ops:
  0.0 1.3 %forward_first.2 = (bf16[2,128,1024]{2,1,0:T(8,128)(2,1)S(1)}, s32[6,1,8]{2,1,0:T(1,128)S(1)}) custom-call(bf16[6,128,1024]{2,1,0:T(8,128)(2,1)} %factor_hbm.3, s32[6,1,8]{2,1,0:T(1,128)} %pattern_hbm.1), custom_call_target="tpu_custom_call" | custom-call | tf_op jit(solution)/shard_map/forward_first/pallas_call | solution.py:22
  1.3 3.0 %collective-permute-start = (bf16[2,128,1024]{2,1,0:T(8,128)(2,1)S(1)}, bf16[2,128,1024]{2,1,0:T(8,128)(2,1)S(1)}, u32[]{:S(2)}, u32[]{:S(2)}) collective-permute-start(bf16[2,128,1024]{2,1,0:T(8,128)(2,1)S(1)} %get-tuple-element.55.refs_1_.refs_2_.refs_3_.refs_0_), channel_id=1, source_target_pairs={{1,0},{0,1},{3,2},{2,3},{5,4},{4,5},{7,6},{6,7},{9,8},{8,9},{11,10... | collective-permute-start | bytes 1572872 | tf_op jit(solution)/shard_map/ppermute | solution.py:250
  4.3 1.9 %forward_first.3 = (f32[32,128]{1,0:T(8,128)S(1)}, bf16[16,32,128]{2,1,0:T(8,128)(2,1)S(1)}, f32[4,32,128]{2,1,0:T(8,128)S(1)}, f32[4,1,128]{2,1,0:T(1,128)S(1)}...) custom-call(f32[4,32,128]{2,1,0:T(8,128)} %rhs_hbm.1, ...), custom_call_target="tpu_custom_call" | custom-call | tf_op jit(solution)/shard_map/forward_first/pallas_call | solution.py:22
  6.2 11.3 %all_to_all.30.refs_0_ = bf16[16,32,128]{2,1,0:T(8,128)(2,1)S(1)} all-to-all(bf16[16,32,128]{2,1,0:T(8,128)(2,1)S(1)} %get-tuple-element.52), channel_id=1, replica_groups={{18,0,4,8,12,16,20,24,28,2,6,10,14,22,26,30},{19,1,5,9,13,17,21,25,29,3..., dimensions={0} | all-to-all | bytes 262144 | tf_op jit(solution)/shard_map/all_to_all | solution.py:63
  17.5 0.5 collective-permute-start.1
  18.0 0.0 collective-permute-done.refs_2_.refs_3_.refs_4_.refs_1_
  18.0 0.7 forward_level.2
  18.7 9.7 %all_to_all.31.refs_1_ = bf16[16,32,128]{2,1,0:T(8,128)(2,1)S(1)} all-to-all(bf16[16,32,128]{2,1,0:T(8,128)(2,1)S(1)} %get-tuple-element.58), channel_id=1, replica_groups={{18,0,4,8,12,16,20,24,28,2,6,10,14,22,26,30},{19,1,5,9,13,17,21,25,29,3..., dimensions={0} | all-to-all | bytes 262144 | tf_op jit(solution)/shard_map/all_to_all | solution.py:63
  28.4 1.5 %collective-permute-start.2 = (bf16[2,128,1024]{2,1,0:T(8,128)(2,1)S(1)}, bf16[2,128,1024]{2,1,0:T(8,128)(2,1)S(1)}, u32[]{:S(2)}, u32[]{:S(2)}) collective-permute-start(bf16[2,128,1024]{2,1,0:T(8,128)(2,1)S(1)} %get-tuple-element.63.refs_7_.refs_5_.refs_4_.refs_6_), channel_id=1, source_target_pairs={{1,0},{0,1},{3,2},{2,3},{5,4},{4,5},{7,6},{6,7},{9,8},{8,9},{11,10... | collective-permute-start | bytes 1572872 | tf_op jit(solution)/shard_map/ppermute | solution.py:250
  30.0 1.4 %collective-permute-done.1.refs_5_.refs_6_.refs_4_.refs_3_ = bf16[2,128,1024]{2,1,0:T(8,128)(2,1)S(1)} collective-permute-done((bf16[2,128,1024]{2,1,0:T(8,128)(2,1)S(1)}, bf16[2,128,1024]{2,1,0:T(8,128)(2,1)S(1)}, u32[]{:S(2)}, u32[]{:S(2)}) %collective-permute-start.1) | collective-permute-done | bytes 524320 | tf_op jit(solution)/shard_map/ppermute | solution.py:250
  31.4 0.8 %forward_level.3 = (f32[32,128]{1,0:T(8,128)S(1)}, bf16[16,32,128]{2,1,0:T(8,128)(2,1)S(1)}) custom-call(f32[4,1,128]{2,1,0:T(1,128)S(1)} %get-tuple-element.46.live_ref, f32[4,32,128]{2,1,0:T(8,128)S(1)} %get-tuple-element.49.rhs_ref, f32[4,128,128]{2,1,0:T(8,128)S(1)} %get-tuple-element.47.inverse_ref, bf16[16,32,128]{2,1,0:T(8,128)(2,1)S(1)} %all_to_all.30.refs_0_, ...), custom_call_target="tpu_custom_call" | custom-call | tf_op jit(solution)/shard_map/forward_level/pallas_call | solution.py:22
  32.2 9.5 %all_to_all.32.refs_2_ = bf16[16,32,128]{2,1,0:T(8,128)(2,1)S(1)} all-to-all(bf16[16,32,128]{2,1,0:T(8,128)(2,1)S(1)} %get-tuple-element.62), channel_id=1, replica_groups={{18,0,4,8,12,16,20,24,28,2,6,10,14,22,26,30},{19,1,5,9,13,17,21,25,29,3..., dimensions={0} | all-to-all | bytes 262144 | tf_op jit(solution)/shard_map/all_to_all | solution.py:63
  41.6 0.7 collective-permute-done.2.refs_8_.refs_6_.refs_5_.refs_7_
  42.4 1.5 %top_level.1 = (f32[32,128]{1,0:T(8,128)S(1)}, bf16[32,128]{1,0:T(8,128)(2,1)S(1)}, f32[8,32,128]{2,1,0:T(8,128)S(1)}, f32[8,32,128]{2,1,0:T(8,128)S(1)}) custom-call(f32[4,1,128]{2,1,0:T(1,128)S(1)} %get-tuple-element.46.live_ref, f32[4,32,128]{2,1,0:T(8,128)S(1)} %get-tuple-element.49.rhs_ref, f32[4,128,128]{2,1,0:T(8,128)S(1)} %get-tuple-element.47.inverse_ref, ...), custom_call_target="tpu_custom_call" | custom-call | tf_op jit(solution)/shard_map/top_level/pallas_call | solution.py:22
  43.9 0.1 collective-permute-start.3
  44.0 0.2 backward_early.2
  44.2 1.1 %collective-permute-done.3.right_ref = f32[8,32,128]{2,1,0:T(8,128)S(1)} collective-permute-done((f32[8,32,128]{2,1,0:T(8,128)S(1)}, f32[8,32,128]{2,1,0:T(8,128)S(1)}, u32[]{:S(2)}, u32[]{:S(2)}) %collective-permute-start.3) | collective-permute-done | bytes 131104 | tf_op jit(solution)/shard_map/ppermute | solution.py:66
  45.3 8.6 %all_to_all.33.sums_ref = f32[8,32,128]{2,1,0:T(8,128)S(1)} all-to-all(f32[8,32,128]{2,1,0:T(8,128)S(1)} %sum_twins.3), channel_id=1, replica_groups={{18,4,26,12,2,20,10,28},{16,6,24,14,0,22,8,30},{19,5,27,13,3,21,11,29},..., dimensions={0} | all-to-all | bytes 262144 | tf_op jit(solution)/shard_map/all_to_all | solution.py:72
  53.9 0.4 backward_level.2
  54.3 0.7 collective-permute-start.4
  55.0 0.3 backward_early.3
  55.3 0.7 collective-permute-done.4.right_ref
  56.0 8.8 %all_to_all.34.sums_ref = f32[8,32,128]{2,1,0:T(8,128)S(1)} all-to-all(f32[8,32,128]{2,1,0:T(8,128)S(1)} %sum_twins.4), channel_id=1, replica_groups={{18,4,26,12,2,20,10,28},{16,6,24,14,0,22,8,30},{19,5,27,13,3,21,11,29},..., dimensions={0} | all-to-all | bytes 262144 | tf_op jit(solution)/shard_map/all_to_all | solution.py:72
  64.8 0.4 backward_level.3
  65.3 0.5 collective-permute-start.5
  65.8 1.0 %collective-permute-done.5.right_ref = f32[8,32,128]{2,1,0:T(8,128)S(1)} collective-permute-done((f32[8,32,128]{2,1,0:T(8,128)S(1)}, f32[8,32,128]{2,1,0:T(8,128)S(1)}, u32[]{:S(2)}, u32[]{:S(2)}) %collective-permute-start.5) | collective-permute-done | bytes 131104 | tf_op jit(solution)/shard_map/ppermute | solution.py:66
  66.8 8.9 %all_to_all.35.sums_ref = f32[8,32,128]{2,1,0:T(8,128)S(1)} all-to-all(f32[8,32,128]{2,1,0:T(8,128)S(1)} %sum_twins.5), channel_id=1, replica_groups={{18,4,26,12,2,20,10,28},{16,6,24,14,0,22,8,30},{19,5,27,13,3,21,11,29},..., dimensions={0} | all-to-all | bytes 262144 | tf_op jit(solution)/shard_map/all_to_all | solution.py:72
  75.7 0.8 %backward_last.1 = f32[4,32,128]{2,1,0:T(8,128)} custom-call(f32[4,1,128]{2,1,0:T(1,128)S(1)} %get-tuple-element.46.live_ref, f32[4,128,128]{2,1,0:T(8,128)S(1)} %get-tuple-element.47.inverse_ref, f32[32,128]{1,0:T(8,128)S(1)} %get-tuple-element.48.solved_ref, f32[8,32,128]{2,1,0:T(8,128)S(1)} %all_to_all.35.sums_ref, ...), custom_call_target="tpu_custom_call" | custom-call | tf_op jit(solution)/shard_map/backward_last/pallas_call | solution.py:22
  (3 shorter events, 0.1 us)
Async XLA Ops:
  1.3 16.7 %collective-permute-start = (bf16[2,128,1024]{2,1,0:T(8,128)(2,1)S(1)}, bf16[2,128,1024]{2,1,0:T(8,128)(2,1)S(1)}, u32[]{:S(2)}, u32[]{:S(2)}) collective-permute-start(bf16[2,128,1024]{2,1,0:T(8,128)(2,1)S(1)} %get-tuple-element.55.refs_1_.refs_2_.refs_3_.refs_0_), channel_id=1, source_target_pairs={{1,0},{0,1},{3,2},{2,3},{5,4},{4,5},{7,6},{6,7},{9,8},{8,9},{11,10... | collective-permute-start | bytes 1572872 | tf_op jit(solution)/shard_map/ppermute | solution.py:250
  17.5 13.9 %collective-permute-start.1 = (bf16[2,128,1024]{2,1,0:T(8,128)(2,1)S(1)}, bf16[2,128,1024]{2,1,0:T(8,128)(2,1)S(1)}, u32[]{:S(2)}, u32[]{:S(2)}) collective-permute-start(bf16[2,128,1024]{2,1,0:T(8,128)(2,1)S(1)} %get-tuple-element.60.refs_4_.refs_5_.refs_3_.refs_2_), channel_id=1, source_target_pairs={{1,0},{0,1},{3,2},{2,3},{5,4},{4,5},{7,6},{6,7},{9,8},{8,9},{11,10... | collective-permute-start | bytes 1572872 | tf_op jit(solution)/shard_map/ppermute | solution.py:250
  28.4 13.9 %collective-permute-start.2 = (bf16[2,128,1024]{2,1,0:T(8,128)(2,1)S(1)}, bf16[2,128,1024]{2,1,0:T(8,128)(2,1)S(1)}, u32[]{:S(2)}, u32[]{:S(2)}) collective-permute-start(bf16[2,128,1024]{2,1,0:T(8,128)(2,1)S(1)} %get-tuple-element.63.refs_7_.refs_5_.refs_4_.refs_6_), channel_id=1, source_target_pairs={{1,0},{0,1},{3,2},{2,3},{5,4},{4,5},{7,6},{6,7},{9,8},{8,9},{11,10... | collective-permute-start | bytes 1572872 | tf_op jit(solution)/shard_map/ppermute | solution.py:250
  43.9 1.4 %collective-permute-start.3 = (f32[8,32,128]{2,1,0:T(8,128)S(1)}, f32[8,32,128]{2,1,0:T(8,128)S(1)}, u32[]{:S(2)}, u32[]{:S(2)}) collective-permute-start(f32[8,32,128]{2,1,0:T(8,128)S(1)} %get-tuple-element.65), channel_id=1, source_target_pairs={{0,2},{2,0},{4,6},{6,4},{8,10},{10,8},{12,14},{14,12},{16,18},{18,... | collective-permute-start | bytes 393224 | tf_op jit(solution)/shard_map/ppermute | solution.py:66
  54.3 1.7 %collective-permute-start.4 = (f32[8,32,128]{2,1,0:T(8,128)S(1)}, f32[8,32,128]{2,1,0:T(8,128)S(1)}, u32[]{:S(2)}, u32[]{:S(2)}) collective-permute-start(f32[8,32,128]{2,1,0:T(8,128)S(1)} %get-tuple-element.73), channel_id=1, source_target_pairs={{0,2},{2,0},{4,6},{6,4},{8,10},{10,8},{12,14},{14,12},{16,18},{18,... | collective-permute-start | bytes 393224 | tf_op jit(solution)/shard_map/ppermute | solution.py:66
  65.3 1.5 %collective-permute-start.5 = (f32[8,32,128]{2,1,0:T(8,128)S(1)}, f32[8,32,128]{2,1,0:T(8,128)S(1)}, u32[]{:S(2)}, u32[]{:S(2)}) collective-permute-start(f32[8,32,128]{2,1,0:T(8,128)S(1)} %get-tuple-element.81), channel_id=1, source_target_pairs={{0,2},{2,0},{4,6},{6,4},{8,10},{10,8},{12,14},{14,12},{16,18},{18,... | collective-permute-start | bytes 393224 | tf_op jit(solution)/shard_map/ppermute | solution.py:66

commit v7 on v6

--- a/solution.py
+++ b/solution.py
@@ -43,16 +43,19 @@
     inverses = inverses.reshape(levels, width, width)
     f32, bf16 = jnp.float32, jnp.bfloat16
 
+    def shaped(*shape):
+        return jax.ShapeDtypeStruct(shape, f32)
+
     block_f32 = jax.ShapeDtypeStruct((rhs, width), f32)
     block_bf16 = jax.ShapeDtypeStruct((rhs, width), bf16)
     spread_bf16 = jax.ShapeDtypeStruct((total_blocks, rhs, width), bf16)
     twins = row_parts // 2
     twins_f32 = jax.ShapeDtypeStruct((twins, rhs, width), f32)
 
-    middle_row = row_parts // 2 + 1
+    middle_row = 2 * (twins // 2 + 1) + 1
     row_order = [middle_row] + [k for k in range(0, row_parts, 2)] + [k for k in range(1, row_parts, 2) if k != middle_row]
     step = next(s for s in range(5, 5 + twins) if math.gcd(s, twins) == 1)
-    twin_order = [(twins // 2 + step * k) % twins for k in range(twins)]
+    twin_orders = [[(root + step * k) % twins for k in range(twins)] for root in (twins // 2, twins // 2 + 1)]
 
     def row_place(index):
         odd_place = twins + index // 2 + jnp.where(index < middle_row, 1, 0)
@@ -68,23 +71,32 @@
         with jax.named_scope("sum_twins"):
             sums = call(add, twins_f32, keep, taken)
         sums, begun = lax.optimization_barrier((sums, begun))
-        one_of_each = [[2 * g + (g + side) % 2 for g in twin_order] for side in (1, 0)]
+        one_of_each = [[2 * g + (g + side) % 2 for g in order] for side, order in zip((1, 0), twin_orders)]
         return lax.all_to_all(sums, "row", 0, 0, axis_index_groups=one_of_each), begun
 
-    def solve_forward(level, live_ref, rhs_ref, inverse_ref, total):
-        live = live_ref[level]
-        vector = (rhs_ref[level] - total) * live
-        product = lax.dot_general(
-            vector, inverse_ref[level], (((1,), (1,)), ((), ())), precision=HIGHEST, preferred_element_type=f32
-        )
-        return product * live
-
-    def solve_backward(level, live_ref, inverse_ref, corrected):
-        live = live_ref[level]
-        product = lax.dot_general(
-            corrected * live, inverse_ref[level], (((1,), (0,)), ((), ())), precision=HIGHEST, preferred_element_type=f32
-        )
-        return product * live
+    left_parts, right_parts = (0, 0, 1, 0, 1, 2), (0, 1, 0, 2, 1, 0)
+    deep = len(left_parts) * width
+    forward_slot = {level: level - 1 for level in range(1, levels - 1)}
+    top_slot = levels - 2
+    backward_slot = {level: levels - 1 + level for level in range(levels - 1)}
+    slots = 2 * levels - 2
+
+    def split(value):
+        parts = []
+        for _ in range(3):
+            parts.append(value.astype(bf16))
+            value = value - parts[-1].astype(f32)
+        return parts
+
+    def store_solver(solver_ref, slot, matrix):
+        parts = split(matrix)
+        for k, part in enumerate(right_parts):
+            solver_ref[slot, k * width : (k + 1) * width, :] = parts[part]
+
+    def solve(solver_ref, slot, vector):
+        parts = split(vector)
+        left = jnp.concatenate([parts[part] for part in left_parts], axis=1)
+        return lax.dot_general(left, solver_ref[slot], (((1,), (0,)), ((), ())), preferred_element_type=f32)
 
     def forward_total(gathered, level, matrices):
         mine = lax.axis_index("col")
@@ -100,7 +112,10 @@
         return total
 
     def add(left_ref, right_ref, out_ref):
-        for place, g in enumerate(twin_order):
+        index = lax.axis_index("row")
+        second = lax.rem(index + index // 2, 2) == 0
+        for place in range(twins):
+            g = jnp.where(second, twin_orders[1][place], twin_orders[0][place])
             out_ref[place] = left_ref[g] + right_ref[g]
 
     def backward_partials(keep_ref, give_ref, solved, lower, matrices, begun=None):
@@ -151,31 +166,45 @@
 
     def first(
         rhs_hbm, factor_hbm, pattern_ref, widths_hbm, inverse_hbm,
-        solved_ref, out_ref, rhs_ref, live_ref, inverse_ref, *refs,
+        solved_ref, out_ref, rhs_ref, solver_ref, *refs,
     ):
         masked_refs = [None, *refs[: len(groups) - 1]]
-        factor_ref, widths_ref, sems = refs[len(groups) - 1 :]
-        order = needed[len(groups[0]) :]
+        factor_ref, inverse_ref, widths_ref, sems = refs[len(groups) - 1 :]
+        later = needed[len(groups[0]) :]
         small = [
-            pltpu.make_async_copy(widths_hbm, widths_ref, sems.at[1]),
-            pltpu.make_async_copy(rhs_hbm, rhs_ref, sems.at[2]),
-            pltpu.make_async_copy(inverse_hbm, inverse_ref, sems.at[3]),
+            pltpu.make_async_copy(widths_hbm, widths_ref, sems.at[0]),
+            pltpu.make_async_copy(rhs_hbm, rhs_ref, sems.at[1]),
+            pltpu.make_async_copy(inverse_hbm, inverse_ref, sems.at[2]),
         ]
         large = [
-            pltpu.make_async_copy(factor_hbm.at[pair], factor_ref.at[pair], sems.at[4 + k])
-            for k, pair in enumerate(order)
+            pltpu.make_async_copy(factor_hbm.at[pair], factor_ref.at[pair], sems.at[3 + k])
+            for k, pair in enumerate(later)
         ]
         for copy in small + large:
             copy.start()
         for copy in small:
             copy.wait()
-        column = lax.broadcasted_iota(jnp.int32, (1, width), 1)
+        row = lax.broadcasted_iota(jnp.int32, (width, width), 0)
+        column = lax.broadcasted_iota(jnp.int32, (width, width), 1)
         for level in range(levels):
-            live_ref[level] = (column < widths_ref[:, level : level + 1]).astype(f32)
-        value = solve_forward(0, live_ref, rhs_ref, inverse_ref, jnp.zeros((rhs, width), f32))
-        solved_ref[...] = value
-        spread(out_ref, value)
-        for copy, pair in zip(large, order):
+            live = jnp.broadcast_to(widths_ref[:, level : level + 1], (width, width))
+            inverse = jnp.where((row < live) & (column < live), inverse_ref[level], 0.0)
+            if level == 0:
+                value = lax.dot_general(
+                    rhs_ref[0], inverse, (((1,), (1,)), ((), ())), precision=HIGHEST, preferred_element_type=f32
+                )
+                solved_ref[...] = value
+                spread(out_ref, value)
+            if level in forward_slot:
+                store_solver(solver_ref, forward_slot[level], inverse.T)
+            if level in backward_slot:
+                store_solver(solver_ref, backward_slot[level], inverse)
+            if level == levels - 1:
+                both = lax.dot_general(
+                    inverse, inverse, (((0,), (0,)), ((), ())), precision=HIGHEST, preferred_element_type=f32
+                )
+                store_solver(solver_ref, top_slot, both)
+        for copy, pair in zip(large, later):
             copy.wait()
             group, place = place_of[pair]
             mask_pair(masked_refs[group], place, pattern_ref, factor_ref, pair)
@@ -188,23 +217,22 @@
         return refs[group * col_parts + shift][place]
 
     def middle(level):
-        def body(live_ref, rhs_ref, inverse_ref, *refs):
+        def body(rhs_ref, solver_ref, *refs):
             gathered, matrices = refs[:level], refs[level:-2]
             solved_ref, out_ref = refs[-2:]
             total = forward_total(gathered, level, matrices)
-            value = solve_forward(level, live_ref, rhs_ref, inverse_ref, total)
+            value = solve(solver_ref, forward_slot[level], rhs_ref[level] - total)
             solved_ref[...] = value
             spread(out_ref, value)
 
         return body
 
-    def top(live_ref, rhs_ref, inverse_ref, *refs):
+    def top(rhs_ref, solver_ref, *refs):
         level = levels - 1
         gathered, matrices = refs[:level], refs[level:-4]
         result_ref, rounded_ref, keep_ref, give_ref = refs[-4:]
         total = forward_total(gathered, level, matrices)
-        value = solve_forward(level, live_ref, rhs_ref, inverse_ref, total)
-        result = solve_backward(level, live_ref, inverse_ref, value)
+        result = solve(solver_ref, top_slot, rhs_ref[level] - total)
         result_ref[...] = result
         rounded = result.astype(bf16)
         rounded_ref[...] = rounded
@@ -221,12 +249,12 @@
         return body
 
     def down(level):
-        def body(live_ref, inverse_ref, solved_ref, sums_ref, early_keep_ref, early_give_ref, *refs):
+        def body(solver_ref, solved_ref, sums_ref, early_keep_ref, early_give_ref, *refs):
             outs = 3 + (level > 1)
             matrices = refs[:-outs]
             keep_ref, give_ref, result_ref = refs[-outs:][:3]
             corrected = solved_ref[...] - jnp.sum(sums_ref[...], axis=0)
-            result = solve_backward(level, live_ref, inverse_ref, corrected)
+            result = solve(solver_ref, backward_slot[level], corrected)
             result_ref[...] = result
             rounded = result.astype(bf16)
             if level > 1:
@@ -236,10 +264,10 @@
 
         return body
 
-    def last(live_ref, inverse_ref, solved_ref, sums_ref, *refs):
+    def last(solver_ref, solved_ref, sums_ref, *refs):
         out_ref = refs[-1]
         corrected = solved_ref[...] - jnp.sum(sums_ref[...], axis=0)
-        out_ref[0] = solve_backward(0, live_ref, inverse_ref, corrected)
+        out_ref[0] = solve(solver_ref, backward_slot[0], corrected)
         for level in range(1, levels):
             out_ref[level] = refs[level - 1][...]
 
@@ -258,7 +286,6 @@
         return blocks, moved
 
     solved, gathered, held = [], [], []
-    shaped = lambda *shape: jax.ShapeDtypeStruct(shape, f32)
     with jax.named_scope("forward_first"):
         operands = [
             pltpu.with_memory_space_constraint(x, pltpu.HBM)
@@ -274,16 +301,17 @@
             ],
         )
         operands[2] = pattern_vmem
-        value, out, right_sides, live, inverses, *masked = call(
+        value, out, right_sides, solver, *masked = call(
             first,
-            (block_f32, spread_bf16, shaped(levels, rhs, width), shaped(levels, 1, width), shaped(levels, width, width))
+            (block_f32, spread_bf16, shaped(levels, rhs, width), jax.ShapeDtypeStruct((slots, deep, width), bf16))
             + tuple(jax.ShapeDtypeStruct((len(group), width, local_cols), bf16) for group in groups[1:]),
             *operands,
             spaces=[pltpu.HBM, pltpu.HBM, pltpu.VMEM, pltpu.HBM, pltpu.HBM],
             scratch=[
                 pltpu.VMEM(factors.shape, bf16),
+                pltpu.VMEM(inverses.shape, f32),
                 pltpu.VMEM((1, levels), jnp.int32),
-                pltpu.SemaphoreType.DMA((4 + pairs,)),
+                pltpu.SemaphoreType.DMA((3 + pairs,)),
             ],
         )
         masked = [masked0, *masked]
@@ -293,7 +321,7 @@
     held.append(moved)
     for level in range(1, levels - 1):
         with jax.named_scope("forward_level"):
-            value, out = call(middle(level), (block_f32, spread_bf16), live, right_sides, inverses, *gathered, *flat(held))
+            value, out = call(middle(level), (block_f32, spread_bf16), right_sides, solver, *gathered, *flat(held))
         solved.append(value)
         blocks, moved = trade_beside(out, level)
         gathered.append(blocks)
@@ -304,7 +332,7 @@
     level = levels - 1
     with jax.named_scope("top_level"):
         results[level], rounded[level], *halves = call(
-            top, (block_f32, block_bf16, twins_f32, twins_f32), live, right_sides, inverses, *gathered, *factors
+            top, (block_f32, block_bf16, twins_f32, twins_f32), right_sides, solver, *gathered, *factors
         )
 
     def begin(lower):
@@ -318,8 +346,7 @@
             keep, give, results[level], *rest = call(
                 down(level),
                 (twins_f32, twins_f32, block_f32) + (block_bf16,) * (level > 1),
-                live,
-                inverses,
+                solver,
                 solved[level],
                 sums,
                 *begun,
@@ -332,8 +359,7 @@
         return call(
             last,
             jax.ShapeDtypeStruct((levels, rhs, width), f32),
-            live,
-            inverses,
+            solver,
             solved[0],
             sums,
             *[results[level] for level in range(1, levels)],

time: 76.9 us -> 75.3 us (0.979)
  blocking collectives: 56.8 us -> 55.4 us
  waiting for transfers between devices: 5 us -> 6.24 us
  Pallas kernels: 8.35 us -> 7.43 us
    all_to_all x3, blocking collectives: 30.5 us -> 29.2 us  [trade(): return lax.all_to_all(blocks, 'row', 0, 0, axis_index_groups=[row_order])]
    ppermute x3, waiting for transfers between devices: 2.17 us -> 3.29 us  [exchange(): shifted.append(lax.ppermute(own, 'col', to_lower))]
    pallas_call x13, Pallas kernels: 8.35 us -> 7.43 us  [call(): pl.pallas_call(kernel, out_shape=outs, in_specs=[pl.BlockSpec(memory_spac...]
where the time goes in v7:
time: 75.3 us; the launch traced here: 75 us
  blocking collectives  55.4 us (74%)
  Pallas kernels  7.43 us (10%)
  waiting for transfers between devices  6.24 us (8%)
  starting transfers between devices  5.86 us (8%)
    all_to_all x3, blocking collectives, trade(): return lax.all_to_all(blocks, 'row', 0, 0, axis_index_groups=[row_order])  29.2 us
    all_to_all x3, blocking collectives, scatter(): lax.all_to_all(sums, 'row', 0, 0, axis_index_groups=one_of_each)  26.2 us
    pallas_call x13, Pallas kernels, call(): pl.pallas_call(kernel, out_shape=outs, in_specs=[pl.BlockSpec(memory_spac...  7.43 us
    ppermute x3, starting transfers between devices, exchange(): shifted.append(lax.ppermute(own, 'col', to_lower))  5.06 us
    ppermute x3, waiting for transfers between devices, exchange(): shifted.append(lax.ppermute(own, 'col', to_lower))  3.29 us
    ppermute x3, waiting for transfers between devices, scatter(): taken = lax.ppermute(give, 'row', [(k, k ^ 1) for k in range(row_parts)])  2.95 us
  transfers between devices with their start and end apart: 6, of which 5 were waited for; matrix products, arithmetic and copies ran while one was open for 0% of the time, Pallas kernels for 5%

profile of v7, /device:TPU:0, one launch (start us, length us, event | category | flops | bytes accessed | tf_op | source)
XLA Modules:
  0.0 75.0 jit_solution(3553683996568901441)
XLA Ops:
  0.0 1.3 %forward_first.2 = (bf16[2,128,1024]{2,1,0:T(8,128)(2,1)S(1)}, s32[6,1,8]{2,1,0:T(1,128)S(1)}) custom-call(bf16[6,128,1024]{2,1,0:T(8,128)(2,1)} %factor_hbm.3, s32[6,1,8]{2,1,0:T(1,128)} %pattern_hbm.1), custom_call_target="tpu_custom_call" | custom-call | tf_op jit(solution)/shard_map/forward_first/pallas_call | solution.py:22
  1.3 3.0 %collective-permute-start = (bf16[2,128,1024]{2,1,0:T(8,128)(2,1)S(1)}, bf16[2,128,1024]{2,1,0:T(8,128)(2,1)S(1)}, u32[]{:S(2)}, u32[]{:S(2)}) collective-permute-start(bf16[2,128,1024]{2,1,0:T(8,128)(2,1)S(1)} %get-tuple-element.53.refs_1_.refs_2_.refs_3_.refs_0_), channel_id=1, source_target_pairs={{1,0},{0,1},{3,2},{2,3},{5,4},{4,5},{7,6},{6,7},{9,8},{8,9},{11,10... | collective-permute-start | bytes 1572872 | tf_op jit(solution)/shard_map/ppermute | solution.py:278
  4.3 2.0 %forward_first.3 = (f32[32,128]{1,0:T(8,128)S(1)}, bf16[16,32,128]{2,1,0:T(8,128)(2,1)S(1)}, f32[4,32,128]{2,1,0:T(8,128)S(1)}, bf16[6,768,128]{2,1,0:T(8,128)(2...) custom-call(f32[4,32,128]{2,1,0:T(8,128)} %rhs_hbm.1, bf16[6,128,1024]{2,1,0:T(8,128)(2,1)} %factor_hbm.3, ...), custom_call_target="tpu_custom_call" | custom-call | tf_op jit(solution)/shard_map/forward_first/pallas_call | solution.py:22
  6.3 10.4 %all_to_all.30.refs_0_ = bf16[16,32,128]{2,1,0:T(8,128)(2,1)S(1)} all-to-all(bf16[16,32,128]{2,1,0:T(8,128)(2,1)S(1)} %get-tuple-element.50), channel_id=1, replica_groups={{22,0,4,8,12,16,20,24,28,2,6,10,14,18,26,30},{23,1,5,9,13,17,21,25,29,3..., dimensions={0} | all-to-all | bytes 262144 | tf_op jit(solution)/shard_map/all_to_all | solution.py:66
  16.7 0.5 collective-permute-start.1
  17.2 0.0 collective-permute-done.refs_2_.refs_3_.refs_4_.refs_1_
  17.2 0.5 forward_level.2
  17.7 9.6 %all_to_all.31.refs_1_ = bf16[16,32,128]{2,1,0:T(8,128)(2,1)S(1)} all-to-all(bf16[16,32,128]{2,1,0:T(8,128)(2,1)S(1)} %get-tuple-element.56), channel_id=1, replica_groups={{22,0,4,8,12,16,20,24,28,2,6,10,14,18,26,30},{23,1,5,9,13,17,21,25,29,3..., dimensions={0} | all-to-all | bytes 262144 | tf_op jit(solution)/shard_map/all_to_all | solution.py:66
  27.3 1.5 %collective-permute-start.2 = (bf16[2,128,1024]{2,1,0:T(8,128)(2,1)S(1)}, bf16[2,128,1024]{2,1,0:T(8,128)(2,1)S(1)}, u32[]{:S(2)}, u32[]{:S(2)}) collective-permute-start(bf16[2,128,1024]{2,1,0:T(8,128)(2,1)S(1)} %get-tuple-element.61.refs_7_.refs_5_.refs_4_.refs_6_), channel_id=1, source_target_pairs={{1,0},{0,1},{3,2},{2,3},{5,4},{4,5},{7,6},{6,7},{9,8},{8,9},{11,10... | collective-permute-start | bytes 1572872 | tf_op jit(solution)/shard_map/ppermute | solution.py:278
  28.9 2.4 %collective-permute-done.1.refs_5_.refs_6_.refs_4_.refs_3_ = bf16[2,128,1024]{2,1,0:T(8,128)(2,1)S(1)} collective-permute-done((bf16[2,128,1024]{2,1,0:T(8,128)(2,1)S(1)}, bf16[2,128,1024]{2,1,0:T(8,128)(2,1)S(1)}, u32[]{:S(2)}, u32[]{:S(2)}) %collective-permute-start.1) | collective-permute-done | bytes 524320 | tf_op jit(solution)/shard_map/ppermute | solution.py:278
  31.2 0.6 forward_level.3
  31.8 9.1 %all_to_all.32.refs_2_ = bf16[16,32,128]{2,1,0:T(8,128)(2,1)S(1)} all-to-all(bf16[16,32,128]{2,1,0:T(8,128)(2,1)S(1)} %get-tuple-element.60), channel_id=1, replica_groups={{22,0,4,8,12,16,20,24,28,2,6,10,14,18,26,30},{23,1,5,9,13,17,21,25,29,3..., dimensions={0} | all-to-all | bytes 262144 | tf_op jit(solution)/shard_map/all_to_all | solution.py:66
  41.0 0.9 %collective-permute-done.2.refs_8_.refs_6_.refs_5_.refs_7_ = bf16[2,128,1024]{2,1,0:T(8,128)(2,1)S(1)} collective-permute-done((bf16[2,128,1024]{2,1,0:T(8,128)(2,1)S(1)}, bf16[2,128,1024]{2,1,0:T(8,128)(2,1)S(1)}, u32[]{:S(2)}, u32[]{:S(2)}) %collective-permute-start.2) | collective-permute-done | bytes 524320 | tf_op jit(solution)/shard_map/ppermute | solution.py:278
  41.9 1.0 %top_level.1 = (f32[32,128]{1,0:T(8,128)S(1)}, bf16[32,128]{1,0:T(8,128)(2,1)S(1)}, f32[8,32,128]{2,1,0:T(8,128)S(1)}, f32[8,32,128]{2,1,0:T(8,128)S(1)}) custom-call(f32[4,32,128]{2,1,0:T(8,128)S(1)} %get-tuple-element.47.rhs_ref, bf16[6,768,128]{2,1,0:T(8,128)(2,1)S(1)} %get-tuple-element.45.solver_ref, bf16[16,32,128]{2,1,0:T(8,128)(2,1)S(1)} %all_to_all.30.refs_0_, ...), custom_call_target="tpu_custom_call" | custom-call | tf_op jit(solution)/shard_map/top_level/pallas_call | solution.py:22
  42.9 0.1 collective-permute-start.3
  43.0 0.2 backward_early.2
  43.2 1.1 %collective-permute-done.3.right_ref = f32[8,32,128]{2,1,0:T(8,128)S(1)} collective-permute-done((f32[8,32,128]{2,1,0:T(8,128)S(1)}, f32[8,32,128]{2,1,0:T(8,128)S(1)}, u32[]{:S(2)}, u32[]{:S(2)}) %collective-permute-start.3) | collective-permute-done | bytes 131104 | tf_op jit(solution)/shard_map/ppermute | solution.py:69
  44.4 8.5 %all_to_all.33.sums_ref = f32[8,32,128]{2,1,0:T(8,128)S(1)} all-to-all(f32[8,32,128]{2,1,0:T(8,128)S(1)} %sum_twins.3), channel_id=1, replica_groups={{18,4,26,12,2,20,10,28},{22,8,30,16,6,24,14,0},{19,5,27,13,3,21,11,29},..., dimensions={0} | all-to-all | bytes 262144 | tf_op jit(solution)/shard_map/all_to_all | solution.py:75
  52.9 0.4 backward_level.2
  53.3 0.4 collective-permute-start.4
  53.6 0.3 backward_early.3
  53.9 0.8 %collective-permute-done.4.right_ref = f32[8,32,128]{2,1,0:T(8,128)S(1)} collective-permute-done((f32[8,32,128]{2,1,0:T(8,128)S(1)}, f32[8,32,128]{2,1,0:T(8,128)S(1)}, u32[]{:S(2)}, u32[]{:S(2)}) %collective-permute-start.4) | collective-permute-done | bytes 131104 | tf_op jit(solution)/shard_map/ppermute | solution.py:69
  54.7 9.0 %all_to_all.34.sums_ref = f32[8,32,128]{2,1,0:T(8,128)S(1)} all-to-all(f32[8,32,128]{2,1,0:T(8,128)S(1)} %sum_twins.4), channel_id=1, replica_groups={{18,4,26,12,2,20,10,28},{22,8,30,16,6,24,14,0},{19,5,27,13,3,21,11,29},..., dimensions={0} | all-to-all | bytes 262144 | tf_op jit(solution)/shard_map/all_to_all | solution.py:75
  63.7 0.4 backward_level.3
  64.1 0.4 collective-permute-start.5
  64.5 1.0 %collective-permute-done.5.right_ref = f32[8,32,128]{2,1,0:T(8,128)S(1)} collective-permute-done((f32[8,32,128]{2,1,0:T(8,128)S(1)}, f32[8,32,128]{2,1,0:T(8,128)S(1)}, u32[]{:S(2)}, u32[]{:S(2)}) %collective-permute-start.5) | collective-permute-done | bytes 131104 | tf_op jit(solution)/shard_map/ppermute | solution.py:69
  65.5 8.6 %all_to_all.35.sums_ref = f32[8,32,128]{2,1,0:T(8,128)S(1)} all-to-all(f32[8,32,128]{2,1,0:T(8,128)S(1)} %sum_twins.5), channel_id=1, replica_groups={{18,4,26,12,2,20,10,28},{22,8,30,16,6,24,14,0},{19,5,27,13,3,21,11,29},..., dimensions={0} | all-to-all | bytes 262144 | tf_op jit(solution)/shard_map/all_to_all | solution.py:75
  74.2 0.8 %backward_last.1 = f32[4,32,128]{2,1,0:T(8,128)} custom-call(bf16[6,768,128]{2,1,0:T(8,128)(2,1)S(1)} %get-tuple-element.45.solver_ref, f32[32,128]{1,0:T(8,128)S(1)} %get-tuple-element.46.solved_ref, f32[8,32,128]{2,1,0:T(8,128)S(1)} %all_to_all.35.sums_ref, f32[32,128]{1,0:T(8,128)S(1)} %get-tuple-element.80.refs_0_, ...), custom_call_target="tpu_custom_call" | custom-call | tf_op jit(solution)/shard_map/backward_last/pallas_call | solution.py:22
  (3 shorter events, 0.1 us)
Async XLA Ops:
  1.3 15.9 %collective-permute-start = (bf16[2,128,1024]{2,1,0:T(8,128)(2,1)S(1)}, bf16[2,128,1024]{2,1,0:T(8,128)(2,1)S(1)}, u32[]{:S(2)}, u32[]{:S(2)}) collective-permute-start(bf16[2,128,1024]{2,1,0:T(8,128)(2,1)S(1)} %get-tuple-element.53.refs_1_.refs_2_.refs_3_.refs_0_), channel_id=1, source_target_pairs={{1,0},{0,1},{3,2},{2,3},{5,4},{4,5},{7,6},{6,7},{9,8},{8,9},{11,10... | collective-permute-start | bytes 1572872 | tf_op jit(solution)/shard_map/ppermute | solution.py:278
  16.7 14.5 %collective-permute-start.1 = (bf16[2,128,1024]{2,1,0:T(8,128)(2,1)S(1)}, bf16[2,128,1024]{2,1,0:T(8,128)(2,1)S(1)}, u32[]{:S(2)}, u32[]{:S(2)}) collective-permute-start(bf16[2,128,1024]{2,1,0:T(8,128)(2,1)S(1)} %get-tuple-element.58.refs_4_.refs_5_.refs_3_.refs_2_), channel_id=1, source_target_pairs={{1,0},{0,1},{3,2},{2,3},{5,4},{4,5},{7,6},{6,7},{9,8},{8,9},{11,10... | collective-permute-start | bytes 1572872 | tf_op jit(solution)/shard_map/ppermute | solution.py:278
  27.3 14.6 %collective-permute-start.2 = (bf16[2,128,1024]{2,1,0:T(8,128)(2,1)S(1)}, bf16[2,128,1024]{2,1,0:T(8,128)(2,1)S(1)}, u32[]{:S(2)}, u32[]{:S(2)}) collective-permute-start(bf16[2,128,1024]{2,1,0:T(8,128)(2,1)S(1)} %get-tuple-element.61.refs_7_.refs_5_.refs_4_.refs_6_), channel_id=1, source_target_pairs={{1,0},{0,1},{3,2},{2,3},{5,4},{4,5},{7,6},{6,7},{9,8},{8,9},{11,10... | collective-permute-start | bytes 1572872 | tf_op jit(solution)/shard_map/ppermute | solution.py:278
  42.9 1.4 %collective-permute-start.3 = (f32[8,32,128]{2,1,0:T(8,128)S(1)}, f32[8,32,128]{2,1,0:T(8,128)S(1)}, u32[]{:S(2)}, u32[]{:S(2)}) collective-permute-start(f32[8,32,128]{2,1,0:T(8,128)S(1)} %get-tuple-element.63), channel_id=1, source_target_pairs={{0,2},{2,0},{4,6},{6,4},{8,10},{10,8},{12,14},{14,12},{16,18},{18,... | collective-permute-start | bytes 393224 | tf_op jit(solution)/shard_map/ppermute | solution.py:69
  53.3 1.4 %collective-permute-start.4 = (f32[8,32,128]{2,1,0:T(8,128)S(1)}, f32[8,32,128]{2,1,0:T(8,128)S(1)}, u32[]{:S(2)}, u32[]{:S(2)}) collective-permute-start(f32[8,32,128]{2,1,0:T(8,128)S(1)} %get-tuple-element.71), channel_id=1, source_target_pairs={{0,2},{2,0},{4,6},{6,4},{8,10},{10,8},{12,14},{14,12},{16,18},{18,... | collective-permute-start | bytes 393224 | tf_op jit(solution)/shard_map/ppermute | solution.py:69
  64.1 1.4 %collective-permute-start.5 = (f32[8,32,128]{2,1,0:T(8,128)S(1)}, f32[8,32,128]{2,1,0:T(8,128)S(1)}, u32[]{:S(2)}, u32[]{:S(2)}) collective-permute-start(f32[8,32,128]{2,1,0:T(8,128)S(1)} %get-tuple-element.79), channel_id=1, source_target_pairs={{0,2},{2,0},{4,6},{6,4},{8,10},{10,8},{12,14},{14,12},{16,18},{18,... | collective-permute-start | bytes 393224 | tf_op jit(solution)/shard_map/ppermute | solution.py:69

commit v8 on v7

--- a/solution.py
+++ b/solution.py
@@ -98,12 +98,14 @@
         left = jnp.concatenate([parts[part] for part in left_parts], axis=1)
         return lax.dot_general(left, solver_ref[slot], (((1,), (0,)), ((), ())), preferred_element_type=f32)
 
-    def forward_total(gathered, level, matrices):
+    def forward_total(gathered, level, matrices, late=None, total=None):
         mine = lax.axis_index("col")
-        total = None
         for shift in range(col_parts):
             start = lax.rem(mine + shift, col_parts) * half
             for lower in range(level):
+                is_late = shift > 0 and place_of[lookup[level, lower]][0] == len(groups) - 1
+                if late is not None and is_late != late:
+                    continue
                 left = jnp.concatenate([gathered[lower][row_place(start + k)] for k in range(half)], axis=1)
                 term = lax.dot_general(
                     left, matrix(matrices, level, lower, shift), (((1,), (1,)), ((), ())), preferred_element_type=f32
@@ -227,11 +229,15 @@
 
         return body
 
-    def top(rhs_ref, solver_ref, *refs):
+    def top_early(*refs):
+        level = levels - 1
+        refs[-1][...] = forward_total(refs[:level], level, refs[level:-1], False)
+
+    def top(rhs_ref, solver_ref, early_ref, *refs):
         level = levels - 1
         gathered, matrices = refs[:level], refs[level:-4]
         result_ref, rounded_ref, keep_ref, give_ref = refs[-4:]
-        total = forward_total(gathered, level, matrices)
+        total = forward_total(gathered, level, matrices, True, early_ref[...])
         result = solve(solver_ref, top_slot, rhs_ref[level] - total)
         result_ref[...] = result
         rounded = result.astype(bf16)
@@ -291,7 +297,8 @@
             pltpu.with_memory_space_constraint(x, pltpu.HBM)
             for x in (right_sides, factors, pattern, live_widths.reshape(1, levels), inverses)
         ]
-        masked0, pattern_vmem = call(first_mask,
+        masked0, pattern_vmem = call(
+            first_mask,
             (jax.ShapeDtypeStruct((len(groups[0]), width, local_cols), bf16), jax.ShapeDtypeStruct(pattern.shape, jnp.int32)),
             operands[1], operands[2], space=pltpu.HBM,
             scratch=[
@@ -330,9 +337,12 @@
     factors = flat(held)
     results, rounded = {}, {}
     level = levels - 1
+    with jax.named_scope("top_early"):
+        arrived = factors[: len(factors) - (col_parts - 1)]
+        early = call(top_early, block_f32, *gathered, *arrived)
     with jax.named_scope("top_level"):
         results[level], rounded[level], *halves = call(
-            top, (block_f32, block_bf16, twins_f32, twins_f32), right_sides, solver, *gathered, *factors
+            top, (block_f32, block_bf16, twins_f32, twins_f32), right_sides, solver, early, *gathered, *factors
         )
 
     def begin(lower):

time: 75.3 us -> 75 us (level)
    pallas_call x13 -> x14, Pallas kernels: 7.43 us -> 7.57 us  [call(): pl.pallas_call(kernel, out_shape=outs, in_specs=[pl.BlockSpec(memory_spac...]
where the time goes in v8:
time: 75 us; the launch traced here: 74.7 us
  blocking collectives  55.4 us (74%)
  Pallas kernels  7.57 us (10%)
  starting transfers between devices  5.85 us (8%)
  waiting for transfers between devices  5.82 us (8%)
    all_to_all x3, blocking collectives, trade(): return lax.all_to_all(blocks, 'row', 0, 0, axis_index_groups=[row_order])  29.2 us
    all_to_all x3, blocking collectives, scatter(): lax.all_to_all(sums, 'row', 0, 0, axis_index_groups=one_of_each)  26.2 us
    pallas_call x14, Pallas kernels, call(): pl.pallas_call(kernel, out_shape=outs, in_specs=[pl.BlockSpec(memory_spac...  7.57 us
    ppermute x3, starting transfers between devices, exchange(): shifted.append(lax.ppermute(own, 'col', to_lower))  5.06 us
    ppermute x3, waiting for transfers between devices, scatter(): taken = lax.ppermute(give, 'row', [(k, k ^ 1) for k in range(row_parts)])  2.96 us
    ppermute x3, waiting for transfers between devices, exchange(): shifted.append(lax.ppermute(own, 'col', to_lower))  2.86 us
  transfers between devices with their start and end apart: 6, of which 5 were waited for; matrix products, arithmetic and copies ran while one was open for 0% of the time, Pallas kernels for 5%

profile of v8, /device:TPU:0, one launch (start us, length us, event | category | flops | bytes accessed | tf_op | source)
XLA Modules:
  0.0 74.7 jit_solution(14140023480927240780)
XLA Ops:
  0.0 1.3 %forward_first.2 = (bf16[2,128,1024]{2,1,0:T(8,128)(2,1)S(1)}, s32[6,1,8]{2,1,0:T(1,128)S(1)}) custom-call(bf16[6,128,1024]{2,1,0:T(8,128)(2,1)} %factor_hbm.3, s32[6,1,8]{2,1,0:T(1,128)} %pattern_hbm.1), custom_call_target="tpu_custom_call" | custom-call | tf_op jit(solution)/shard_map/forward_first/pallas_call | solution.py:22
  1.3 3.0 %collective-permute-start = (bf16[2,128,1024]{2,1,0:T(8,128)(2,1)S(1)}, bf16[2,128,1024]{2,1,0:T(8,128)(2,1)S(1)}, u32[]{:S(2)}, u32[]{:S(2)}) collective-permute-start(bf16[2,128,1024]{2,1,0:T(8,128)(2,1)S(1)} %get-tuple-element.53.refs_1_.refs_2_.refs_3_.refs_0_), channel_id=1, source_target_pairs={{1,0},{0,1},{3,2},{2,3},{5,4},{4,5},{7,6},{6,7},{9,8},{8,9},{11,10... | collective-permute-start | bytes 1572872 | tf_op jit(solution)/shard_map/ppermute | solution.py:284
  4.3 2.0 %forward_first.3 = (f32[32,128]{1,0:T(8,128)S(1)}, bf16[16,32,128]{2,1,0:T(8,128)(2,1)S(1)}, f32[4,32,128]{2,1,0:T(8,128)S(1)}, bf16[6,768,128]{2,1,0:T(8,128)(2...) custom-call(f32[4,32,128]{2,1,0:T(8,128)} %rhs_hbm.1, bf16[6,128,1024]{2,1,0:T(8,128)(2,1)} %factor_hbm.3, ...), custom_call_target="tpu_custom_call" | custom-call | tf_op jit(solution)/shard_map/forward_first/pallas_call | solution.py:22
  6.3 10.4 %all_to_all.30.refs_0_ = bf16[16,32,128]{2,1,0:T(8,128)(2,1)S(1)} all-to-all(bf16[16,32,128]{2,1,0:T(8,128)(2,1)S(1)} %get-tuple-element.50), channel_id=1, replica_groups={{22,0,4,8,12,16,20,24,28,2,6,10,14,18,26,30},{23,1,5,9,13,17,21,25,29,3..., dimensions={0} | all-to-all | bytes 262144 | tf_op jit(solution)/shard_map/all_to_all | solution.py:66
  16.7 0.5 collective-permute-start.1
  17.2 0.0 collective-permute-done.refs_2_.refs_3_.refs_4_.refs_1_
  17.2 0.5 forward_level.2
  17.7 9.6 %all_to_all.31.refs_1_ = bf16[16,32,128]{2,1,0:T(8,128)(2,1)S(1)} all-to-all(bf16[16,32,128]{2,1,0:T(8,128)(2,1)S(1)} %get-tuple-element.56), channel_id=1, replica_groups={{22,0,4,8,12,16,20,24,28,2,6,10,14,18,26,30},{23,1,5,9,13,17,21,25,29,3..., dimensions={0} | all-to-all | bytes 262144 | tf_op jit(solution)/shard_map/all_to_all | solution.py:66
  27.3 1.5 %collective-permute-start.2 = (bf16[2,128,1024]{2,1,0:T(8,128)(2,1)S(1)}, bf16[2,128,1024]{2,1,0:T(8,128)(2,1)S(1)}, u32[]{:S(2)}, u32[]{:S(2)}) collective-permute-start(bf16[2,128,1024]{2,1,0:T(8,128)(2,1)S(1)} %get-tuple-element.61.refs_7_.refs_5_.refs_4_.refs_6_), channel_id=1, source_target_pairs={{1,0},{0,1},{3,2},{2,3},{5,4},{4,5},{7,6},{6,7},{9,8},{8,9},{11,10... | collective-permute-start | bytes 1572872 | tf_op jit(solution)/shard_map/ppermute | solution.py:284
  28.9 2.4 %collective-permute-done.1.refs_5_.refs_6_.refs_4_.refs_3_ = bf16[2,128,1024]{2,1,0:T(8,128)(2,1)S(1)} collective-permute-done((bf16[2,128,1024]{2,1,0:T(8,128)(2,1)S(1)}, bf16[2,128,1024]{2,1,0:T(8,128)(2,1)S(1)}, u32[]{:S(2)}, u32[]{:S(2)}) %collective-permute-start.1) | collective-permute-done | bytes 524320 | tf_op jit(solution)/shard_map/ppermute | solution.py:284
  31.2 0.6 forward_level.3
  31.8 9.1 %all_to_all.32.refs_2_ = bf16[16,32,128]{2,1,0:T(8,128)(2,1)S(1)} all-to-all(bf16[16,32,128]{2,1,0:T(8,128)(2,1)S(1)} %get-tuple-element.60), channel_id=1, replica_groups={{22,0,4,8,12,16,20,24,28,2,6,10,14,18,26,30},{23,1,5,9,13,17,21,25,29,3..., dimensions={0} | all-to-all | bytes 262144 | tf_op jit(solution)/shard_map/all_to_all | solution.py:66
  41.0 0.4 top_early.1.early_ref
  41.4 0.5 collective-permute-done.2.refs_8_.refs_6_.refs_5_.refs_7_
  41.9 0.7 top_level.1
  42.7 0.1 collective-permute-start.3
  42.7 0.2 backward_early.2
  42.9 1.1 %collective-permute-done.3.right_ref = f32[8,32,128]{2,1,0:T(8,128)S(1)} collective-permute-done((f32[8,32,128]{2,1,0:T(8,128)S(1)}, f32[8,32,128]{2,1,0:T(8,128)S(1)}, u32[]{:S(2)}, u32[]{:S(2)}) %collective-permute-start.3) | collective-permute-done | bytes 131104 | tf_op jit(solution)/shard_map/ppermute | solution.py:69
  44.1 8.5 %all_to_all.33.sums_ref = f32[8,32,128]{2,1,0:T(8,128)S(1)} all-to-all(f32[8,32,128]{2,1,0:T(8,128)S(1)} %sum_twins.3), channel_id=1, replica_groups={{18,4,26,12,2,20,10,28},{22,8,30,16,6,24,14,0},{19,5,27,13,3,21,11,29},..., dimensions={0} | all-to-all | bytes 262144 | tf_op jit(solution)/shard_map/all_to_all | solution.py:75
  52.6 0.4 backward_level.2
  53.0 0.4 collective-permute-start.4
  53.3 0.3 backward_early.3
  53.6 0.8 %collective-permute-done.4.right_ref = f32[8,32,128]{2,1,0:T(8,128)S(1)} collective-permute-done((f32[8,32,128]{2,1,0:T(8,128)S(1)}, f32[8,32,128]{2,1,0:T(8,128)S(1)}, u32[]{:S(2)}, u32[]{:S(2)}) %collective-permute-start.4) | collective-permute-done | bytes 131104 | tf_op jit(solution)/shard_map/ppermute | solution.py:69
  54.4 9.0 %all_to_all.34.sums_ref = f32[8,32,128]{2,1,0:T(8,128)S(1)} all-to-all(f32[8,32,128]{2,1,0:T(8,128)S(1)} %sum_twins.4), channel_id=1, replica_groups={{18,4,26,12,2,20,10,28},{22,8,30,16,6,24,14,0},{19,5,27,13,3,21,11,29},..., dimensions={0} | all-to-all | bytes 262144 | tf_op jit(solution)/shard_map/all_to_all | solution.py:75
  63.4 0.4 backward_level.3
  63.8 0.4 collective-permute-start.5
  64.2 1.0 %collective-permute-done.5.right_ref = f32[8,32,128]{2,1,0:T(8,128)S(1)} collective-permute-done((f32[8,32,128]{2,1,0:T(8,128)S(1)}, f32[8,32,128]{2,1,0:T(8,128)S(1)}, u32[]{:S(2)}, u32[]{:S(2)}) %collective-permute-start.5) | collective-permute-done | bytes 131104 | tf_op jit(solution)/shard_map/ppermute | solution.py:69
  65.2 8.6 %all_to_all.35.sums_ref = f32[8,32,128]{2,1,0:T(8,128)S(1)} all-to-all(f32[8,32,128]{2,1,0:T(8,128)S(1)} %sum_twins.5), channel_id=1, replica_groups={{18,4,26,12,2,20,10,28},{22,8,30,16,6,24,14,0},{19,5,27,13,3,21,11,29},..., dimensions={0} | all-to-all | bytes 262144 | tf_op jit(solution)/shard_map/all_to_all | solution.py:75
  73.9 0.8 %backward_last.1 = f32[4,32,128]{2,1,0:T(8,128)} custom-call(bf16[6,768,128]{2,1,0:T(8,128)(2,1)S(1)} %get-tuple-element.45.solver_ref, f32[32,128]{1,0:T(8,128)S(1)} %get-tuple-element.46.solved_ref, f32[8,32,128]{2,1,0:T(8,128)S(1)} %all_to_all.35.sums_ref, f32[32,128]{1,0:T(8,128)S(1)} %get-tuple-element.80.refs_0_, ...), custom_call_target="tpu_custom_call" | custom-call | tf_op jit(solution)/shard_map/backward_last/pallas_call | solution.py:22
  (3 shorter events, 0.0 us)
Async XLA Ops:
  1.3 15.9 %collective-permute-start = (bf16[2,128,1024]{2,1,0:T(8,128)(2,1)S(1)}, bf16[2,128,1024]{2,1,0:T(8,128)(2,1)S(1)}, u32[]{:S(2)}, u32[]{:S(2)}) collective-permute-start(bf16[2,128,1024]{2,1,0:T(8,128)(2,1)S(1)} %get-tuple-element.53.refs_1_.refs_2_.refs_3_.refs_0_), channel_id=1, source_target_pairs={{1,0},{0,1},{3,2},{2,3},{5,4},{4,5},{7,6},{6,7},{9,8},{8,9},{11,10... | collective-permute-start | bytes 1572872 | tf_op jit(solution)/shard_map/ppermute | solution.py:284
  16.7 14.5 %collective-permute-start.1 = (bf16[2,128,1024]{2,1,0:T(8,128)(2,1)S(1)}, bf16[2,128,1024]{2,1,0:T(8,128)(2,1)S(1)}, u32[]{:S(2)}, u32[]{:S(2)}) collective-permute-start(bf16[2,128,1024]{2,1,0:T(8,128)(2,1)S(1)} %get-tuple-element.58.refs_4_.refs_5_.refs_3_.refs_2_), channel_id=1, source_target_pairs={{1,0},{0,1},{3,2},{2,3},{5,4},{4,5},{7,6},{6,7},{9,8},{8,9},{11,10... | collective-permute-start | bytes 1572872 | tf_op jit(solution)/shard_map/ppermute | solution.py:284
  27.3 14.6 %collective-permute-start.2 = (bf16[2,128,1024]{2,1,0:T(8,128)(2,1)S(1)}, bf16[2,128,1024]{2,1,0:T(8,128)(2,1)S(1)}, u32[]{:S(2)}, u32[]{:S(2)}) collective-permute-start(bf16[2,128,1024]{2,1,0:T(8,128)(2,1)S(1)} %get-tuple-element.61.refs_7_.refs_5_.refs_4_.refs_6_), channel_id=1, source_target_pairs={{1,0},{0,1},{3,2},{2,3},{5,4},{4,5},{7,6},{6,7},{9,8},{8,9},{11,10... | collective-permute-start | bytes 1572872 | tf_op jit(solution)/shard_map/ppermute | solution.py:284
  42.7 1.4 %collective-permute-start.3 = (f32[8,32,128]{2,1,0:T(8,128)S(1)}, f32[8,32,128]{2,1,0:T(8,128)S(1)}, u32[]{:S(2)}, u32[]{:S(2)}) collective-permute-start(f32[8,32,128]{2,1,0:T(8,128)S(1)} %get-tuple-element.63), channel_id=1, source_target_pairs={{0,2},{2,0},{4,6},{6,4},{8,10},{10,8},{12,14},{14,12},{16,18},{18,... | collective-permute-start | bytes 393224 | tf_op jit(solution)/shard_map/ppermute | solution.py:69
  53.0 1.4 %collective-permute-start.4 = (f32[8,32,128]{2,1,0:T(8,128)S(1)}, f32[8,32,128]{2,1,0:T(8,128)S(1)}, u32[]{:S(2)}, u32[]{:S(2)}) collective-permute-start(f32[8,32,128]{2,1,0:T(8,128)S(1)} %get-tuple-element.71), channel_id=1, source_target_pairs={{0,2},{2,0},{4,6},{6,4},{8,10},{10,8},{12,14},{14,12},{16,18},{18,... | collective-permute-start | bytes 393224 | tf_op jit(solution)/shard_map/ppermute | solution.py:69
  63.8 1.4 %collective-permute-start.5 = (f32[8,32,128]{2,1,0:T(8,128)S(1)}, f32[8,32,128]{2,1,0:T(8,128)S(1)}, u32[]{:S(2)}, u32[]{:S(2)}) collective-permute-start(f32[8,32,128]{2,1,0:T(8,128)S(1)} %get-tuple-element.79), channel_id=1, source_target_pairs={{0,2},{2,0},{4,6},{6,4},{8,10},{10,8},{12,14},{14,12},{16,18},{18,... | collective-permute-start | bytes 393224 | tf_op jit(solution)/shard_map/ppermute | solution.py:69

commit v9 on v8

--- a/solution.py
+++ b/solution.py
@@ -65,8 +65,9 @@
     def trade(blocks):
         return lax.all_to_all(blocks, "row", 0, 0, axis_index_groups=[row_order])
 
-    def scatter(keep, give, early=None):
+    def scatter(begin_keep, give, early=None):
         taken = lax.ppermute(give, "row", [(k, k ^ 1) for k in range(row_parts)])
+        keep = begin_keep()
         begun = early() if early else ()
         with jax.named_scope("sum_twins"):
             sums = call(add, twins_f32, keep, taken)
@@ -120,25 +121,34 @@
             g = jnp.where(second, twin_orders[1][place], twin_orders[0][place])
             out_ref[place] = left_ref[g] + right_ref[g]
 
-    def backward_partials(keep_ref, give_ref, solved, lower, matrices, begun=None):
+    def backward_partials(out_ref, solved, lower, matrices, begun, give):
         mine = lax.axis_index("col")
         index = lax.axis_index("row")
         for shift in range(col_parts):
             start = lax.rem(mine + shift, col_parts) * half
+            pairs_of = [(start // 2 + k, 2 * k) for k in range(half // 2)]
+            offsets = []
+            for g, block in pairs_of:
+                odd = lax.rem(index + index // 2 + g, 2)
+                chosen = block + (1 - odd if give else odd)
+                offsets.append(pl.multiple_of(chosen * width, width))
             total = None
             for level, vector in solved.items():
-                term = lax.dot_general(
-                    vector, matrix(matrices, level, lower, shift), (((1,), (0,)), ((), ())), preferred_element_type=f32
-                )
+                group, place = place_of[lookup[level, lower]]
+                ref = matrices[group * col_parts + shift]
+                right = jnp.concatenate([ref[place, :, pl.ds(offset, width)] for offset in offsets], axis=1)
+                term = lax.dot_general(vector, right, (((1,), (0,)), ((), ())), preferred_element_type=f32)
                 total = term if total is None else total + term
-            for block in range(0, half, 2):
-                even = total[:, block * width : (block + 1) * width]
-                uneven = total[:, (block + 1) * width : (block + 2) * width]
-                g = start // 2 + block // 2
-                kept, given = (0.0, 0.0) if begun is None else (begun[0][g], begun[1][g])
-                odd = lax.rem(index + index // 2 + g, 2) == 1
-                keep_ref[g] = jnp.where(odd, uneven, even) + kept
-                give_ref[g] = jnp.where(odd, even, uneven) + given
+            for k, (g, _) in enumerate(pairs_of):
+                block = total[:, k * width : (k + 1) * width]
+                out_ref[g] = block if begun is None else block + begun[g]
+
+    def keep_partials(level):
+        def body(rounded_ref, *refs):
+            begun, matrices = (refs[0], refs[1:-1]) if level < levels - 1 else (None, refs[:-1])
+            backward_partials(refs[-1], {level: rounded_ref[...]}, level - 1, matrices, begun, False)
+
+        return body
 
     def spread(out_ref, value):
         out_ref[...] = jnp.broadcast_to(value.astype(bf16)[None], out_ref.shape)
@@ -235,14 +245,14 @@
 
     def top(rhs_ref, solver_ref, early_ref, *refs):
         level = levels - 1
-        gathered, matrices = refs[:level], refs[level:-4]
-        result_ref, rounded_ref, keep_ref, give_ref = refs[-4:]
+        gathered, matrices = refs[:level], refs[level:-3]
+        result_ref, rounded_ref, give_ref = refs[-3:]
         total = forward_total(gathered, level, matrices, True, early_ref[...])
         result = solve(solver_ref, top_slot, rhs_ref[level] - total)
         result_ref[...] = result
         rounded = result.astype(bf16)
         rounded_ref[...] = rounded
-        backward_partials(keep_ref, give_ref, {level: rounded}, level - 1, matrices)
+        backward_partials(give_ref, {level: rounded}, level - 1, matrices, None, True)
 
     def backward_early(lower):
         known = range(lower + 2, levels)
@@ -250,23 +260,21 @@
         def body(*refs):
             solved = {level: refs[k][...] for k, level in enumerate(known)}
             matrices, (keep_ref, give_ref) = refs[len(known) : -2], refs[-2:]
-            backward_partials(keep_ref, give_ref, solved, lower, matrices)
+            backward_partials(keep_ref, solved, lower, matrices, None, False)
+            backward_partials(give_ref, solved, lower, matrices, None, True)
 
         return body
 
     def down(level):
-        def body(solver_ref, solved_ref, sums_ref, early_keep_ref, early_give_ref, *refs):
-            outs = 3 + (level > 1)
-            matrices = refs[:-outs]
-            keep_ref, give_ref, result_ref = refs[-outs:][:3]
+        def body(solver_ref, solved_ref, sums_ref, early_give_ref, *refs):
+            matrices = refs[:-3]
+            give_ref, result_ref, rounded_ref = refs[-3:]
             corrected = solved_ref[...] - jnp.sum(sums_ref[...], axis=0)
             result = solve(solver_ref, backward_slot[level], corrected)
             result_ref[...] = result
             rounded = result.astype(bf16)
-            if level > 1:
-                refs[-1][...] = rounded
-            begun = early_keep_ref, early_give_ref
-            backward_partials(keep_ref, give_ref, {level: rounded}, level - 1, matrices, begun)
+            rounded_ref[...] = rounded
+            backward_partials(give_ref, {level: rounded}, level - 1, matrices, early_give_ref, True)
 
         return body
 
@@ -341,8 +349,8 @@
         arrived = factors[: len(factors) - (col_parts - 1)]
         early = call(top_early, block_f32, *gathered, *arrived)
     with jax.named_scope("top_level"):
-        results[level], rounded[level], *halves = call(
-            top, (block_f32, block_bf16, twins_f32, twins_f32), right_sides, solver, early, *gathered, *factors
+        results[level], rounded[level], give = call(
+            top, (block_f32, block_bf16, twins_f32), right_sides, solver, early, *gathered, *factors
         )
 
     def begin(lower):
@@ -350,21 +358,19 @@
             known = [rounded[level] for level in range(lower + 2, levels)]
             return call(backward_early(lower), (twins_f32, twins_f32), *known, *factors)
 
+    def keep_of(level, *begun):
+        with jax.named_scope("backward_keep"):
+            return call(keep_partials(level), twins_f32, rounded[level], *begun, *factors)
+
+    keep = lambda: keep_of(levels - 1)
     for level in range(levels - 2, 0, -1):
-        sums, begun = scatter(*halves, lambda: begin(level - 1))
+        sums, begun = scatter(keep, give, lambda: begin(level - 1))
         with jax.named_scope("backward_level"):
-            keep, give, results[level], *rest = call(
-                down(level),
-                (twins_f32, twins_f32, block_f32) + (block_bf16,) * (level > 1),
-                solver,
-                solved[level],
-                sums,
-                *begun,
-                *factors,
+            give, results[level], rounded[level] = call(
+                down(level), (twins_f32, block_f32, block_bf16), solver, solved[level], sums, begun[1], *factors
             )
-        halves = keep, give
-        rounded[level] = rest[0] if rest else None
-    sums, _ = scatter(*halves)
+        keep = lambda level=level, begun=begun: keep_of(level, begun[0])
+    sums, _ = scatter(keep, give)
     with jax.named_scope("backward_last"):
         return call(
             last,

time: 75 us -> 74.8 us (level)
  waiting for transfers between devices: 5.82 us -> 4.88 us
    ppermute x3, waiting for transfers between devices: 2.96 us -> 2.02 us  [scatter(): taken = lax.ppermute(give, 'row', [(k, k ^ 1) for k in range(row_parts)])]
    pallas_call x14 -> x17, Pallas kernels: 7.57 us -> 8.3 us  [call(): pl.pallas_call(kernel, out_shape=outs, in_specs=[pl.BlockSpec(memory_spac...]
  transfers between devices with their start and end apart: 6 -> 6, of which waited for: 5 -> 5; matrix products, arithmetic and copies ran while one was open for 0% -> 0% of each run, Pallas kernels for 5% -> 7%
where the time goes in v9:
time: 74.8 us; the launch traced here: 74.5 us
  blocking collectives  55.4 us (74%)
  Pallas kernels  8.3 us (11%)
  starting transfers between devices  5.85 us (8%)
  waiting for transfers between devices  4.88 us (7%)
    all_to_all x3, blocking collectives, trade(): return lax.all_to_all(blocks, 'row', 0, 0, axis_index_groups=[row_order])  29.2 us
    all_to_all x3, blocking collectives, scatter(): lax.all_to_all(sums, 'row', 0, 0, axis_index_groups=one_of_each)  26.2 us
    pallas_call x17, Pallas kernels, call(): pl.pallas_call(kernel, out_shape=outs, in_specs=[pl.BlockSpec(memory_spac...  8.3 us
    ppermute x3, starting transfers between devices, exchange(): shifted.append(lax.ppermute(own, 'col', to_lower))  5.06 us
    ppermute x3, waiting for transfers between devices, exchange(): shifted.append(lax.ppermute(own, 'col', to_lower))  2.86 us
    ppermute x3, waiting for transfers between devices, scatter(): taken = lax.ppermute(give, 'row', [(k, k ^ 1) for k in range(row_parts)])  2.02 us
  transfers between devices with their start and end apart: 6, of which 5 were waited for; matrix products, arithmetic and copies ran while one was open for 0% of the time, Pallas kernels for 7%

profile of v9, /device:TPU:0, one launch (start us, length us, event | category | flops | bytes accessed | tf_op | source)
XLA Modules:
  0.0 74.5 jit_solution(5105607302702390838)
XLA Ops:
  0.0 1.3 %forward_first.2 = (bf16[2,128,1024]{2,1,0:T(8,128)(2,1)S(1)}, s32[6,1,8]{2,1,0:T(1,128)S(1)}) custom-call(bf16[6,128,1024]{2,1,0:T(8,128)(2,1)} %factor_hbm.3, s32[6,1,8]{2,1,0:T(1,128)} %pattern_hbm.1), custom_call_target="tpu_custom_call" | custom-call | tf_op jit(solution)/shard_map/forward_first/pallas_call | solution.py:22
  1.3 3.0 %collective-permute-start = (bf16[2,128,1024]{2,1,0:T(8,128)(2,1)S(1)}, bf16[2,128,1024]{2,1,0:T(8,128)(2,1)S(1)}, u32[]{:S(2)}, u32[]{:S(2)}) collective-permute-start(bf16[2,128,1024]{2,1,0:T(8,128)(2,1)S(1)} %get-tuple-element.51.refs_1_.refs_2_.refs_3_.refs_0_), channel_id=1, source_target_pairs={{1,0},{0,1},{3,2},{2,3},{5,4},{4,5},{7,6},{6,7},{9,8},{8,9},{11,10... | collective-permute-start | bytes 1572872 | tf_op jit(solution)/shard_map/ppermute | solution.py:292
  4.3 2.0 %forward_first.3 = (f32[32,128]{1,0:T(8,128)S(1)}, bf16[16,32,128]{2,1,0:T(8,128)(2,1)S(1)}, f32[4,32,128]{2,1,0:T(8,128)S(1)}, bf16[6,768,128]{2,1,0:T(8,128)(2...) custom-call(f32[4,32,128]{2,1,0:T(8,128)} %rhs_hbm.1, bf16[6,128,1024]{2,1,0:T(8,128)(2,1)} %factor_hbm.3, ...), custom_call_target="tpu_custom_call" | custom-call | tf_op jit(solution)/shard_map/forward_first/pallas_call | solution.py:22
  6.3 10.4 %all_to_all.30.refs_0_ = bf16[16,32,128]{2,1,0:T(8,128)(2,1)S(1)} all-to-all(bf16[16,32,128]{2,1,0:T(8,128)(2,1)S(1)} %get-tuple-element.48), channel_id=1, replica_groups={{22,0,4,8,12,16,20,24,28,2,6,10,14,18,26,30},{23,1,5,9,13,17,21,25,29,3..., dimensions={0} | all-to-all | bytes 262144 | tf_op jit(solution)/shard_map/all_to_all | solution.py:66
  16.7 0.5 collective-permute-start.1
  17.2 0.0 collective-permute-done.refs_2_.refs_3_.refs_4_.refs_1_
  17.2 0.5 forward_level.2
  17.7 9.6 %all_to_all.31.refs_1_ = bf16[16,32,128]{2,1,0:T(8,128)(2,1)S(1)} all-to-all(bf16[16,32,128]{2,1,0:T(8,128)(2,1)S(1)} %get-tuple-element.54), channel_id=1, replica_groups={{22,0,4,8,12,16,20,24,28,2,6,10,14,18,26,30},{23,1,5,9,13,17,21,25,29,3..., dimensions={0} | all-to-all | bytes 262144 | tf_op jit(solution)/shard_map/all_to_all | solution.py:66
  27.3 1.5 %collective-permute-start.2 = (bf16[2,128,1024]{2,1,0:T(8,128)(2,1)S(1)}, bf16[2,128,1024]{2,1,0:T(8,128)(2,1)S(1)}, u32[]{:S(2)}, u32[]{:S(2)}) collective-permute-start(bf16[2,128,1024]{2,1,0:T(8,128)(2,1)S(1)} %get-tuple-element.59.refs_7_.refs_4_.refs_5_.refs_6_), channel_id=1, source_target_pairs={{1,0},{0,1},{3,2},{2,3},{5,4},{4,5},{7,6},{6,7},{9,8},{8,9},{11,10... | collective-permute-start | bytes 1572872 | tf_op jit(solution)/shard_map/ppermute | solution.py:292
  28.9 2.4 %collective-permute-done.1.refs_5_.refs_6_.refs_3_.refs_4_ = bf16[2,128,1024]{2,1,0:T(8,128)(2,1)S(1)} collective-permute-done((bf16[2,128,1024]{2,1,0:T(8,128)(2,1)S(1)}, bf16[2,128,1024]{2,1,0:T(8,128)(2,1)S(1)}, u32[]{:S(2)}, u32[]{:S(2)}) %collective-permute-start.1) | collective-permute-done | bytes 524320 | tf_op jit(solution)/shard_map/ppermute | solution.py:292
  31.2 0.6 forward_level.3
  31.8 9.1 %all_to_all.32.refs_2_ = bf16[16,32,128]{2,1,0:T(8,128)(2,1)S(1)} all-to-all(bf16[16,32,128]{2,1,0:T(8,128)(2,1)S(1)} %get-tuple-element.58), channel_id=1, replica_groups={{22,0,4,8,12,16,20,24,28,2,6,10,14,18,26,30},{23,1,5,9,13,17,21,25,29,3..., dimensions={0} | all-to-all | bytes 262144 | tf_op jit(solution)/shard_map/all_to_all | solution.py:66
  41.0 0.4 top_early.1.early_ref
  41.4 0.5 collective-permute-done.2.refs_8_.refs_5_.refs_6_.refs_7_
  41.9 0.6 top_level.1
  42.6 0.1 collective-permute-start.3
  42.6 0.2 backward_keep.3.left_ref
  42.9 0.3 backward_early.2
  43.2 0.8 %collective-permute-done.3.right_ref = f32[8,32,128]{2,1,0:T(8,128)S(1)} collective-permute-done((f32[8,32,128]{2,1,0:T(8,128)S(1)}, f32[8,32,128]{2,1,0:T(8,128)S(1)}, u32[]{:S(2)}, u32[]{:S(2)}) %collective-permute-start.3) | collective-permute-done | bytes 131104 | tf_op jit(solution)/shard_map/ppermute | solution.py:69
  44.0 8.5 %all_to_all.33.sums_ref = f32[8,32,128]{2,1,0:T(8,128)S(1)} all-to-all(f32[8,32,128]{2,1,0:T(8,128)S(1)} %sum_twins.3), channel_id=1, replica_groups={{18,4,26,12,2,20,10,28},{22,8,30,16,6,24,14,0},{19,5,27,13,3,21,11,29},..., dimensions={0} | all-to-all | bytes 262144 | tf_op jit(solution)/shard_map/all_to_all | solution.py:76
  52.5 0.3 backward_level.2
  52.8 0.3 collective-permute-start.4
  53.2 0.5 backward_early.3
  53.6 0.2 backward_keep.4.left_ref
  53.9 0.4 collective-permute-done.4.right_ref
  54.3 9.0 %all_to_all.34.sums_ref = f32[8,32,128]{2,1,0:T(8,128)S(1)} all-to-all(f32[8,32,128]{2,1,0:T(8,128)S(1)} %sum_twins.4), channel_id=1, replica_groups={{18,4,26,12,2,20,10,28},{22,8,30,16,6,24,14,0},{19,5,27,13,3,21,11,29},..., dimensions={0} | all-to-all | bytes 262144 | tf_op jit(solution)/shard_map/all_to_all | solution.py:76
  63.3 0.3 backward_level.3
  63.6 0.4 collective-permute-start.5
  64.0 0.2 backward_keep.5.left_ref
  64.2 0.8 %collective-permute-done.5.right_ref = f32[8,32,128]{2,1,0:T(8,128)S(1)} collective-permute-done((f32[8,32,128]{2,1,0:T(8,128)S(1)}, f32[8,32,128]{2,1,0:T(8,128)S(1)}, u32[]{:S(2)}, u32[]{:S(2)}) %collective-permute-start.5) | collective-permute-done | bytes 131104 | tf_op jit(solution)/shard_map/ppermute | solution.py:69
  65.0 8.6 %all_to_all.35.sums_ref = f32[8,32,128]{2,1,0:T(8,128)S(1)} all-to-all(f32[8,32,128]{2,1,0:T(8,128)S(1)} %sum_twins.5), channel_id=1, replica_groups={{18,4,26,12,2,20,10,28},{22,8,30,16,6,24,14,0},{19,5,27,13,3,21,11,29},..., dimensions={0} | all-to-all | bytes 262144 | tf_op jit(solution)/shard_map/all_to_all | solution.py:76
  73.7 0.8 %backward_last.1 = f32[4,32,128]{2,1,0:T(8,128)} custom-call(bf16[6,768,128]{2,1,0:T(8,128)(2,1)S(1)} %get-tuple-element.43.solver_ref, f32[32,128]{1,0:T(8,128)S(1)} %get-tuple-element.44.solved_ref, f32[8,32,128]{2,1,0:T(8,128)S(1)} %all_to_all.35.sums_ref, f32[32,128]{1,0:T(8,128)S(1)} %get-tuple-element.76.refs_0_, ...), custom_call_target="tpu_custom_call" | custom-call | tf_op jit(solution)/shard_map/backward_last/pallas_call | solution.py:22
  (3 shorter events, 0.0 us)
Async XLA Ops:
  1.3 15.9 %collective-permute-start = (bf16[2,128,1024]{2,1,0:T(8,128)(2,1)S(1)}, bf16[2,128,1024]{2,1,0:T(8,128)(2,1)S(1)}, u32[]{:S(2)}, u32[]{:S(2)}) collective-permute-start(bf16[2,128,1024]{2,1,0:T(8,128)(2,1)S(1)} %get-tuple-element.51.refs_1_.refs_2_.refs_3_.refs_0_), channel_id=1, source_target_pairs={{1,0},{0,1},{3,2},{2,3},{5,4},{4,5},{7,6},{6,7},{9,8},{8,9},{11,10... | collective-permute-start | bytes 1572872 | tf_op jit(solution)/shard_map/ppermute | solution.py:292
  16.7 14.5 %collective-permute-start.1 = (bf16[2,128,1024]{2,1,0:T(8,128)(2,1)S(1)}, bf16[2,128,1024]{2,1,0:T(8,128)(2,1)S(1)}, u32[]{:S(2)}, u32[]{:S(2)}) collective-permute-start(bf16[2,128,1024]{2,1,0:T(8,128)(2,1)S(1)} %get-tuple-element.56.refs_4_.refs_5_.refs_2_.refs_3_), channel_id=1, source_target_pairs={{1,0},{0,1},{3,2},{2,3},{5,4},{4,5},{7,6},{6,7},{9,8},{8,9},{11,10... | collective-permute-start | bytes 1572872 | tf_op jit(solution)/shard_map/ppermute | solution.py:292
  27.3 14.6 %collective-permute-start.2 = (bf16[2,128,1024]{2,1,0:T(8,128)(2,1)S(1)}, bf16[2,128,1024]{2,1,0:T(8,128)(2,1)S(1)}, u32[]{:S(2)}, u32[]{:S(2)}) collective-permute-start(bf16[2,128,1024]{2,1,0:T(8,128)(2,1)S(1)} %get-tuple-element.59.refs_7_.refs_4_.refs_5_.refs_6_), channel_id=1, source_target_pairs={{1,0},{0,1},{3,2},{2,3},{5,4},{4,5},{7,6},{6,7},{9,8},{8,9},{11,10... | collective-permute-start | bytes 1572872 | tf_op jit(solution)/shard_map/ppermute | solution.py:292
  42.6 1.4 %collective-permute-start.3 = (f32[8,32,128]{2,1,0:T(8,128)S(1)}, f32[8,32,128]{2,1,0:T(8,128)S(1)}, u32[]{:S(2)}, u32[]{:S(2)}) collective-permute-start(f32[8,32,128]{2,1,0:T(8,128)S(1)} %get-tuple-element.61), channel_id=1, source_target_pairs={{0,2},{2,0},{4,6},{6,4},{8,10},{10,8},{12,14},{14,12},{16,18},{18,... | collective-permute-start | bytes 393224 | tf_op jit(solution)/shard_map/ppermute | solution.py:69
  52.8 1.4 %collective-permute-start.4 = (f32[8,32,128]{2,1,0:T(8,128)S(1)}, f32[8,32,128]{2,1,0:T(8,128)S(1)}, u32[]{:S(2)}, u32[]{:S(2)}) collective-permute-start(f32[8,32,128]{2,1,0:T(8,128)S(1)} %get-tuple-element.68), channel_id=1, source_target_pairs={{0,2},{2,0},{4,6},{6,4},{8,10},{10,8},{12,14},{14,12},{16,18},{18,... | collective-permute-start | bytes 393224 | tf_op jit(solution)/shard_map/ppermute | solution.py:69
  63.6 1.4 %collective-permute-start.5 = (f32[8,32,128]{2,1,0:T(8,128)S(1)}, f32[8,32,128]{2,1,0:T(8,128)S(1)}, u32[]{:S(2)}, u32[]{:S(2)}) collective-permute-start(f32[8,32,128]{2,1,0:T(8,128)S(1)} %get-tuple-element.75), channel_id=1, source_target_pairs={{0,2},{2,0},{4,6},{6,4},{8,10},{10,8},{12,14},{14,12},{16,18},{18,... | collective-permute-start | bytes 393224 | tf_op jit(solution)/shard_map/ppermute | solution.py:69

commit v10 on v9

--- a/solution.py
+++ b/solution.py
@@ -104,7 +104,7 @@
         for shift in range(col_parts):
             start = lax.rem(mine + shift, col_parts) * half
             for lower in range(level):
-                is_late = shift > 0 and place_of[lookup[level, lower]][0] == len(groups) - 1
+                is_late = shift > 0 and place_of[lookup[level, lower]][0] == level - 1
                 if late is not None and is_late != late:
                     continue
                 left = jnp.concatenate([gathered[lower][row_place(start + k)] for k in range(half)], axis=1)
@@ -230,12 +230,21 @@
 
     def middle(level):
         def body(rhs_ref, solver_ref, *refs):
-            gathered, matrices = refs[:level], refs[level:-2]
             solved_ref, out_ref = refs[-2:]
-            total = forward_total(gathered, level, matrices)
+            if level == 1:
+                total = forward_total(refs[:1], level, refs[1:-2])
+            else:
+                gathered, matrices = refs[1 : 1 + level], refs[1 + level : -2]
+                total = forward_total(gathered, level, matrices, True, refs[0][...])
             value = solve(solver_ref, forward_slot[level], rhs_ref[level] - total)
             solved_ref[...] = value
             spread(out_ref, value)
+
+        return body
+
+    def part_early(level):
+        def body(*refs):
+            refs[-1][...] = forward_total(refs[:level], level, refs[level:-1], False)
 
         return body
 
@@ -336,7 +345,13 @@
     held.append(moved)
     for level in range(1, levels - 1):
         with jax.named_scope("forward_level"):
-            value, out = call(middle(level), (block_f32, spread_bf16), right_sides, solver, *gathered, *flat(held))
+            early = []
+            if level > 1:
+                arrived = flat(held)[: -(col_parts - 1)]
+                early = [call(part_early(level), block_f32, *gathered, *arrived)]
+            value, out = call(
+                middle(level), (block_f32, spread_bf16), right_sides, solver, *early, *gathered, *flat(held)
+            )
         solved.append(value)
         blocks, moved = trade_beside(out, level)
         gathered.append(blocks)

time: 74.8 us -> 74.8 us (level)
    pallas_call x17 -> x18, Pallas kernels: 8.3 us -> 8.37 us  [call(): pl.pallas_call(kernel, out_shape=outs, in_specs=[pl.BlockSpec(memory_spac...]
where the time goes in v10:
time: 74.8 us; the launch traced here: 74.5 us
  blocking collectives  55.4 us (74%)
  Pallas kernels  8.37 us (11%)
  starting transfers between devices  5.86 us (8%)
  waiting for transfers between devices  4.79 us (6%)
    all_to_all x3, blocking collectives, trade(): return lax.all_to_all(blocks, 'row', 0, 0, axis_index_groups=[row_order])  29.2 us
    all_to_all x3, blocking collectives, scatter(): lax.all_to_all(sums, 'row', 0, 0, axis_index_groups=one_of_each)  26.2 us
    pallas_call x18, Pallas kernels, call(): pl.pallas_call(kernel, out_shape=outs, in_specs=[pl.BlockSpec(memory_spac...  8.37 us
    ppermute x3, starting transfers between devices, exchange(): shifted.append(lax.ppermute(own, 'col', to_lower))  5.06 us
    ppermute x3, waiting for transfers between devices, exchange(): shifted.append(lax.ppermute(own, 'col', to_lower))  2.78 us
    ppermute x3, waiting for transfers between devices, scatter(): taken = lax.ppermute(give, 'row', [(k, k ^ 1) for k in range(row_parts)])  2.01 us
  transfers between devices with their start and end apart: 6, of which 5 were waited for; matrix products, arithmetic and copies ran while one was open for 0% of the time, Pallas kernels for 7%

profile of v10, /device:TPU:0, one launch (start us, length us, event | category | flops | bytes accessed | tf_op | source)
XLA Modules:
  0.0 74.5 jit_solution(2018037338521850385)
XLA Ops:
  0.0 1.3 %forward_first.2 = (bf16[2,128,1024]{2,1,0:T(8,128)(2,1)S(1)}, s32[6,1,8]{2,1,0:T(1,128)S(1)}) custom-call(bf16[6,128,1024]{2,1,0:T(8,128)(2,1)} %factor_hbm.3, s32[6,1,8]{2,1,0:T(1,128)} %pattern_hbm.1), custom_call_target="tpu_custom_call" | custom-call | tf_op jit(solution)/shard_map/forward_first/pallas_call | solution.py:22
  1.3 3.0 %collective-permute-start = (bf16[2,128,1024]{2,1,0:T(8,128)(2,1)S(1)}, bf16[2,128,1024]{2,1,0:T(8,128)(2,1)S(1)}, u32[]{:S(2)}, u32[]{:S(2)}) collective-permute-start(bf16[2,128,1024]{2,1,0:T(8,128)(2,1)S(1)} %get-tuple-element.51.refs_1_.refs_2_.refs_3_.refs_0_), channel_id=1, source_target_pairs={{1,0},{0,1},{3,2},{2,3},{5,4},{4,5},{7,6},{6,7},{9,8},{8,9},{11,10... | collective-permute-start | bytes 1572872 | tf_op jit(solution)/shard_map/ppermute | solution.py:301
  4.3 2.0 %forward_first.3 = (f32[32,128]{1,0:T(8,128)S(1)}, bf16[16,32,128]{2,1,0:T(8,128)(2,1)S(1)}, f32[4,32,128]{2,1,0:T(8,128)S(1)}, bf16[6,768,128]{2,1,0:T(8,128)(2...) custom-call(f32[4,32,128]{2,1,0:T(8,128)} %rhs_hbm.1, bf16[6,128,1024]{2,1,0:T(8,128)(2,1)} %factor_hbm.3, ...), custom_call_target="tpu_custom_call" | custom-call | tf_op jit(solution)/shard_map/forward_first/pallas_call | solution.py:22
  6.3 10.4 %all_to_all.30.refs_0_.refs_1_ = bf16[16,32,128]{2,1,0:T(8,128)(2,1)S(1)} all-to-all(bf16[16,32,128]{2,1,0:T(8,128)(2,1)S(1)} %get-tuple-element.48), channel_id=1, replica_groups={{22,0,4,8,12,16,20,24,28,2,6,10,14,18,26,30},{23,1,5,9,13,17,21,25,29,3..., dimensions={0} | all-to-all | bytes 262144 | tf_op jit(solution)/shard_map/all_to_all | solution.py:66
  16.7 0.5 collective-permute-start.1
  17.2 0.0 collective-permute-done.refs_2_.refs_3_.refs_4_.refs_1_
  17.2 0.5 forward_level.3
  17.7 9.6 %all_to_all.31.refs_1_.refs_2_ = bf16[16,32,128]{2,1,0:T(8,128)(2,1)S(1)} all-to-all(bf16[16,32,128]{2,1,0:T(8,128)(2,1)S(1)} %get-tuple-element.54), channel_id=1, replica_groups={{22,0,4,8,12,16,20,24,28,2,6,10,14,18,26,30},{23,1,5,9,13,17,21,25,29,3..., dimensions={0} | all-to-all | bytes 262144 | tf_op jit(solution)/shard_map/all_to_all | solution.py:66
  27.3 1.5 %collective-permute-start.2 = (bf16[2,128,1024]{2,1,0:T(8,128)(2,1)S(1)}, bf16[2,128,1024]{2,1,0:T(8,128)(2,1)S(1)}, u32[]{:S(2)}, u32[]{:S(2)}) collective-permute-start(bf16[2,128,1024]{2,1,0:T(8,128)(2,1)S(1)} %get-tuple-element.59.refs_7_.refs_4_.refs_5_.refs_6_), channel_id=1, source_target_pairs={{1,0},{0,1},{3,2},{2,3},{5,4},{4,5},{7,6},{6,7},{9,8},{8,9},{11,10... | collective-permute-start | bytes 1572872 | tf_op jit(solution)/shard_map/ppermute | solution.py:301
  28.9 0.3 forward_level.4.refs_0_
  29.2 2.0 %collective-permute-done.1.refs_6_.refs_3_.refs_4_.refs_5_ = bf16[2,128,1024]{2,1,0:T(8,128)(2,1)S(1)} collective-permute-done((bf16[2,128,1024]{2,1,0:T(8,128)(2,1)S(1)}, bf16[2,128,1024]{2,1,0:T(8,128)(2,1)S(1)}, u32[]{:S(2)}, u32[]{:S(2)}) %collective-permute-start.1) | collective-permute-done | bytes 524320 | tf_op jit(solution)/shard_map/ppermute | solution.py:301
  31.2 0.3 forward_level.5
  31.6 9.1 %all_to_all.32.refs_2_ = bf16[16,32,128]{2,1,0:T(8,128)(2,1)S(1)} all-to-all(bf16[16,32,128]{2,1,0:T(8,128)(2,1)S(1)} %get-tuple-element.58), channel_id=1, replica_groups={{22,0,4,8,12,16,20,24,28,2,6,10,14,18,26,30},{23,1,5,9,13,17,21,25,29,3..., dimensions={0} | all-to-all | bytes 262144 | tf_op jit(solution)/shard_map/all_to_all | solution.py:66
  40.7 0.4 top_early.1.early_ref
  41.2 0.8 %collective-permute-done.2.refs_8_.refs_5_.refs_6_.refs_7_ = bf16[2,128,1024]{2,1,0:T(8,128)(2,1)S(1)} collective-permute-done((bf16[2,128,1024]{2,1,0:T(8,128)(2,1)S(1)}, bf16[2,128,1024]{2,1,0:T(8,128)(2,1)S(1)}, u32[]{:S(2)}, u32[]{:S(2)}) %collective-permute-start.2) | collective-permute-done | bytes 524320 | tf_op jit(solution)/shard_map/ppermute | solution.py:301
  41.9 0.6 top_level.1
  42.6 0.1 collective-permute-start.3
  42.6 0.2 backward_keep.3.left_ref
  42.9 0.3 backward_early.2
  43.2 0.8 %collective-permute-done.3.right_ref = f32[8,32,128]{2,1,0:T(8,128)S(1)} collective-permute-done((f32[8,32,128]{2,1,0:T(8,128)S(1)}, f32[8,32,128]{2,1,0:T(8,128)S(1)}, u32[]{:S(2)}, u32[]{:S(2)}) %collective-permute-start.3) | collective-permute-done | bytes 131104 | tf_op jit(solution)/shard_map/ppermute | solution.py:69
  44.0 8.5 %all_to_all.33.sums_ref = f32[8,32,128]{2,1,0:T(8,128)S(1)} all-to-all(f32[8,32,128]{2,1,0:T(8,128)S(1)} %sum_twins.3), channel_id=1, replica_groups={{18,4,26,12,2,20,10,28},{22,8,30,16,6,24,14,0},{19,5,27,13,3,21,11,29},..., dimensions={0} | all-to-all | bytes 262144 | tf_op jit(solution)/shard_map/all_to_all | solution.py:76
  52.5 0.3 backward_level.2
  52.8 0.4 collective-permute-start.4
  53.2 0.5 backward_early.3
  53.6 0.2 backward_keep.4.left_ref
  53.9 0.4 collective-permute-done.4.right_ref
  54.3 9.0 %all_to_all.34.sums_ref = f32[8,32,128]{2,1,0:T(8,128)S(1)} all-to-all(f32[8,32,128]{2,1,0:T(8,128)S(1)} %sum_twins.4), channel_id=1, replica_groups={{18,4,26,12,2,20,10,28},{22,8,30,16,6,24,14,0},{19,5,27,13,3,21,11,29},..., dimensions={0} | all-to-all | bytes 262144 | tf_op jit(solution)/shard_map/all_to_all | solution.py:76
  63.3 0.3 backward_level.3
  63.6 0.4 collective-permute-start.5
  64.0 0.2 backward_keep.5.left_ref
  64.2 0.8 %collective-permute-done.5.right_ref = f32[8,32,128]{2,1,0:T(8,128)S(1)} collective-permute-done((f32[8,32,128]{2,1,0:T(8,128)S(1)}, f32[8,32,128]{2,1,0:T(8,128)S(1)}, u32[]{:S(2)}, u32[]{:S(2)}) %collective-permute-start.5) | collective-permute-done | bytes 131104 | tf_op jit(solution)/shard_map/ppermute | solution.py:69
  65.0 8.6 %all_to_all.35.sums_ref = f32[8,32,128]{2,1,0:T(8,128)S(1)} all-to-all(f32[8,32,128]{2,1,0:T(8,128)S(1)} %sum_twins.5), channel_id=1, replica_groups={{18,4,26,12,2,20,10,28},{22,8,30,16,6,24,14,0},{19,5,27,13,3,21,11,29},..., dimensions={0} | all-to-all | bytes 262144 | tf_op jit(solution)/shard_map/all_to_all | solution.py:76
  73.7 0.8 %backward_last.1 = f32[4,32,128]{2,1,0:T(8,128)} custom-call(bf16[6,768,128]{2,1,0:T(8,128)(2,1)S(1)} %get-tuple-element.43.solver_ref, f32[32,128]{1,0:T(8,128)S(1)} %get-tuple-element.44.solved_ref, f32[8,32,128]{2,1,0:T(8,128)S(1)} %all_to_all.35.sums_ref, f32[32,128]{1,0:T(8,128)S(1)} %get-tuple-element.76.refs_0_, ...), custom_call_target="tpu_custom_call" | custom-call | tf_op jit(solution)/shard_map/backward_last/pallas_call | solution.py:22
  (3 shorter events, 0.1 us)
Async XLA Ops:
  1.3 15.9 %collective-permute-start = (bf16[2,128,1024]{2,1,0:T(8,128)(2,1)S(1)}, bf16[2,128,1024]{2,1,0:T(8,128)(2,1)S(1)}, u32[]{:S(2)}, u32[]{:S(2)}) collective-permute-start(bf16[2,128,1024]{2,1,0:T(8,128)(2,1)S(1)} %get-tuple-element.51.refs_1_.refs_2_.refs_3_.refs_0_), channel_id=1, source_target_pairs={{1,0},{0,1},{3,2},{2,3},{5,4},{4,5},{7,6},{6,7},{9,8},{8,9},{11,10... | collective-permute-start | bytes 1572872 | tf_op jit(solution)/shard_map/ppermute | solution.py:301
  16.7 14.5 %collective-permute-start.1 = (bf16[2,128,1024]{2,1,0:T(8,128)(2,1)S(1)}, bf16[2,128,1024]{2,1,0:T(8,128)(2,1)S(1)}, u32[]{:S(2)}, u32[]{:S(2)}) collective-permute-start(bf16[2,128,1024]{2,1,0:T(8,128)(2,1)S(1)} %get-tuple-element.56.refs_4_.refs_5_.refs_2_.refs_3_), channel_id=1, source_target_pairs={{1,0},{0,1},{3,2},{2,3},{5,4},{4,5},{7,6},{6,7},{9,8},{8,9},{11,10... | collective-permute-start | bytes 1572872 | tf_op jit(solution)/shard_map/ppermute | solution.py:301
  27.3 14.6 %collective-permute-start.2 = (bf16[2,128,1024]{2,1,0:T(8,128)(2,1)S(1)}, bf16[2,128,1024]{2,1,0:T(8,128)(2,1)S(1)}, u32[]{:S(2)}, u32[]{:S(2)}) collective-permute-start(bf16[2,128,1024]{2,1,0:T(8,128)(2,1)S(1)} %get-tuple-element.59.refs_7_.refs_4_.refs_5_.refs_6_), channel_id=1, source_target_pairs={{1,0},{0,1},{3,2},{2,3},{5,4},{4,5},{7,6},{6,7},{9,8},{8,9},{11,10... | collective-permute-start | bytes 1572872 | tf_op jit(solution)/shard_map/ppermute | solution.py:301
  42.6 1.4 %collective-permute-start.3 = (f32[8,32,128]{2,1,0:T(8,128)S(1)}, f32[8,32,128]{2,1,0:T(8,128)S(1)}, u32[]{:S(2)}, u32[]{:S(2)}) collective-permute-start(f32[8,32,128]{2,1,0:T(8,128)S(1)} %get-tuple-element.61), channel_id=1, source_target_pairs={{0,2},{2,0},{4,6},{6,4},{8,10},{10,8},{12,14},{14,12},{16,18},{18,... | collective-permute-start | bytes 393224 | tf_op jit(solution)/shard_map/ppermute | solution.py:69
  52.8 1.4 %collective-permute-start.4 = (f32[8,32,128]{2,1,0:T(8,128)S(1)}, f32[8,32,128]{2,1,0:T(8,128)S(1)}, u32[]{:S(2)}, u32[]{:S(2)}) collective-permute-start(f32[8,32,128]{2,1,0:T(8,128)S(1)} %get-tuple-element.68), channel_id=1, source_target_pairs={{0,2},{2,0},{4,6},{6,4},{8,10},{10,8},{12,14},{14,12},{16,18},{18,... | collective-permute-start | bytes 393224 | tf_op jit(solution)/shard_map/ppermute | solution.py:69
  63.6 1.4 %collective-permute-start.5 = (f32[8,32,128]{2,1,0:T(8,128)S(1)}, f32[8,32,128]{2,1,0:T(8,128)S(1)}, u32[]{:S(2)}, u32[]{:S(2)}) collective-permute-start(f32[8,32,128]{2,1,0:T(8,128)S(1)} %get-tuple-element.75), channel_id=1, source_target_pairs={{0,2},{2,0},{4,6},{6,4},{8,10},{10,8},{12,14},{14,12},{16,18},{18,... | collective-permute-start | bytes 393224 | tf_op jit(solution)/shard_map/ppermute | solution.py:69
